TPU v7x, 512 devices: a whole 4x4x16 slice. The times are simulated.
512 devices in a mesh: rows: 16 (over x, z_hi, core), cols: 32 (over z_lo, y).
Axes of the slice: x: 4, y: 4, z: 16 (z_hi: 2, z_lo: 8; z = z_hi * 8 + z_lo), core: 2. Of those that a mesh axis runs over, the one named last changes fastest.
Arguments:
- train_hidden: bfloat16 [512, 8, 4096], P(('rows', 'cols')), may hold values from -6 to 6
- train_cotangent: bfloat16 [512, 8, 4096], P(('rows', 'cols')), may hold values from -6 to 6
- train_lengths: int32 [512], P(('rows', 'cols')), may hold values from 1 to 8, 3072 in all
- roll_hidden: bfloat16 [512, 8, 4096], P(('cols', 'rows')), may hold values from -6 to 6
- roll_cotangent: bfloat16 [512, 8, 4096], P(('cols', 'rows')), may hold values from -6 to 6
- roll_lengths: int32 [512], P(('cols', 'rows')), may hold values from 1 to 8, 3072 in all
- gate_weight: bfloat16 [4096, 14336], P('rows', 'cols'), may hold values from -0.09375 to 0.09375
- up_weight: bfloat16 [4096, 14336], P('rows', 'cols'), may hold values from -0.09375 to 0.09375
- in_project: bfloat16 [14336, 64], P('cols'), may hold values from -0.046875 to 0.046875
- out_project: bfloat16 [4096, 64], replicated, may hold values from -0.09375 to 0.09375
Outputs:
- scores: float32 [512, 512], P('rows', 'cols')
All inputs are finite; a program needn't handle non-finite values. No bound on the sum of `train_lengths` or of `roll_lengths` on one device may be relied on, other than what follows from the above.
Results may differ from a plain program's by a relative error of at most 0.0041.
Values may be sent and summed in bfloat16 or wider, within the bound.
No kernel may reach another device: no remote copies, remote signals or barrier semaphores. Data moves between devices by JAX's collectives and lax.ppermute only.
A program may use at most 64 MiB of HBM per device.

v0:
```python
import jax
import jax.numpy as jnp
from jax import lax
from jax.sharding import PartitionSpec as P

RANK = 64


def on_device(
    train_hidden,
    train_cotangent,
    train_lengths,
    roll_hidden,
    roll_cotangent,
    roll_lengths,
    gate_weight,
    up_weight,
    in_project,
    out_project,
):
    width = train_hidden.shape[2]
    length = train_hidden.shape[1]
    rank = in_project.shape[1]
    stacked = jnp.stack([train_hidden, roll_hidden])
    grouped = lax.all_gather(stacked, "cols", axis=1, tiled=True)
    members = grouped.shape[1]
    flat = grouped.reshape(-1, width)
    gate = jnp.dot(
        flat,
        lax.all_gather(gate_weight, "rows", axis=0, tiled=True),
        preferred_element_type=jnp.float32,
    )
    up = jnp.dot(
        flat,
        lax.all_gather(up_weight, "rows", axis=0, tiled=True),
        preferred_element_type=jnp.float32,
    )
    act = (jax.nn.silu(gate) * up).astype(jnp.bfloat16)
    partial_left = jnp.dot(act, in_project, preferred_element_type=jnp.float32).reshape(
        2, members, length, rank
    )
    left = lax.psum_scatter(partial_left, "cols", scatter_dimension=1, tiled=True)
    cotangents = jnp.stack([train_cotangent, roll_cotangent])
    right = jnp.einsum("sntd,dk->sntk", cotangents, out_project, preferred_element_type=jnp.float32)
    lengths = jnp.stack([train_lengths, roll_lengths])
    live = (jnp.arange(length, dtype=jnp.int32)[None, None, :] < lengths[:, :, None]).astype(
        jnp.float32
    )
    grad = jnp.einsum(
        "snta,sntb->snab", left * live[:, :, :, None], right, precision=lax.Precision.HIGHEST
    )
    grad = grad.reshape(2, -1, rank * rank)
    unit = grad / jnp.sqrt(jnp.mean(grad * grad, axis=2, keepdims=True) + 1e-06)
    train_all = lax.all_gather(unit[0], "cols", axis=0, tiled=True)
    roll_all = lax.all_gather(unit[1], "rows", axis=0, tiled=True)
    return jnp.dot(train_all, roll_all.T, precision=lax.Precision.HIGHEST) / RANK


def solution(mesh):
    placed = (
        P(("rows", "cols"), None, None),
        P(("rows", "cols"), None, None),
        P(("rows", "cols")),
        P(("cols", "rows"), None, None),
        P(("cols", "rows"), None, None),
        P(("cols", "rows")),
        P("rows", "cols"),
        P("rows", "cols"),
        P("cols", None),
        P(),
    )
    return jax.shard_map(
        on_device, mesh=mesh, in_specs=placed, out_specs=P("rows", "cols"), check_vma=False
    )
```

profile of v0, /device:TPU:1, one launch (start us, length us, event | category | flops | bytes accessed | tf_op | source)
XLA Modules:
  0.0 1089.1 jit_solution(920265279413174783)
XLA Ops:
  6.5 0.0 copy-start
  6.5 0.0 all-gather.8.cloned.1.call-start
  6.5 0.7 all-gather.8.cloned.1.call-update
  7.3 0.0 all-gather.6.cloned.1.call-start
  7.3 1.5 pad_maximum_fusion
  8.8 0.0 all-gather.6.cloned.1.call-update
  8.9 0.0 all-gather.10.cloned.1.call-start
  8.9 0.7 all-gather.10.cloned.1.call-update
  9.6 0.0 all-reduce.3.cloned.1.call-start
  10.9 1.3 dynamic-slice
  12.2 0.1 add_bitcast_fusion
  12.3 0.0 copy-done
  12.3 1.1 fusion.9
  13.4 115.1 %all-gather.8.cloned.1.call-done = bf16[4096,448]{0,1:T(8,128)(2,1)} async-done(((bf16[256,448]{0,1:T(8,128)(2,1)}), bf16[4096,448]{0,1:T(8,128)(2,1)}) %all-gather.8.cloned.1.call-update) | async-done | bytes 3670032 | tf_op jit(solution)/shard_map/all_gather | solution.py:30
  128.5 202.7 %all-gather.6.cloned.1.call-done = bf16[2,32,8,4096]{3,2,1,0:T(8,128)(2,1)} async-done(((bf16[2,1,8,4096]{3,2,1,0:T(8,128)(2,1)}), bf16[2,32,8,4096]{3,2,1,0:T(8,128)(2,1)}) %all-gather.6.cloned.1.call-update) | async-done | bytes 4194320 | tf_op jit(solution)/shard_map/all_gather | solution.py:25
  331.2 0.0 copy-start.1
  331.2 5.4 fusion.24
  336.7 128.1 %all-gather.10.cloned.1.call-done = bf16[4096,448]{0,1:T(8,128)(2,1)} async-done(((bf16[256,448]{0,1:T(8,128)(2,1)}), bf16[4096,448]{0,1:T(8,128)(2,1)}) %all-gather.10.cloned.1.call-update) | async-done | bytes 3670032 | tf_op jit(solution)/shard_map/all_gather | solution.py:35
  464.7 0.0 copy-done.1
  464.7 6.5 fusion.1
  471.2 0.0 all-reduce.3.cloned.1.call-update
  471.2 0.1 compare_convert_fusion
  471.3 422.8 %all-reduce.3.cloned.1.call-done = f32[2,32,8,64]{3,2,1,0:T(8,128)} async-done(((f32[2,32,8,64]{3,2,1,0:T(8,128)}), f32[2,32,8,64]{3,2,1,0:T(8,128)}) %all-reduce.3.cloned.1.call-update) | async-done | bytes 131088
  894.1 1.8 multiply_reduce_fusion
  895.9 0.1 reshape.106
  896.1 0.1 broadcast_divide_fusion
  896.2 109.4 %all-gather = f32[32,1,4096]{2,1,0:T(1,128)S(1)} all-gather(f32[1,1,4096]{2,1,0:T(1,128)S(1)} %get-tuple-element.6), channel_id=2, replica_groups=mesh['rows'=16,'cols'=32] {'cols'}, dimensions={0}, use_global_device_ids=true | all-gather | bytes 540672 | tf_op jit(solution)/shard_map/all_gather | solution.py:54
  1005.6 75.5 %all-gather.1 = f32[16,1,4096]{2,1,0:T(1,128)S(1)} all-gather(f32[1,1,4096]{2,1,0:T(1,128)S(1)} %get-tuple-element.5), channel_id=3, replica_groups=mesh['rows'=16,'cols'=32] {'rows'}, dimensions={0}, use_global_device_ids=true | all-gather | bytes 278528 | tf_op jit(solution)/shard_map/all_gather | solution.py:55
  1081.1 1.5 convolution_multiply_fusion.1
  (2 shorter events, 0.0 us)
Async XLA Ops:
  6.5 5.8 copy-start
  6.5 122.0 %all-gather.8.cloned.1.call-start = ((), (), s32[]{:S(2)}) async-start(), calls=%async_computation.1 | async-start | bytes 3899392 | tf_op jit(solution)/shard_map/all_gather | solution.py:30
  7.3 324.0 %all-gather.6.cloned.1.call-start = ((), (), s32[]{:S(2)}) async-start(), calls=%async_computation | async-start | bytes 4325376 | tf_op jit(solution)/shard_map/all_gather | solution.py:25
  8.9 455.9 %all-gather.10.cloned.1.call-start = ((), (), s32[]{:S(2)}) async-start(), calls=%async_computation.2 | async-start | bytes 3899392 | tf_op jit(solution)/shard_map/all_gather | solution.py:35
  9.6 884.5 %all-reduce.3.cloned.1.call-start = ((), (), s32[]{:S(2)}) async-start(), calls=%async_computation.3 | async-start | bytes 524288
  331.2 133.5 %copy-start.1 = (bf16[448,64]{0,1:T(8,128)(2,1)S(1)}, bf16[448,64]{0,1:T(8,128)(2,1)}, u32[]{:S(2)}) copy-start(bf16[448,64]{0,1:T(8,128)(2,1)} %param.18) | copy-start | bytes 172036
Sparse Core Ops, SparseCore 0:
  10.5 117.9 all-gather.7
  130.6 200.5 all-gather.5
  334.4 130.3 all-gather.9
  471.3 422.7 all-reduce.2
where the time goes:
time: 1090 us
  waiting for transfers between devices  870 us (80%)
  blocking collectives  185 us (17%)
  matrix products  16.4 us (2%)
  between operations  14.5 us (1%)
    unnamed x5, waiting for transfers between devices  424 us
    all_gather x1, waiting for transfers between devices, on_device(): grouped = lax.all_gather(stacked, 'cols', axis=1, tiled=True)  203 us
    all_gather x1, waiting for transfers between devices, on_device(): lax.all_gather(up_weight, 'rows', axis=0, tiled=True)  128 us
    all_gather x1, waiting for transfers between devices, on_device(): lax.all_gather(gate_weight, 'rows', axis=0, tiled=True)  115 us
    all_gather x1, blocking collectives, on_device(): train_all = lax.all_gather(unit[0], 'cols', axis=0, tiled=True)  109 us
    all_gather x1, blocking collectives, on_device(): roll_all = lax.all_gather(unit[1], 'rows', axis=0, tiled=True)  75.5 us
  transfers between devices with their start and end apart: 4, of which 4 were waited for; matrix products, arithmetic and copies ran while one was open for 1% of the time, Pallas kernels for 0%

commit v1 on v0

v1 whole, which is shorter than its diff:
```python
import functools

import jax
import jax.numpy as jnp
from jax import lax
from jax.experimental import pallas as pl
from jax.experimental.pallas import tpu as pltpu
from jax.sharding import Mesh, PartitionSpec as P

RANK = 64
NX, NZH, NCO, NZL, NY = 4, 2, 2, 8, 4
HIGH = lax.Precision.HIGHEST


def mlp_kernel(nw, xplan, wk_ref, xr_ref, *refs):
    w_refs = refs[:nw]
    x_refs = refs[nw : nw + len(xplan)]
    ip_ref, out_ref, wv, xv, acc, wsem, xsem = refs[nw + len(xplan) :]
    wcopies = [pltpu.make_async_copy(w_refs[p], wv.at[p], wsem.at[p]) for p in range(nw)]
    xcopies = []
    for i, parts in enumerate(xplan):
        for j, slot in enumerate(parts):
            row = pl.multiple_of(xr_ref[slot] * 16, 16)
            xcopies.append(
                pltpu.make_async_copy(
                    x_refs[i].at[pl.ds(16 * j, 16)], xv.at[pl.ds(row, 16)], xsem.at[slot]
                )
            )
    for c in xcopies:
        c.start()
    for c in wcopies:
        c.start()
    for c in xcopies:
        c.wait()
    for p in range(nw):
        wcopies[p].wait()
        col = pl.multiple_of(wk_ref[p] * 256, 256)
        part = jnp.dot(xv[:, pl.ds(col, 256)], wv[p], preferred_element_type=jnp.float32)
        if p == 0:
            acc[...] = part
        else:
            acc[...] += part
    half = acc.shape[1] // 2
    for m in range(4):
        rows = acc[m * 128 : (m + 1) * 128, :]
        gate, up = rows[:, :half], rows[:, half:]
        act = (gate / (1.0 + jnp.exp(-gate)) * up).astype(jnp.bfloat16)
        left = jnp.dot(act, ip_ref[...], preferred_element_type=jnp.float32)
        left = left.reshape(8, 2, 8, RANK)
        out_ref[m * 8 : (m + 1) * 8] = jnp.concatenate([left[:, 0], left[:, 1]], axis=-1)


def mlp(wk, xr, ws, xs, xplan, ip):
    nw = len(ws)
    any_ = pl.BlockSpec(memory_space=pl.ANY)
    smem = pl.BlockSpec(memory_space=pltpu.SMEM)
    return pl.pallas_call(
        functools.partial(mlp_kernel, nw, xplan),
        out_shape=jax.ShapeDtypeStruct((32, 8, 2 * RANK), jnp.float32),
        in_specs=[smem, smem] + [any_] * (nw + len(xs)) + [pl.BlockSpec(memory_space=pltpu.VMEM)],
        out_specs=pl.BlockSpec(memory_space=pltpu.VMEM),
        scratch_shapes=[
            pltpu.VMEM((nw,) + ws[0].shape, jnp.bfloat16),
            pltpu.VMEM((512, xs[0].shape[1]), jnp.bfloat16),
            pltpu.VMEM((512, ws[0].shape[1]), jnp.float32),
            pltpu.SemaphoreType.DMA((nw,)),
            pltpu.SemaphoreType.DMA((32,)),
        ],
        compiler_params=pltpu.CompilerParams(vmem_limit_bytes=40 << 20),
        name="mlp",
    )(wk, xr, *ws, *xs, ip)


def norm_kernel(parts_ref, right_ref, live_ref, train_ref, roll_ref):
    left = jnp.sum(parts_ref[...], axis=0)
    for s, ref in ((0, train_ref), (1, roll_ref)):
        one = left[:, s * RANK : (s + 1) * RANK] * live_ref[s]
        right = right_ref[s]
        grad = lax.dot_general(
            one, right, (((0,), (0,)), ((), ())), precision=HIGH, preferred_element_type=jnp.float32
        )
        mean = jnp.sum(grad * grad) / (RANK * RANK)
        inv = 1.0 / jnp.sqrt(jnp.full((8, RANK), mean + 1e-6))
        ref[...] = jnp.concatenate([one * inv, right], axis=-1)


def score_kernel(train_ref, roll_ref, out_ref):
    t = train_ref[...].reshape(-1, 2 * RANK)
    r = roll_ref[...].reshape(-1, 2 * RANK)
    dims = (((1,), (1,)), ((), ()))
    a = lax.dot_general(
        t[:, :RANK], r[:, :RANK], dims, precision=HIGH, preferred_element_type=jnp.float32
    )
    b = lax.dot_general(
        t[:, RANK:], r[:, RANK:], dims, precision=HIGH, preferred_element_type=jnp.float32
    )
    both = jnp.sum((a * b).reshape(32, 8, 128), axis=1)
    pick = (
        lax.broadcasted_iota(jnp.int32, (128, 16), 0) // 8
        == lax.broadcasted_iota(jnp.int32, (128, 16), 1)
    ).astype(jnp.float32)
    out_ref[...] = jnp.dot(both, pick, precision=HIGH, preferred_element_type=jnp.float32) / RANK


def shift(n, k):
    return [(i, (i + k) % n) for i in range(n)]


def on_device(
    train_hidden,
    train_cotangent,
    train_lengths,
    roll_hidden,
    roll_cotangent,
    roll_lengths,
    gate_weight,
    up_weight,
    in_project,
    out_project,
):
    x, zh, co, zl, y = (lax.axis_index(a) for a in ("x", "zh", "co", "zl", "y"))
    width = train_hidden.shape[2]
    own = jnp.concatenate([train_hidden[0], roll_hidden[0]], axis=0)
    w = jnp.concatenate([gate_weight, up_weight], axis=1)

    far = lax.ppermute(own, "zl", [(i, i ^ 4) for i in range(8)])
    other = lax.ppermute(w, "zh", shift(2, 1))

    xs, xplan, xr = [], [], []

    def add_x(array, spots):
        xs.append(array)
        slots = []
        for s in spots:
            slots.append(len(xr))
            xr.append(s)
        xplan.append(tuple(slots))

    def over_y(array, zls):
        add_x(array, [z * 4 + y for z in zls])
        for k in (1, 3, 2):
            add_x(lax.ppermute(array, "y", shift(NY, k)), [z * 4 + (y - k) % NY for z in zls])

    over_y(own, [zl])
    over_y(far, [zl ^ 4])
    pair = jnp.concatenate([own, far], axis=0)
    for k in (1, 3, 2):
        got = lax.ppermute(pair, "zl", [(i, (i & 4) | ((i + k) & 3)) for i in range(8)])
        z = (zl & 4) | ((zl - k) & 3)
        over_y(got, [z, z ^ 4])

    ws, wk = [], []
    for block, h in ((w, zh), (other, 1 - zh)):
        for k in (0, 1, 3, 2):
            got = block if k == 0 else lax.ppermute(block, "x", shift(NX, k))
            ws.append(got)
            wk.append((x - k) % NX * 4 + h * 2 + co)
    for i in range(8):
        ws.append(lax.ppermute(ws[i], "co", shift(2, 1)))
        wk.append(wk[i] + 1 - 2 * co)

    parts = mlp(
        jnp.stack(wk).astype(jnp.int32),
        jnp.stack(xr).astype(jnp.int32),
        ws,
        xs,
        tuple(xplan),
        in_project,
    )
    cot = jnp.concatenate([train_cotangent[0], roll_cotangent[0]], axis=0)
    right = jnp.dot(cot, out_project, preferred_element_type=jnp.float32).reshape(2, 8, RANK)
    lengths = jnp.stack([train_lengths, roll_lengths])
    live = (jnp.arange(8, dtype=jnp.int32)[None, :] < lengths).astype(jnp.float32)[:, :, None]
    live = jnp.broadcast_to(live, (2, 8, RANK))

    parts = lax.all_to_all(parts, ("zl", "y"), 0, 0, tiled=True)
    small = jax.ShapeDtypeStruct((8, 2 * RANK), jnp.float32)
    train, roll = pl.pallas_call(norm_kernel, out_shape=(small, small), name="norm")(
        parts, right, live
    )
    train_all = lax.all_to_all(
        jnp.broadcast_to(train, (32, 8, 2 * RANK)), ("zl", "y"), 0, 0, tiled=True
    )
    roll_all = lax.all_to_all(
        jnp.broadcast_to(roll, (16, 8, 2 * RANK)), ("x", "zh", "co"), 0, 0, tiled=True
    )
    return pl.pallas_call(
        score_kernel, out_shape=jax.ShapeDtypeStruct((32, 16), jnp.float32), name="score"
    )(train_all, roll_all)


def solution(mesh):
    fine = Mesh(mesh.devices.reshape(NX, NZH, NCO, NZL, NY), ("x", "zh", "co", "zl", "y"))
    rows, cols = ("x", "zh", "co"), ("zl", "y")
    placed = (
        P(rows + cols, None, None),
        P(rows + cols, None, None),
        P(rows + cols),
        P(cols + rows, None, None),
        P(cols + rows, None, None),
        P(cols + rows),
        P(rows, cols),
        P(rows, cols),
        P(cols, None),
        P(),
    )
    return jax.shard_map(
        on_device, mesh=fine, in_specs=placed, out_specs=P(rows, cols), check_vma=False
    )
```

time: 1090 us -> 285 us (0.26)
  waiting for transfers between devices: 870 us -> 20.2 us
  starting transfers between devices: 0.12 us -> 160 us
  blocking collectives: 185 us -> 42.6 us
  local copies, waits for them, and re-layouts: 1.38 us -> 33.6 us
  Pallas kernels: 0 us -> 20.4 us
  matrix products: 16.4 us -> 0.85 us
  between operations: 14.5 us -> 2.3 us
    all_gather x3 -> x0, waiting for transfers between devices: 446 us -> none  [the longest x1 203 us: on_device(): grouped = lax.all_gather(stacked, 'cols', axis=1, tiled=True)]
    unnamed x5 -> x0, waiting for transfers between devices: 424 us -> none
    all_gather x2 -> x0, blocking collectives: 185 us -> none  [the longest x1 109 us: on_device(): train_all = lax.all_gather(unit[0], 'cols', axis=0, tiled=True)]
    ppermute x0 -> x34, starting transfers between devices: none -> 133 us  [the longest x15 48.5 us: over_y(): lax.ppermute(array, 'y', shift(NY, k))]
    all_to_all x0 -> x2, blocking collectives: none -> 42.6 us  [the longest x1 25.4 us: on_device(): lax.all_to_all(jnp.broadcast_to(roll, (16, 8, 2 * RANK)), ('x', 'zh', 'co...]
    unnamed x5 -> x99, local copies, waits for them, and re-layouts: 1.28 us -> 30.6 us
    all_to_all x0 -> x1, starting transfers between devices: none -> 27.6 us  [on_device(): parts = lax.all_to_all(parts, ('zl', 'y'), 0, 0, tiled=True)]
    pallas_call x0 -> x3, Pallas kernels: none -> 20.4 us  [the longest x1 16.1 us: mlp(): pl.pallas_call(functools.partial(mlp_kernel, nw, xplan), out_shape=jax.Sh...]
  transfers between devices with their start and end apart: 4 -> 35, of which waited for: 4 -> 3; matrix products, arithmetic and copies ran while one was open for 1% -> 1% of each run, Pallas kernels for 0% -> 0%
where the time goes in v1:
time: 285 us; the launch traced here: 282 us
  starting transfers between devices  160 us (56%)
  blocking collectives  42.6 us (15%)
  local copies, waits for them, and re-layouts  33.6 us (12%)
  Pallas kernels  20.4 us (7%)
  waiting for transfers between devices  20.2 us (7%)
    ppermute x15, starting transfers between devices, over_y(): lax.ppermute(array, 'y', shift(NY, k))  48.5 us
    unnamed x99, local copies, waits for them, and re-layouts  30.6 us
    ppermute x8, starting transfers between devices, on_device(): ws.append(lax.ppermute(ws[i], 'co', shift(2, 1)))  29.1 us
    all_to_all x1, starting transfers between devices, on_device(): parts = lax.all_to_all(parts, ('zl', 'y'), 0, 0, tiled=True)  27.6 us
    all_to_all x1, blocking collectives, on_device(): lax.all_to_all(jnp.broadcast_to(roll, (16, 8, 2 * RANK)), ('x', 'zh', 'co...  25.4 us
    ppermute x6, starting transfers between devices, on_device(): got = block if k == 0 else lax.ppermute(block, 'x', shift(NX, k))  21 us
    all_to_all x1, blocking collectives, on_device(): lax.all_to_all(jnp.broadcast_to(train, (32, 8, 2 * RANK)), ('zl', 'y'), 0...  17.2 us
    pallas_call x1, Pallas kernels, mlp(): pl.pallas_call(functools.partial(mlp_kernel, nw, xplan), out_shape=jax.Sh...  16.1 us
  transfers between devices with their start and end apart: 35, of which 3 were waited for; matrix products, arithmetic and copies ran while one was open for 1% of the time, Pallas kernels for 0%

profile of v1, /device:TPU:1, one launch (start us, length us, event | category | flops | bytes accessed | tf_op | source)
XLA Modules:
  0.0 282.3 jit_solution(2179204618930096871)
XLA Ops:
  0.0 0.9 pad_maximum_fusion.2.refs_16_
  1.0 9.8 %collective-permute-start.18 = (bf16[16,4096]{1,0:T(8,128)(2,1)S(1)}, bf16[16,4096]{1,0:T(8,128)(2,1)S(1)}, u32[]{:S(2)}, u32[]{:S(2)}) collective-permute-start(bf16[16,4096]{1,0:T(8,128)(2,1)S(1)} %pad_maximum_fusion.2.refs_16_), channel_id=1, source_target_pairs={{0,16},{4,20},{8,24},{12,28},{16,0},{20,4},{24,8},{28,12},{1,17},{... | collective-permute-start | bytes 393224 | tf_op jit(solution)/shard_map/ppermute | solution.py:126
  10.8 3.2 %collective-permute-start.15 = (bf16[16,4096]{1,0:T(8,128)(2,1)S(1)}, bf16[16,4096]{1,0:T(8,128)(2,1)S(1)}, u32[]{:S(2)}, u32[]{:S(2)}) collective-permute-start(bf16[16,4096]{1,0:T(8,128)(2,1)S(1)} %pad_maximum_fusion.2.refs_16_), channel_id=1, source_target_pairs={{0,1},{1,2},{2,3},{3,0},{4,5},{5,6},{6,7},{7,4},{8,9},{9,10},{10,1... | collective-permute-start | bytes 393224 | tf_op jit(solution)/shard_map/ppermute | solution.py:142
  14.0 3.4 %collective-permute-start.16 = (bf16[16,4096]{1,0:T(8,128)(2,1)S(1)}, bf16[16,4096]{1,0:T(8,128)(2,1)S(1)}, u32[]{:S(2)}, u32[]{:S(2)}) collective-permute-start(bf16[16,4096]{1,0:T(8,128)(2,1)S(1)} %pad_maximum_fusion.2.refs_16_), channel_id=1, source_target_pairs={{0,3},{1,0},{2,1},{3,2},{4,7},{5,4},{6,5},{7,6},{8,11},{9,8},{10,9... | collective-permute-start | bytes 393224 | tf_op jit(solution)/shard_map/ppermute | solution.py:142
  17.3 3.5 %collective-permute-start.17 = (bf16[16,4096]{1,0:T(8,128)(2,1)S(1)}, bf16[16,4096]{1,0:T(8,128)(2,1)S(1)}, u32[]{:S(2)}, u32[]{:S(2)}) collective-permute-start(bf16[16,4096]{1,0:T(8,128)(2,1)S(1)} %pad_maximum_fusion.2.refs_16_), channel_id=1, source_target_pairs={{0,2},{1,3},{2,0},{3,1},{4,6},{5,7},{6,4},{7,5},{8,10},{9,11},{10,... | collective-permute-start | bytes 393224 | tf_op jit(solution)/shard_map/ppermute | solution.py:142
  21.7 3.7 %collective-permute-start.22 = (bf16[32,4096]{1,0:T(8,128)(2,1)}, bf16[32,4096]{1,0:T(8,128)(2,1)S(1)}, u32[]{:S(2)}, u32[]{:S(2)}) collective-permute-start(bf16[32,4096]{1,0:T(8,128)(2,1)} %pad_maximum_fusion.1), channel_id=1, source_target_pairs={{0,4},{4,8},{8,12},{12,0},{16,20},{20,24},{24,28},{28,16},{1,5},{5... | collective-permute-start | bytes 786440 | tf_op jit(solution)/shard_map/ppermute | solution.py:148
  25.3 4.7 %collective-permute-start.26 = (bf16[32,4096]{1,0:T(8,128)(2,1)}, bf16[32,4096]{1,0:T(8,128)(2,1)}, u32[]{:S(2)}, u32[]{:S(2)}) collective-permute-start(bf16[32,4096]{1,0:T(8,128)(2,1)} %pad_maximum_fusion.1), channel_id=1, source_target_pairs={{0,12},{4,0},{8,4},{12,8},{16,28},{20,16},{24,20},{28,24},{1,13},{... | collective-permute-start | bytes 786440 | tf_op jit(solution)/shard_map/ppermute | solution.py:148
  30.1 3.5 %collective-permute-start.19 = (bf16[16,4096]{1,0:T(8,128)(2,1)S(1)}, bf16[16,4096]{1,0:T(8,128)(2,1)S(1)}, u32[]{:S(2)}, u32[]{:S(2)}) collective-permute-start(bf16[16,4096]{1,0:T(8,128)(2,1)S(1)} %collective-permute-done.18.refs_20_), channel_id=1, source_target_pairs={{0,1},{1,2},{2,3},{3,0},{4,5},{5,6},{6,7},{7,4},{8,9},{9,10},{10,1... | collective-permute-start | bytes 393224 | tf_op jit(solution)/shard_map/ppermute | solution.py:142
  33.6 3.4 %collective-permute-start.20 = (bf16[16,4096]{1,0:T(8,128)(2,1)S(1)}, bf16[16,4096]{1,0:T(8,128)(2,1)S(1)}, u32[]{:S(2)}, u32[]{:S(2)}) collective-permute-start(bf16[16,4096]{1,0:T(8,128)(2,1)S(1)} %collective-permute-done.18.refs_20_), channel_id=1, source_target_pairs={{0,3},{1,0},{2,1},{3,2},{4,7},{5,4},{6,5},{7,6},{8,11},{9,8},{10,9... | collective-permute-start | bytes 393224 | tf_op jit(solution)/shard_map/ppermute | solution.py:142
  37.0 3.5 %collective-permute-start.21 = (bf16[16,4096]{1,0:T(8,128)(2,1)S(1)}, bf16[16,4096]{1,0:T(8,128)(2,1)S(1)}, u32[]{:S(2)}, u32[]{:S(2)}) collective-permute-start(bf16[16,4096]{1,0:T(8,128)(2,1)S(1)} %collective-permute-done.18.refs_20_), channel_id=1, source_target_pairs={{0,2},{1,3},{2,0},{3,1},{4,6},{5,7},{6,4},{7,5},{8,10},{9,11},{10,... | collective-permute-start | bytes 393224 | tf_op jit(solution)/shard_map/ppermute | solution.py:142
  41.7 1.9 collective-permute-start.30
  44.3 14.1 %collective-permute-start.3 = (bf16[256,896]{1,0:T(8,128)(2,1)S(1)}, bf16[256,896]{1,0:T(8,128)(2,1)S(1)}, u32[]{:S(2)}, u32[]{:S(2)}) collective-permute-start(bf16[256,896]{1,0:T(8,128)(2,1)S(1)} %pad_maximum_fusion.refs_0_), channel_id=1, source_target_pairs={{0,64},{64,0},{1,65},{65,1},{2,66},{66,2},{3,67},{67,3},{4,68},{68... | collective-permute-start | bytes 1376264 | tf_op jit(solution)/shard_map/ppermute | solution.py:127
  59.1 4.6 %collective-permute-start.2 = (bf16[256,896]{1,0:T(8,128)(2,1)S(1)}, bf16[256,896]{1,0:T(8,128)(2,1)S(1)}, u32[]{:S(2)}, u32[]{:S(2)}) collective-permute-start(bf16[256,896]{1,0:T(8,128)(2,1)S(1)} %pad_maximum_fusion.refs_0_), channel_id=1, source_target_pairs={{0,256},{128,384},{256,0},{384,128},{1,257},{129,385},{257,1},{385... | collective-permute-start | bytes 1376264 | tf_op jit(solution)/shard_map/ppermute | solution.py:155
  63.8 2.2 collective-permute-start
  66.0 4.3 %collective-permute-start.1 = (bf16[256,896]{1,0:T(8,128)(2,1)S(1)}, bf16[256,896]{1,0:T(8,128)(2,1)S(1)}, u32[]{:S(2)}, u32[]{:S(2)}) collective-permute-start(bf16[256,896]{1,0:T(8,128)(2,1)S(1)} %pad_maximum_fusion.refs_0_), channel_id=1, source_target_pairs={{0,384},{128,0},{256,128},{384,256},{1,385},{129,1},{257,129},{385... | collective-permute-start | bytes 1376264 | tf_op jit(solution)/shard_map/ppermute | solution.py:155
  70.3 5.4 %collective-permute-start.7 = (bf16[256,896]{1,0:T(8,128)(2,1)S(1)}, bf16[256,896]{1,0:T(8,128)(2,1)S(1)}, u32[]{:S(2)}, u32[]{:S(2)}) collective-permute-start(bf16[256,896]{1,0:T(8,128)(2,1)S(1)} %pad_maximum_fusion.refs_0_), channel_id=1, source_target_pairs={{0,32},{32,0},{1,33},{33,1},{2,34},{34,2},{3,35},{35,3},{4,36},{36... | collective-permute-start | bytes 1376264 | tf_op jit(solution)/shard_map/ppermute | solution.py:159
  75.7 9.8 %collective-permute-done.3.refs_4_ = bf16[256,896]{1,0:T(8,128)(2,1)S(1)} collective-permute-done((bf16[256,896]{1,0:T(8,128)(2,1)S(1)}, bf16[256,896]{1,0:T(8,128)(2,1)S(1)}, u32[]{:S(2)}, u32[]{:S(2)}) %collective-permute-start.3) | collective-permute-done | bytes 458784 | tf_op jit(solution)/shard_map/ppermute | solution.py:127
  85.5 2.3 collective-permute-start.23
  87.8 4.2 %collective-permute-start.24 = (bf16[32,4096]{1,0:T(8,128)(2,1)S(1)}, bf16[32,4096]{1,0:T(8,128)(2,1)S(1)}, u32[]{:S(2)}, u32[]{:S(2)}) collective-permute-start(bf16[32,4096]{1,0:T(8,128)(2,1)S(1)} %collective-permute-done.22.refs_24_), channel_id=1, source_target_pairs={{0,3},{1,0},{2,1},{3,2},{4,7},{5,4},{6,5},{7,6},{8,11},{9,8},{10,9... | collective-permute-start | bytes 786440 | tf_op jit(solution)/shard_map/ppermute | solution.py:142
  92.0 3.0 %collective-permute-start.25 = (bf16[32,4096]{1,0:T(8,128)(2,1)S(1)}, bf16[32,4096]{1,0:T(8,128)(2,1)S(1)}, u32[]{:S(2)}, u32[]{:S(2)}) collective-permute-start(bf16[32,4096]{1,0:T(8,128)(2,1)S(1)} %collective-permute-done.22.refs_24_), channel_id=1, source_target_pairs={{0,2},{1,3},{2,0},{3,1},{4,6},{5,7},{6,4},{7,5},{8,10},{9,11},{10,... | collective-permute-start | bytes 786440 | tf_op jit(solution)/shard_map/ppermute | solution.py:142
  95.1 1.9 collective-permute-start.27
  97.8 4.6 %collective-permute-start.28 = (bf16[32,4096]{1,0:T(8,128)(2,1)}, bf16[32,4096]{1,0:T(8,128)(2,1)S(1)}, u32[]{:S(2)}, u32[]{:S(2)}) collective-permute-start(bf16[32,4096]{1,0:T(8,128)(2,1)} %collective-permute-done.26.refs_28_), channel_id=1, source_target_pairs={{0,3},{1,0},{2,1},{3,2},{4,7},{5,4},{6,5},{7,6},{8,11},{9,8},{10,9... | collective-permute-start | bytes 786440 | tf_op jit(solution)/shard_map/ppermute | solution.py:142
  103.1 2.5 collective-permute-start.29
  106.4 1.9 collective-permute-start.31
  109.0 4.6 %collective-permute-start.32 = (bf16[32,4096]{1,0:T(8,128)(2,1)S(1)}, bf16[32,4096]{1,0:T(8,128)(2,1)S(1)}, u32[]{:S(2)}, u32[]{:S(2)}) collective-permute-start(bf16[32,4096]{1,0:T(8,128)(2,1)S(1)} %collective-permute-done.30.refs_32_), channel_id=1, source_target_pairs={{0,3},{1,0},{2,1},{3,2},{4,7},{5,4},{6,5},{7,6},{8,11},{9,8},{10,9... | collective-permute-start | bytes 786440 | tf_op jit(solution)/shard_map/ppermute | solution.py:142
  114.3 3.0 %collective-permute-start.33 = (bf16[32,4096]{1,0:T(8,128)(2,1)S(1)}, bf16[32,4096]{1,0:T(8,128)(2,1)S(1)}, u32[]{:S(2)}, u32[]{:S(2)}) collective-permute-start(bf16[32,4096]{1,0:T(8,128)(2,1)S(1)} %collective-permute-done.30.refs_32_), channel_id=1, source_target_pairs={{0,2},{1,3},{2,0},{3,1},{4,6},{5,7},{6,4},{7,5},{8,10},{9,11},{10,... | collective-permute-start | bytes 786440 | tf_op jit(solution)/shard_map/ppermute | solution.py:142
  118.8 3.1 %collective-permute-start.4 = (bf16[256,896]{1,0:T(8,128)(2,1)S(1)}, bf16[256,896]{1,0:T(8,128)(2,1)}, u32[]{:S(2)}, u32[]{:S(2)}) collective-permute-start(bf16[256,896]{1,0:T(8,128)(2,1)S(1)} %collective-permute-done.3.refs_4_), channel_id=1, source_target_pairs={{0,128},{128,256},{256,384},{384,0},{1,129},{129,257},{257,385},{3... | collective-permute-start | bytes 1376264 | tf_op jit(solution)/shard_map/ppermute | solution.py:155
  122.6 3.4 %collective-permute-start.5 = (bf16[256,896]{1,0:T(8,128)(2,1)S(1)}, bf16[256,896]{1,0:T(8,128)(2,1)}, u32[]{:S(2)}, u32[]{:S(2)}) collective-permute-start(bf16[256,896]{1,0:T(8,128)(2,1)S(1)} %collective-permute-done.3.refs_4_), channel_id=1, source_target_pairs={{0,384},{128,0},{256,128},{384,256},{1,385},{129,1},{257,129},{385... | collective-permute-start | bytes 1376264 | tf_op jit(solution)/shard_map/ppermute | solution.py:155
  126.7 3.4 %collective-permute-start.6 = (bf16[256,896]{1,0:T(8,128)(2,1)S(1)}, bf16[256,896]{1,0:T(8,128)(2,1)}, u32[]{:S(2)}, u32[]{:S(2)}) collective-permute-start(bf16[256,896]{1,0:T(8,128)(2,1)S(1)} %collective-permute-done.3.refs_4_), channel_id=1, source_target_pairs={{0,256},{128,384},{256,0},{384,128},{1,257},{129,385},{257,1},{385... | collective-permute-start | bytes 1376264 | tf_op jit(solution)/shard_map/ppermute | solution.py:155
  130.9 10.8 %collective-permute-start.11 = (bf16[256,896]{1,0:T(8,128)(2,1)S(1)}, bf16[256,896]{1,0:T(8,128)(2,1)S(1)}, u32[]{:S(2)}, u32[]{:S(2)}) collective-permute-start(bf16[256,896]{1,0:T(8,128)(2,1)S(1)} %collective-permute-done.3.refs_4_), channel_id=1, source_target_pairs={{0,32},{32,0},{1,33},{33,1},{2,34},{34,2},{3,35},{35,3},{4,36},{36... | collective-permute-start | bytes 1376264 | tf_op jit(solution)/shard_map/ppermute | solution.py:159
  142.4 1.9 collective-permute-start.10
  144.3 2.4 collective-permute-start.8
  146.8 1.9 collective-permute-start.9
  148.7 2.4 collective-permute-start.12
  152.0 1.9 collective-permute-start.13
  154.7 2.4 collective-permute-start.14
  158.8 1.0 copy-done.2
  159.8 1.0 copy-done.4
  160.9 1.0 copy-done.6
  161.9 0.9 copy-done.8
  162.8 0.9 copy-done.10
  163.8 0.9 copy-done.12
  164.7 0.9 copy-done.14
  165.7 0.9 copy-done.16
  166.6 0.9 copy-done.18
  167.6 0.9 copy-done.20
  168.5 0.9 copy-done.22
  169.5 0.9 copy-done.24
  170.4 0.9 copy-done.26
  171.4 0.9 copy-done.28
  172.3 0.9 copy-done.30
  173.2 0.9 copy-done.32
  174.1 0.9 copy-done.34
  175.0 0.9 copy-done.36
  175.9 0.9 copy-done.38
  176.8 16.1 %mlp.1 = f32[32,8,128]{2,1,0:T(8,128)} custom-call(s32[16]{0:T(128)S(1)} %stack.177.wk_ref, s32[32]{0:T(128)S(1)} %stack.210.xr_ref, bf16[256,896]{1,0:T(8,128)(2,1)S(1)} %pad_maximum_fusion.refs_0_, bf16[256,896]{1,0:T(8,128)(2,1)S(1)} %collective-permute-done.refs_1_, bf16[256,896]{1,0:T(8,128)(2,1)S(1)} %collective-permute-done.1.refs_2_, ...), custom_call_target="tpu_custom_call" | custom-call | tf_op jit(solution)/shard_map/mlp/pallas_call | solution.py:57
  193.0 27.6 %all-to-all-start = ((f32[32,8,128]{2,1,0:T(8,128)}), f32[32,8,128]{2,1,0:T(8,128)S(1)}, u32[]{:S(2)}, u32[]{:S(2)}) async-start(f32[32,8,128]{2,1,0:T(8,128)} %mlp.1), calls=%async_computation | async-start | bytes 262144 | tf_op jit(solution)/shard_map/all_to_all | solution.py:176
  222.0 0.9 convolution_bitcast_fusion.right_ref
  222.9 9.8 %all-to-all-done.parts_ref = f32[32,8,128]{2,1,0:T(8,128)S(1)} async-done(((f32[32,8,128]{2,1,0:T(8,128)}), f32[32,8,128]{2,1,0:T(8,128)S(1)}, u32[]{:S(2)}, u32[]{:S(2)}) %all-to-all-start) | async-done | bytes 131104 | tf_op jit(solution)/shard_map/all_to_all | solution.py:176
  233.4 2.1 norm.1
  236.2 25.4 %all_to_all.15.roll_ref = f32[16,8,128]{2,1,0:T(8,128)} all-to-all(f32[16,8,128]{2,1,0:T(8,128)S(1)} %broadcast_in_dim.15), channel_id=1, replica_groups=mesh['x'=4,'zh'=2,'co'=2,'zl'=8,'y'=4] {'x','zh','co'}, dimensions={0} | all-to-all | bytes 131072 | tf_op jit(solution)/shard_map/all_to_all | solution.py:184
  261.6 17.2 %all_to_all.16.train_ref = f32[32,8,128]{2,1,0:T(8,128)} all-to-all(f32[32,8,128]{2,1,0:T(8,128)S(1)} %broadcast_in_dim.14), channel_id=1, replica_groups=mesh['x'=4,'zh'=2,'co'=2,'zl'=8,'y'=4] {'zl','y'}, dimensions={0} | all-to-all | bytes 262144 | tf_op jit(solution)/shard_map/all_to_all | solution.py:181
  278.8 2.1 score.1
  280.9 1.4 copy.14
  (122 shorter events, 15.7 us)
Async XLA Ops:
  0.0 221.9 %copy-start = (bf16[4096,64]{0,1:T(8,128)(2,1)S(1)}, bf16[4096,64]{0,1:T(8,128)(2,1)}, u32[]{:S(2)}) copy-start(bf16[4096,64]{0,1:T(8,128)(2,1)} %param.19) | copy-start | bytes 1572868
  0.0 20.9 %copy-start.40 = (bf16[1,8,4096]{2,1,0:T(8,128)(2,1)S(1)}, bf16[1,8,4096]{2,1,0:T(8,128)(2,1)}, u32[]{:S(2)}) copy-start(bf16[1,8,4096]{2,1,0:T(8,128)(2,1)} %param.13) | copy-start | bytes 196612
  0.0 20.9 %copy-start.41 = (bf16[1,8,4096]{2,1,0:T(8,128)(2,1)S(1)}, bf16[1,8,4096]{2,1,0:T(8,128)(2,1)}, u32[]{:S(2)}) copy-start(bf16[1,8,4096]{2,1,0:T(8,128)(2,1)} %param.10) | copy-start | bytes 196612
  1.0 39.6 %copy-start.42 = (bf16[256,448]{0,1:T(8,128)(2,1)S(1)}, bf16[256,448]{0,1:T(8,128)(2,1)}, u32[]{:S(2)}) copy-start(bf16[256,448]{0,1:T(8,128)(2,1)} %param.16) | copy-start | bytes 688132
  1.0 19.9 %collective-permute-start.18 = (bf16[16,4096]{1,0:T(8,128)(2,1)S(1)}, bf16[16,4096]{1,0:T(8,128)(2,1)S(1)}, u32[]{:S(2)}, u32[]{:S(2)}) collective-permute-start(bf16[16,4096]{1,0:T(8,128)(2,1)S(1)} %pad_maximum_fusion.2.refs_16_), channel_id=1, source_target_pairs={{0,16},{4,20},{8,24},{12,28},{16,0},{20,4},{24,8},{28,12},{1,17},{... | collective-permute-start | bytes 393224 | tf_op jit(solution)/shard_map/ppermute | solution.py:126
  10.8 19.3 %collective-permute-start.15 = (bf16[16,4096]{1,0:T(8,128)(2,1)S(1)}, bf16[16,4096]{1,0:T(8,128)(2,1)S(1)}, u32[]{:S(2)}, u32[]{:S(2)}) collective-permute-start(bf16[16,4096]{1,0:T(8,128)(2,1)S(1)} %pad_maximum_fusion.2.refs_16_), channel_id=1, source_target_pairs={{0,1},{1,2},{2,3},{3,0},{4,5},{5,6},{6,7},{7,4},{8,9},{9,10},{10,1... | collective-permute-start | bytes 393224 | tf_op jit(solution)/shard_map/ppermute | solution.py:142
  14.0 19.6 %collective-permute-start.16 = (bf16[16,4096]{1,0:T(8,128)(2,1)S(1)}, bf16[16,4096]{1,0:T(8,128)(2,1)S(1)}, u32[]{:S(2)}, u32[]{:S(2)}) collective-permute-start(bf16[16,4096]{1,0:T(8,128)(2,1)S(1)} %pad_maximum_fusion.2.refs_16_), channel_id=1, source_target_pairs={{0,3},{1,0},{2,1},{3,2},{4,7},{5,4},{6,5},{7,6},{8,11},{9,8},{10,9... | collective-permute-start | bytes 393224 | tf_op jit(solution)/shard_map/ppermute | solution.py:142
  17.3 19.6 %collective-permute-start.17 = (bf16[16,4096]{1,0:T(8,128)(2,1)S(1)}, bf16[16,4096]{1,0:T(8,128)(2,1)S(1)}, u32[]{:S(2)}, u32[]{:S(2)}) collective-permute-start(bf16[16,4096]{1,0:T(8,128)(2,1)S(1)} %pad_maximum_fusion.2.refs_16_), channel_id=1, source_target_pairs={{0,2},{1,3},{2,0},{3,1},{4,6},{5,7},{6,4},{7,5},{8,10},{9,11},{10,... | collective-permute-start | bytes 393224 | tf_op jit(solution)/shard_map/ppermute | solution.py:142
  21.7 19.1 %copy-start.43 = (bf16[256,448]{0,1:T(8,128)(2,1)S(1)}, bf16[256,448]{0,1:T(8,128)(2,1)}, u32[]{:S(2)}) copy-start(bf16[256,448]{0,1:T(8,128)(2,1)} %param.17) | copy-start | bytes 688132
  21.7 42.1 %collective-permute-start.22 = (bf16[32,4096]{1,0:T(8,128)(2,1)}, bf16[32,4096]{1,0:T(8,128)(2,1)S(1)}, u32[]{:S(2)}, u32[]{:S(2)}) collective-permute-start(bf16[32,4096]{1,0:T(8,128)(2,1)} %pad_maximum_fusion.1), channel_id=1, source_target_pairs={{0,4},{4,8},{8,12},{12,0},{16,20},{20,24},{24,28},{28,16},{1,5},{5... | collective-permute-start | bytes 786440 | tf_op jit(solution)/shard_map/ppermute | solution.py:148
  25.3 40.7 %collective-permute-start.26 = (bf16[32,4096]{1,0:T(8,128)(2,1)}, bf16[32,4096]{1,0:T(8,128)(2,1)}, u32[]{:S(2)}, u32[]{:S(2)}) collective-permute-start(bf16[32,4096]{1,0:T(8,128)(2,1)} %pad_maximum_fusion.1), channel_id=1, source_target_pairs={{0,12},{4,0},{8,4},{12,8},{16,28},{20,16},{24,20},{28,24},{1,13},{... | collective-permute-start | bytes 786440 | tf_op jit(solution)/shard_map/ppermute | solution.py:148
  30.1 10.6 %copy-start.27 = (bf16[16,4096]{1,0:T(8,128)(2,1)}, bf16[16,4096]{1,0:T(8,128)(2,1)S(1)}, u32[]{:S(2)}) copy-start(bf16[16,4096]{1,0:T(8,128)(2,1)S(1)} %collective-permute-done.15.refs_17_) | copy-start | bytes 393220
  30.1 10.9 %collective-permute-start.19 = (bf16[16,4096]{1,0:T(8,128)(2,1)S(1)}, bf16[16,4096]{1,0:T(8,128)(2,1)S(1)}, u32[]{:S(2)}, u32[]{:S(2)}) collective-permute-start(bf16[16,4096]{1,0:T(8,128)(2,1)S(1)} %collective-permute-done.18.refs_20_), channel_id=1, source_target_pairs={{0,1},{1,2},{2,3},{3,0},{4,5},{5,6},{6,7},{7,4},{8,9},{9,10},{10,1... | collective-permute-start | bytes 393224 | tf_op jit(solution)/shard_map/ppermute | solution.py:142
  33.6 7.1 %copy-start.29 = (bf16[16,4096]{1,0:T(8,128)(2,1)}, bf16[16,4096]{1,0:T(8,128)(2,1)S(1)}, u32[]{:S(2)}) copy-start(bf16[16,4096]{1,0:T(8,128)(2,1)S(1)} %collective-permute-done.16.refs_18_) | copy-start | bytes 393220
  33.6 10.0 %collective-permute-start.20 = (bf16[16,4096]{1,0:T(8,128)(2,1)S(1)}, bf16[16,4096]{1,0:T(8,128)(2,1)S(1)}, u32[]{:S(2)}, u32[]{:S(2)}) collective-permute-start(bf16[16,4096]{1,0:T(8,128)(2,1)S(1)} %collective-permute-done.18.refs_20_), channel_id=1, source_target_pairs={{0,3},{1,0},{2,1},{3,2},{4,7},{5,4},{6,5},{7,6},{8,11},{9,8},{10,9... | collective-permute-start | bytes 393224 | tf_op jit(solution)/shard_map/ppermute | solution.py:142
  37.0 3.7 %copy-start.31 = (bf16[16,4096]{1,0:T(8,128)(2,1)}, bf16[16,4096]{1,0:T(8,128)(2,1)S(1)}, u32[]{:S(2)}) copy-start(bf16[16,4096]{1,0:T(8,128)(2,1)S(1)} %collective-permute-done.17.refs_19_) | copy-start | bytes 393220
  37.0 21.5 %collective-permute-start.21 = (bf16[16,4096]{1,0:T(8,128)(2,1)S(1)}, bf16[16,4096]{1,0:T(8,128)(2,1)S(1)}, u32[]{:S(2)}, u32[]{:S(2)}) collective-permute-start(bf16[16,4096]{1,0:T(8,128)(2,1)S(1)} %collective-permute-done.18.refs_20_), channel_id=1, source_target_pairs={{0,2},{1,3},{2,0},{3,1},{4,6},{5,7},{6,4},{7,5},{8,10},{9,11},{10,... | collective-permute-start | bytes 393224 | tf_op jit(solution)/shard_map/ppermute | solution.py:142
  41.7 28.6 %collective-permute-start.30 = (bf16[32,4096]{1,0:T(8,128)(2,1)}, bf16[32,4096]{1,0:T(8,128)(2,1)S(1)}, u32[]{:S(2)}, u32[]{:S(2)}) collective-permute-start(bf16[32,4096]{1,0:T(8,128)(2,1)} %pad_maximum_fusion.1), channel_id=1, source_target_pairs={{0,8},{4,12},{8,0},{12,4},{16,24},{20,28},{24,16},{28,20},{1,9},{5... | collective-permute-start | bytes 786440 | tf_op jit(solution)/shard_map/ppermute | solution.py:148
  44.3 41.2 %collective-permute-start.3 = (bf16[256,896]{1,0:T(8,128)(2,1)S(1)}, bf16[256,896]{1,0:T(8,128)(2,1)S(1)}, u32[]{:S(2)}, u32[]{:S(2)}) collective-permute-start(bf16[256,896]{1,0:T(8,128)(2,1)S(1)} %pad_maximum_fusion.refs_0_), channel_id=1, source_target_pairs={{0,64},{64,0},{1,65},{65,1},{2,66},{66,2},{3,67},{67,3},{4,68},{68... | collective-permute-start | bytes 1376264 | tf_op jit(solution)/shard_map/ppermute | solution.py:127
  59.1 28.7 %collective-permute-start.2 = (bf16[256,896]{1,0:T(8,128)(2,1)S(1)}, bf16[256,896]{1,0:T(8,128)(2,1)S(1)}, u32[]{:S(2)}, u32[]{:S(2)}) collective-permute-start(bf16[256,896]{1,0:T(8,128)(2,1)S(1)} %pad_maximum_fusion.refs_0_), channel_id=1, source_target_pairs={{0,256},{128,384},{256,0},{384,128},{1,257},{129,385},{257,1},{385... | collective-permute-start | bytes 1376264 | tf_op jit(solution)/shard_map/ppermute | solution.py:155
  63.8 28.3 %collective-permute-start = (bf16[256,896]{1,0:T(8,128)(2,1)S(1)}, bf16[256,896]{1,0:T(8,128)(2,1)S(1)}, u32[]{:S(2)}, u32[]{:S(2)}) collective-permute-start(bf16[256,896]{1,0:T(8,128)(2,1)S(1)} %pad_maximum_fusion.refs_0_), channel_id=1, source_target_pairs={{0,128},{128,256},{256,384},{384,0},{1,129},{129,257},{257,385},{3... | collective-permute-start | bytes 1376264 | tf_op jit(solution)/shard_map/ppermute | solution.py:155
  66.0 29.1 %collective-permute-start.1 = (bf16[256,896]{1,0:T(8,128)(2,1)S(1)}, bf16[256,896]{1,0:T(8,128)(2,1)S(1)}, u32[]{:S(2)}, u32[]{:S(2)}) collective-permute-start(bf16[256,896]{1,0:T(8,128)(2,1)S(1)} %pad_maximum_fusion.refs_0_), channel_id=1, source_target_pairs={{0,384},{128,0},{256,128},{384,256},{1,385},{129,1},{257,129},{385... | collective-permute-start | bytes 1376264 | tf_op jit(solution)/shard_map/ppermute | solution.py:155
  70.3 26.7 %collective-permute-start.7 = (bf16[256,896]{1,0:T(8,128)(2,1)S(1)}, bf16[256,896]{1,0:T(8,128)(2,1)S(1)}, u32[]{:S(2)}, u32[]{:S(2)}) collective-permute-start(bf16[256,896]{1,0:T(8,128)(2,1)S(1)} %pad_maximum_fusion.refs_0_), channel_id=1, source_target_pairs={{0,32},{32,0},{1,33},{33,1},{2,34},{34,2},{3,35},{35,3},{4,36},{36... | collective-permute-start | bytes 1376264 | tf_op jit(solution)/shard_map/ppermute | solution.py:159
  85.5 16.9 %collective-permute-start.23 = (bf16[32,4096]{1,0:T(8,128)(2,1)S(1)}, bf16[32,4096]{1,0:T(8,128)(2,1)S(1)}, u32[]{:S(2)}, u32[]{:S(2)}) collective-permute-start(bf16[32,4096]{1,0:T(8,128)(2,1)S(1)} %collective-permute-done.22.refs_24_), channel_id=1, source_target_pairs={{0,1},{1,2},{2,3},{3,0},{4,5},{5,6},{6,7},{7,4},{8,9},{9,10},{10,1... | collective-permute-start | bytes 786440 | tf_op jit(solution)/shard_map/ppermute | solution.py:142
  87.8 17.8 %collective-permute-start.24 = (bf16[32,4096]{1,0:T(8,128)(2,1)S(1)}, bf16[32,4096]{1,0:T(8,128)(2,1)S(1)}, u32[]{:S(2)}, u32[]{:S(2)}) collective-permute-start(bf16[32,4096]{1,0:T(8,128)(2,1)S(1)} %collective-permute-done.22.refs_24_), channel_id=1, source_target_pairs={{0,3},{1,0},{2,1},{3,2},{4,7},{5,4},{6,5},{7,6},{8,11},{9,8},{10,9... | collective-permute-start | bytes 786440 | tf_op jit(solution)/shard_map/ppermute | solution.py:142
  92.0 16.2 %collective-permute-start.25 = (bf16[32,4096]{1,0:T(8,128)(2,1)S(1)}, bf16[32,4096]{1,0:T(8,128)(2,1)S(1)}, u32[]{:S(2)}, u32[]{:S(2)}) collective-permute-start(bf16[32,4096]{1,0:T(8,128)(2,1)S(1)} %collective-permute-done.22.refs_24_), channel_id=1, source_target_pairs={{0,2},{1,3},{2,0},{3,1},{4,6},{5,7},{6,4},{7,5},{8,10},{9,11},{10,... | collective-permute-start | bytes 786440 | tf_op jit(solution)/shard_map/ppermute | solution.py:142
  95.1 18.5 %collective-permute-start.27 = (bf16[32,4096]{1,0:T(8,128)(2,1)}, bf16[32,4096]{1,0:T(8,128)(2,1)S(1)}, u32[]{:S(2)}, u32[]{:S(2)}) collective-permute-start(bf16[32,4096]{1,0:T(8,128)(2,1)} %collective-permute-done.26.refs_28_), channel_id=1, source_target_pairs={{0,1},{1,2},{2,3},{3,0},{4,5},{5,6},{6,7},{7,4},{8,9},{9,10},{10,1... | collective-permute-start | bytes 786440 | tf_op jit(solution)/shard_map/ppermute | solution.py:142
  97.8 20.2 %collective-permute-start.28 = (bf16[32,4096]{1,0:T(8,128)(2,1)}, bf16[32,4096]{1,0:T(8,128)(2,1)S(1)}, u32[]{:S(2)}, u32[]{:S(2)}) collective-permute-start(bf16[32,4096]{1,0:T(8,128)(2,1)} %collective-permute-done.26.refs_28_), channel_id=1, source_target_pairs={{0,3},{1,0},{2,1},{3,2},{4,7},{5,4},{6,5},{7,6},{8,11},{9,8},{10,9... | collective-permute-start | bytes 786440 | tf_op jit(solution)/shard_map/ppermute | solution.py:142
  103.1 18.8 %collective-permute-start.29 = (bf16[32,4096]{1,0:T(8,128)(2,1)}, bf16[32,4096]{1,0:T(8,128)(2,1)S(1)}, u32[]{:S(2)}, u32[]{:S(2)}) collective-permute-start(bf16[32,4096]{1,0:T(8,128)(2,1)} %collective-permute-done.26.refs_28_), channel_id=1, source_target_pairs={{0,2},{1,3},{2,0},{3,1},{4,6},{5,7},{6,4},{7,5},{8,10},{9,11},{10,... | collective-permute-start | bytes 786440 | tf_op jit(solution)/shard_map/ppermute | solution.py:142
  106.4 19.6 %collective-permute-start.31 = (bf16[32,4096]{1,0:T(8,128)(2,1)S(1)}, bf16[32,4096]{1,0:T(8,128)(2,1)S(1)}, u32[]{:S(2)}, u32[]{:S(2)}) collective-permute-start(bf16[32,4096]{1,0:T(8,128)(2,1)S(1)} %collective-permute-done.30.refs_32_), channel_id=1, source_target_pairs={{0,1},{1,2},{2,3},{3,0},{4,5},{5,6},{6,7},{7,4},{8,9},{9,10},{10,1... | collective-permute-start | bytes 786440 | tf_op jit(solution)/shard_map/ppermute | solution.py:142
  109.0 21.2 %collective-permute-start.32 = (bf16[32,4096]{1,0:T(8,128)(2,1)S(1)}, bf16[32,4096]{1,0:T(8,128)(2,1)S(1)}, u32[]{:S(2)}, u32[]{:S(2)}) collective-permute-start(bf16[32,4096]{1,0:T(8,128)(2,1)S(1)} %collective-permute-done.30.refs_32_), channel_id=1, source_target_pairs={{0,3},{1,0},{2,1},{3,2},{4,7},{5,4},{6,5},{7,6},{8,11},{9,8},{10,9... | collective-permute-start | bytes 786440 | tf_op jit(solution)/shard_map/ppermute | solution.py:142
  114.3 27.4 %collective-permute-start.33 = (bf16[32,4096]{1,0:T(8,128)(2,1)S(1)}, bf16[32,4096]{1,0:T(8,128)(2,1)S(1)}, u32[]{:S(2)}, u32[]{:S(2)}) collective-permute-start(bf16[32,4096]{1,0:T(8,128)(2,1)S(1)} %collective-permute-done.30.refs_32_), channel_id=1, source_target_pairs={{0,2},{1,3},{2,0},{3,1},{4,6},{5,7},{6,4},{7,5},{8,10},{9,11},{10,... | collective-permute-start | bytes 786440 | tf_op jit(solution)/shard_map/ppermute | solution.py:142
  118.8 25.6 %collective-permute-start.4 = (bf16[256,896]{1,0:T(8,128)(2,1)S(1)}, bf16[256,896]{1,0:T(8,128)(2,1)}, u32[]{:S(2)}, u32[]{:S(2)}) collective-permute-start(bf16[256,896]{1,0:T(8,128)(2,1)S(1)} %collective-permute-done.3.refs_4_), channel_id=1, source_target_pairs={{0,128},{128,256},{256,384},{384,0},{1,129},{129,257},{257,385},{3... | collective-permute-start | bytes 1376264 | tf_op jit(solution)/shard_map/ppermute | solution.py:155
  122.6 24.2 %collective-permute-start.5 = (bf16[256,896]{1,0:T(8,128)(2,1)S(1)}, bf16[256,896]{1,0:T(8,128)(2,1)}, u32[]{:S(2)}, u32[]{:S(2)}) collective-permute-start(bf16[256,896]{1,0:T(8,128)(2,1)S(1)} %collective-permute-done.3.refs_4_), channel_id=1, source_target_pairs={{0,384},{128,0},{256,128},{384,256},{1,385},{129,1},{257,129},{385... | collective-permute-start | bytes 1376264 | tf_op jit(solution)/shard_map/ppermute | solution.py:155
  126.7 22.0 %collective-permute-start.6 = (bf16[256,896]{1,0:T(8,128)(2,1)S(1)}, bf16[256,896]{1,0:T(8,128)(2,1)}, u32[]{:S(2)}, u32[]{:S(2)}) collective-permute-start(bf16[256,896]{1,0:T(8,128)(2,1)S(1)} %collective-permute-done.3.refs_4_), channel_id=1, source_target_pairs={{0,256},{128,384},{256,0},{384,128},{1,257},{129,385},{257,1},{385... | collective-permute-start | bytes 1376264 | tf_op jit(solution)/shard_map/ppermute | solution.py:155
  130.9 20.2 %collective-permute-start.11 = (bf16[256,896]{1,0:T(8,128)(2,1)S(1)}, bf16[256,896]{1,0:T(8,128)(2,1)S(1)}, u32[]{:S(2)}, u32[]{:S(2)}) collective-permute-start(bf16[256,896]{1,0:T(8,128)(2,1)S(1)} %collective-permute-done.3.refs_4_), channel_id=1, source_target_pairs={{0,32},{32,0},{1,33},{33,1},{2,34},{34,2},{3,35},{35,3},{4,36},{36... | collective-permute-start | bytes 1376264 | tf_op jit(solution)/shard_map/ppermute | solution.py:159
  142.4 11.5 %collective-permute-start.10 = (bf16[256,896]{1,0:T(8,128)(2,1)S(1)}, bf16[256,896]{1,0:T(8,128)(2,1)S(1)}, u32[]{:S(2)}, u32[]{:S(2)}) collective-permute-start(bf16[256,896]{1,0:T(8,128)(2,1)S(1)} %collective-permute-done.2.refs_3_), channel_id=1, source_target_pairs={{0,32},{32,0},{1,33},{33,1},{2,34},{34,2},{3,35},{35,3},{4,36},{36... | collective-permute-start | bytes 1376264 | tf_op jit(solution)/shard_map/ppermute | solution.py:159
  144.3 14.0 %collective-permute-start.8 = (bf16[256,896]{1,0:T(8,128)(2,1)S(1)}, bf16[256,896]{1,0:T(8,128)(2,1)}, u32[]{:S(2)}, u32[]{:S(2)}) collective-permute-start(bf16[256,896]{1,0:T(8,128)(2,1)S(1)} %collective-permute-done.refs_1_), channel_id=1, source_target_pairs={{0,32},{32,0},{1,33},{33,1},{2,34},{34,2},{3,35},{35,3},{4,36},{36... | collective-permute-start | bytes 1376264 | tf_op jit(solution)/shard_map/ppermute | solution.py:159
  146.8 11.6 %collective-permute-start.9 = (bf16[256,896]{1,0:T(8,128)(2,1)S(1)}, bf16[256,896]{1,0:T(8,128)(2,1)}, u32[]{:S(2)}, u32[]{:S(2)}) collective-permute-start(bf16[256,896]{1,0:T(8,128)(2,1)S(1)} %collective-permute-done.1.refs_2_), channel_id=1, source_target_pairs={{0,32},{32,0},{1,33},{33,1},{2,34},{34,2},{3,35},{35,3},{4,36},{36... | collective-permute-start | bytes 1376264 | tf_op jit(solution)/shard_map/ppermute | solution.py:159
  148.7 9.7 %collective-permute-start.12 = (bf16[256,896]{1,0:T(8,128)(2,1)}, bf16[256,896]{1,0:T(8,128)(2,1)}, u32[]{:S(2)}, u32[]{:S(2)}) collective-permute-start(bf16[256,896]{1,0:T(8,128)(2,1)} %collective-permute-done.4.refs_5_), channel_id=1, source_target_pairs={{0,32},{32,0},{1,33},{33,1},{2,34},{34,2},{3,35},{35,3},{4,36},{36... | collective-permute-start | bytes 1376264 | tf_op jit(solution)/shard_map/ppermute | solution.py:159
  152.0 6.4 %collective-permute-start.13 = (bf16[256,896]{1,0:T(8,128)(2,1)}, bf16[256,896]{1,0:T(8,128)(2,1)}, u32[]{:S(2)}, u32[]{:S(2)}) collective-permute-start(bf16[256,896]{1,0:T(8,128)(2,1)} %collective-permute-done.5.refs_6_), channel_id=1, source_target_pairs={{0,32},{32,0},{1,33},{33,1},{2,34},{34,2},{3,35},{35,3},{4,36},{36... | collective-permute-start | bytes 1376264 | tf_op jit(solution)/shard_map/ppermute | solution.py:159
  154.7 4.2 %collective-permute-start.14 = (bf16[256,896]{1,0:T(8,128)(2,1)}, bf16[256,896]{1,0:T(8,128)(2,1)}, u32[]{:S(2)}, u32[]{:S(2)}) collective-permute-start(bf16[256,896]{1,0:T(8,128)(2,1)} %collective-permute-done.6.refs_7_), channel_id=1, source_target_pairs={{0,32},{32,0},{1,33},{33,1},{2,34},{34,2},{3,35},{35,3},{4,36},{36... | collective-permute-start | bytes 1376264 | tf_op jit(solution)/shard_map/ppermute | solution.py:159
  158.8 1.0 copy-start.2
  159.8 1.0 copy-start.4
  160.9 1.0 copy-start.6
  161.9 0.9 copy-start.8
  162.8 0.9 copy-start.10
  163.8 0.9 copy-start.12
  164.7 0.9 copy-start.14
  165.7 0.9 copy-start.16
  166.6 0.9 copy-start.18
  167.6 0.9 copy-start.20
  168.5 0.9 copy-start.22
  169.5 0.9 copy-start.24
  170.4 0.9 copy-start.26
  171.4 0.9 copy-start.28
  172.3 0.9 copy-start.30
  174.1 0.9 copy-start.34
  175.0 0.9 copy-start.36
  175.9 0.9 copy-start.38
  193.0 29.0 %copy-start.45 = (bf16[1,8,4096]{2,1,0:T(8,128)(2,1)S(1)}, bf16[1,8,4096]{2,1,0:T(8,128)(2,1)}, u32[]{:S(2)}) copy-start(bf16[1,8,4096]{2,1,0:T(8,128)(2,1)} %param.14) | copy-start | bytes 196612
  193.0 29.0 %copy-start.46 = (bf16[1,8,4096]{2,1,0:T(8,128)(2,1)S(1)}, bf16[1,8,4096]{2,1,0:T(8,128)(2,1)}, u32[]{:S(2)}) copy-start(bf16[1,8,4096]{2,1,0:T(8,128)(2,1)} %param.11) | copy-start | bytes 196612
  193.0 39.7 %all-to-all-start = ((f32[32,8,128]{2,1,0:T(8,128)}), f32[32,8,128]{2,1,0:T(8,128)S(1)}, u32[]{:S(2)}, u32[]{:S(2)}) async-start(f32[32,8,128]{2,1,0:T(8,128)} %mlp.1), calls=%async_computation | async-start | bytes 262144 | tf_op jit(solution)/shard_map/all_to_all | solution.py:176
  236.2 25.4 %copy-start.47 = (f32[8,128]{1,0:T(8,128)S(1)}, f32[8,128]{1,0:T(8,128)}, u32[]{:S(2)}) copy-start(f32[8,128]{1,0:T(8,128)} %get-tuple-element.7) | copy-start | bytes 12292
  (19 other events, 13.9 us)

commit v2 on v1

v2 whole, which is shorter than its diff:
```python
import functools

import jax
import jax.numpy as jnp
from jax import lax
from jax.experimental import pallas as pl
from jax.experimental.pallas import tpu as pltpu
from jax.sharding import Mesh, PartitionSpec as P

RANK = 64
NX, NZH, NCO, NZL, NY = 4, 2, 2, 8, 4
HIGH = lax.Precision.HIGHEST


def mlp_kernel(nx, nw, cols_ref, slot_ref, *refs):
    x_refs = refs[:nx]
    w_refs = refs[nx : nx + nw]
    ip_ref, out_ref, xv, wv, acc, xsem, wsem = refs[nx + nw :]
    copies, at = [], 0
    for i, x_ref in enumerate(x_refs):
        n = x_ref.shape[0]
        copies.append(pltpu.make_async_copy(x_ref, xv.at[pl.ds(at, n)], xsem.at[i]))
        at += n
    loads = [pltpu.make_async_copy(w_refs[p], wv.at[p], wsem.at[p]) for p in range(nw)]
    for c in copies:
        c.start()
    for c in loads:
        c.start()
    for c in copies:
        c.wait()
    for p in range(nw):
        loads[p].wait()
        picked = []
        for j in range(4):
            col = pl.multiple_of(cols_ref[p * 4 + j] * 256, 256)
            picked.append(xv[:, pl.ds(col, 256)])
        part = jnp.dot(
            jnp.concatenate(picked, axis=1),
            wv[p].reshape(1024, wv.shape[3]),
            preferred_element_type=jnp.float32,
        )
        if p == 0:
            acc[...] = part
        else:
            acc[...] += part
    half = acc.shape[1] // 2
    for m in range(4):
        rows = acc[m * 128 : (m + 1) * 128, :]
        gate, up = rows[:, :half], rows[:, half:]
        act = (gate / (1.0 + jnp.exp(-gate)) * up).astype(jnp.bfloat16)
        left = jnp.dot(act, ip_ref[...], preferred_element_type=jnp.float32)
        left = left.reshape(8, 2, 8, RANK)
        left = jnp.concatenate([left[:, 0], left[:, 1]], axis=-1)
        for i in range(8):
            out_ref[slot_ref[m * 8 + i]] = left[i]


def mlp(cols, slots, xs, ws, ip):
    any_ = pl.BlockSpec(memory_space=pl.ANY)
    smem = pl.BlockSpec(memory_space=pltpu.SMEM)
    nx, nw = len(xs), len(ws)
    return pl.pallas_call(
        functools.partial(mlp_kernel, nx, nw),
        out_shape=jax.ShapeDtypeStruct((32, 8, 2 * RANK), jnp.float32),
        in_specs=[smem, smem] + [any_] * (nx + nw) + [pl.BlockSpec(memory_space=pltpu.VMEM)],
        out_specs=pl.BlockSpec(memory_space=pltpu.VMEM),
        scratch_shapes=[
            pltpu.VMEM((512, xs[0].shape[1]), jnp.bfloat16),
            pltpu.VMEM((nw,) + ws[0].shape, jnp.bfloat16),
            pltpu.VMEM((512, ws[0].shape[2]), jnp.float32),
            pltpu.SemaphoreType.DMA((nx,)),
            pltpu.SemaphoreType.DMA((nw,)),
        ],
        compiler_params=pltpu.CompilerParams(vmem_limit_bytes=60 << 20),
        name="mlp",
    )(cols, slots, *xs, *ws, ip)


def norm_kernel(parts_ref, right_ref, live_ref, train_ref, roll_ref):
    left = jnp.sum(parts_ref[...], axis=0)
    for s, ref in ((0, train_ref), (1, roll_ref)):
        one = left[:, s * RANK : (s + 1) * RANK] * live_ref[s]
        right = right_ref[s]
        grad = lax.dot_general(
            one, right, (((0,), (0,)), ((), ())), precision=HIGH, preferred_element_type=jnp.float32
        )
        mean = jnp.sum(grad * grad) / (RANK * RANK)
        inv = 1.0 / jnp.sqrt(jnp.full((8, RANK), mean + 1e-6))
        ref[...] = jnp.concatenate([one * inv, right], axis=-1)


def score_kernel(train_ref, roll_ref, out_ref):
    t = train_ref[...].reshape(-1, 2 * RANK)
    r = roll_ref[...].reshape(-1, 2 * RANK)
    dims = (((1,), (1,)), ((), ()))
    a = lax.dot_general(
        t[:, :RANK], r[:, :RANK], dims, precision=HIGH, preferred_element_type=jnp.float32
    )
    b = lax.dot_general(
        t[:, RANK:], r[:, RANK:], dims, precision=HIGH, preferred_element_type=jnp.float32
    )
    both = jnp.sum((a * b).reshape(32, 8, 128), axis=1)
    pick = (
        lax.broadcasted_iota(jnp.int32, (128, 16), 0) // 8
        == lax.broadcasted_iota(jnp.int32, (128, 16), 1)
    ).astype(jnp.float32)
    out_ref[...] = jnp.dot(both, pick, precision=HIGH, preferred_element_type=jnp.float32) / RANK


def shift(n, k):
    return [(i, (i + k) % n) for i in range(n)]


def on_device(
    train_hidden,
    train_cotangent,
    train_lengths,
    roll_hidden,
    roll_cotangent,
    roll_lengths,
    gate_weight,
    up_weight,
    in_project,
    out_project,
):
    x, zh, co, zl, y = (lax.axis_index(a) for a in ("x", "zh", "co", "zl", "y"))
    width = train_hidden.shape[2]
    own = jnp.concatenate([train_hidden[0], roll_hidden[0]], axis=0)
    w = jnp.concatenate([gate_weight, up_weight], axis=1)

    other = lax.ppermute(w, "zh", shift(2, 1))

    block, zls = own, [zl]
    for k in (4, 2):
        got = lax.ppermute(block, "zl", [(i, i ^ k) for i in range(NZL)])
        block, zls = jnp.concatenate([block, got], axis=0), zls + [z ^ k for z in zls]
    twin = lax.ppermute(block, "zl", [(i, i ^ 1) for i in range(NZL)])

    first, second = [1, 0, 3, 2], [3, 2, 1, 0]
    step1 = [(c * NY + i, c * NY + (first, second)[c][i]) for c in range(2) for i in range(NY)]
    step2 = [(c * NY + i, c * NY + (second, first)[c][i]) for c in range(2) for i in range(NY)]
    y1 = jnp.where(co == 0, y ^ 1, 3 - y)
    y2 = jnp.where(co == 0, 3 - y, y ^ 1)
    y3 = y ^ 2
    xs, slots = [], []
    for part, at in ((block, zls), (twin, [z ^ 1 for z in zls])):
        got = lax.ppermute(part, ("co", "y"), step1)
        both = jnp.concatenate([part, got], axis=0)
        xs += [both, lax.ppermute(both, ("co", "y"), step2)]
        slots += [z * NY + o for o in (y, y1, y2, y3) for z in at]

    def over_x(a):
        spread = jnp.broadcast_to(a, (NX,) + a.shape)
        return lax.all_to_all(spread, "x", 0, 0, tiled=True)

    ws, cols = [], []
    for a, h in ((w, zh), (other, 1 - zh)):
        a = over_x(a)
        ws += [a, lax.ppermute(a, "co", shift(2, 1))]
        cols += [i * 4 + h * 2 + c for c in (co, 1 - co) for i in range(NX)]

    parts = mlp(
        jnp.stack(cols).astype(jnp.int32), jnp.stack(slots).astype(jnp.int32), xs, ws, in_project
    )
    cot = jnp.concatenate([train_cotangent[0], roll_cotangent[0]], axis=0)
    right = jnp.dot(cot, out_project, preferred_element_type=jnp.float32).reshape(2, 8, RANK)
    lengths = jnp.stack([train_lengths, roll_lengths])
    live = (jnp.arange(8, dtype=jnp.int32)[None, :] < lengths).astype(jnp.float32)[:, :, None]
    live = jnp.broadcast_to(live, (2, 8, RANK))

    parts = lax.all_to_all(parts, ("zl", "y"), 0, 0, tiled=True)
    small = jax.ShapeDtypeStruct((8, 2 * RANK), jnp.float32)
    train, roll = pl.pallas_call(norm_kernel, out_shape=(small, small), name="norm")(
        parts, right, live
    )
    far = lax.ppermute(roll, "zh", shift(2, 1))
    train_all = lax.all_to_all(
        jnp.broadcast_to(train, (32, 8, 2 * RANK)), ("zl", "y"), 0, 0, tiled=True
    )
    pair = jnp.where(zh == 0, jnp.stack([roll, far]), jnp.stack([far, roll]))
    roll_all = lax.all_to_all(
        jnp.broadcast_to(pair, (8, 2, 8, 2 * RANK)), ("x", "co"), 0, 0, tiled=True
    )
    roll_all = roll_all.reshape(NX, NCO, NZH, 8, 2 * RANK).transpose(0, 2, 1, 3, 4)
    roll_all = roll_all.reshape(16, 8, 2 * RANK)
    return pl.pallas_call(
        score_kernel, out_shape=jax.ShapeDtypeStruct((32, 16), jnp.float32), name="score"
    )(train_all, roll_all)


def solution(mesh):
    fine = Mesh(mesh.devices.reshape(NX, NZH, NCO, NZL, NY), ("x", "zh", "co", "zl", "y"))
    rows, cols = ("x", "zh", "co"), ("zl", "y")
    placed = (
        P(rows + cols, None, None),
        P(rows + cols, None, None),
        P(rows + cols),
        P(cols + rows, None, None),
        P(cols + rows, None, None),
        P(cols + rows),
        P(rows, cols),
        P(rows, cols),
        P(cols, None),
        P(),
    )
    return jax.shard_map(
        on_device, mesh=fine, in_specs=placed, out_specs=P(rows, cols), check_vma=False
    )
```

time: 285 us -> 213 us (0.75)
  starting transfers between devices: 160 us -> 78.2 us
  waiting for transfers between devices: 20.2 us -> 81.2 us
  blocking collectives: 42.6 us -> 13.1 us
  local copies, waits for them, and re-layouts: 33.6 us -> 18.6 us
  Pallas kernels: 20.4 us -> 14.7 us
    ppermute x33 -> x10, starting transfers between devices: 119 us -> 45 us  [the longest x2 12.7 us: on_device(): got = lax.ppermute(block, 'zl', [(i, i ^ k) for i in range(NZL)])]
    ppermute x33 -> x10, waiting for transfers between devices: 0.5 us -> 44.1 us  [the longest x2 19.9 us: on_device(): got = lax.ppermute(block, 'zl', [(i, i ^ k) for i in range(NZL)])]
    all_to_all x2 -> x1, blocking collectives: 42.6 us -> 13.1 us  [on_device(): lax.all_to_all(jnp.broadcast_to(pair, (8, 2, 8, 2 * RANK)), ('x', 'co'),...]
    unnamed x99 -> x27, local copies, waits for them, and re-layouts: 30.6 us -> 6.11 us
    all_to_all x0 -> x3, waiting for transfers between devices: none -> 21.6 us  [the longest x1 11.5 us: on_device(): lax.all_to_all(jnp.broadcast_to(train, (32, 8, 2 * RANK)), ('zl', 'y'), 0...]
    all_to_all x1, starting transfers between devices: 27.6 us -> 9.28 us  [on_device(): parts = lax.all_to_all(parts, ('zl', 'y'), 0, 0, tiled=True)]
    all_to_all x0 -> x3, starting transfers between devices: none -> 13.3 us  [the longest x2 8.54 us: over_x(): return lax.all_to_all(spread, 'x', 0, 0, tiled=True)]
    pallas_call x1, Pallas kernels: 16.1 us -> 10.4 us  [mlp(): pl.pallas_call(functools.partial(mlp_kernel, nx, nw), out_shape=jax.Shape...]
  transfers between devices with their start and end apart: 35 -> 15, of which waited for: 3 -> 9; matrix products, arithmetic and copies ran while one was open for 1% -> 8% of each run, Pallas kernels for 0% -> 0%
where the time goes in v2:
time: 213 us; the launch traced here: 211 us
  waiting for transfers between devices  81.2 us (38%)
  starting transfers between devices  78.2 us (37%)
  local copies, waits for them, and re-layouts  18.6 us (9%)
  Pallas kernels  14.7 us (7%)
  blocking collectives  13.1 us (6%)
  other arithmetic  2.56 us (1%)
    ppermute x2, waiting for transfers between devices, on_device(): got = lax.ppermute(block, 'zl', [(i, i ^ k) for i in range(NZL)])  19.9 us
    ppermute x2, waiting for transfers between devices, on_device(): xs += [both, lax.ppermute(both, ('co', 'y'), step2)]  14.6 us
    all_to_all x1, blocking collectives, on_device(): lax.all_to_all(jnp.broadcast_to(pair, (8, 2, 8, 2 * RANK)), ('x', 'co'),...  13.1 us
    ppermute x2, starting transfers between devices, on_device(): got = lax.ppermute(block, 'zl', [(i, i ^ k) for i in range(NZL)])  12.7 us
    all_to_all x1, waiting for transfers between devices, on_device(): lax.all_to_all(jnp.broadcast_to(train, (32, 8, 2 * RANK)), ('zl', 'y'), 0...  11.5 us
    ppermute x1, starting transfers between devices, on_device(): far = lax.ppermute(roll, 'zh', shift(2, 1))  10.8 us
    ppermute x1, starting transfers between devices, on_device(): other = lax.ppermute(w, 'zh', shift(2, 1))  10.6 us
    pallas_call x1, Pallas kernels, mlp(): pl.pallas_call(functools.partial(mlp_kernel, nx, nw), out_shape=jax.Shape...  10.4 us
  transfers between devices with their start and end apart: 15, of which 9 were waited for; matrix products, arithmetic and copies ran while one was open for 8% of the time, Pallas kernels for 0%

profile of v2, /device:TPU:1, one launch (start us, length us, event | category | flops | bytes accessed | tf_op | source)
XLA Modules:
  0.0 210.8 jit_solution(4849558961641254391)
XLA Ops:
  0.0 0.9 pad_maximum_fusion.2
  0.9 9.6 %collective-permute-start = (bf16[16,4096]{1,0:T(8,128)(2,1)S(1)}, bf16[16,4096]{1,0:T(8,128)(2,1)S(1)}, u32[]{:S(2)}, u32[]{:S(2)}) collective-permute-start(bf16[16,4096]{1,0:T(8,128)(2,1)S(1)} %pad_maximum_fusion.2), channel_id=1, source_target_pairs={{0,16},{4,20},{8,24},{12,28},{16,0},{20,4},{24,8},{28,12},{1,17},{... | collective-permute-start | bytes 393224 | tf_op jit(solution)/shard_map/ppermute | solution.py:135
  10.6 1.0 constant_dynamic-update-slice_fusion.8
  11.6 1.0 constant_dynamic-update-slice_fusion.7
  12.5 10.6 %collective-permute-start.8 = (bf16[256,896]{0,1:T(8,128)(2,1)S(1)}, bf16[256,896]{0,1:T(8,128)(2,1)}, u32[]{:S(2)}, u32[]{:S(2)}) collective-permute-start(bf16[256,896]{0,1:T(8,128)(2,1)S(1)} %constant_dynamic-update-slice_fusion.7), channel_id=1, source_target_pairs={{0,64},{64,0},{1,65},{65,1},{2,66},{66,2},{3,67},{67,3},{4,68},{68... | collective-permute-start | bytes 1376264 | tf_op jit(solution)/shard_map/ppermute | solution.py:131
  23.2 0.2 copy.15
  23.4 1.4 broadcast_in_dim.19
  24.8 4.1 %all-to-all-start = ((bf16[4,256,896]{2,1,0:T(8,128)(2,1)}), bf16[4,256,896]{2,1,0:T(8,128)(2,1)S(1)}, u32[]{:S(2)}, u32[]{:S(2)}) async-start(bf16[4,256,896]{2,1,0:T(8,128)(2,1)} %broadcast_in_dim.19), calls=%async_computation | async-start | bytes 3670016 | tf_op jit(solution)/shard_map/all_to_all | solution.py:154
  29.0 0.6 constant_dynamic-update-slice_fusion.4
  29.6 0.0 collective-permute-done
  29.6 0.0 copy-done.4
  29.6 0.7 pad_maximum_fusion.1
  30.3 3.1 %collective-permute-start.1 = (bf16[32,4096]{1,0:T(8,128)(2,1)}, bf16[32,4096]{1,0:T(8,128)(2,1)S(1)}, u32[]{:S(2)}, u32[]{:S(2)}) collective-permute-start(bf16[32,4096]{1,0:T(8,128)(2,1)} %pad_maximum_fusion.1), channel_id=1, source_target_pairs={{0,8},{4,12},{8,0},{12,4},{16,24},{20,28},{24,16},{28,20},{1,9},{5... | collective-permute-start | bytes 786440 | tf_op jit(solution)/shard_map/ppermute | solution.py:135
  33.4 0.6 constant_dynamic-update-slice_fusion.3
  34.0 5.6 %collective-permute-done.8 = bf16[256,896]{0,1:T(8,128)(2,1)} collective-permute-done((bf16[256,896]{0,1:T(8,128)(2,1)S(1)}, bf16[256,896]{0,1:T(8,128)(2,1)}, u32[]{:S(2)}, u32[]{:S(2)}) %collective-permute-start.8) | collective-permute-done | bytes 458784 | tf_op jit(solution)/shard_map/ppermute | solution.py:131
  39.6 1.3 copy.16
  40.9 10.1 %all-to-all-done.refs_4_ = bf16[4,256,896]{2,1,0:T(8,128)(2,1)S(1)} async-done(((bf16[4,256,896]{2,1,0:T(8,128)(2,1)}), bf16[4,256,896]{2,1,0:T(8,128)(2,1)S(1)}, u32[]{:S(2)}, u32[]{:S(2)}) %all-to-all-start) | async-done | bytes 1835040 | tf_op jit(solution)/shard_map/all_to_all | solution.py:154
  51.0 1.5 broadcast_in_dim.20
  52.5 4.4 %all-to-all-start.1 = ((bf16[4,256,896]{2,1,0:T(8,128)(2,1)}), bf16[4,256,896]{2,1,0:T(8,128)(2,1)}, u32[]{:S(2)}, u32[]{:S(2)}) async-start(bf16[4,256,896]{2,1,0:T(8,128)(2,1)} %broadcast_in_dim.20), calls=%async_computation.1 | async-start | bytes 3670016 | tf_op jit(solution)/shard_map/all_to_all | solution.py:154
  56.9 19.9 %collective-permute-done.1 = bf16[32,4096]{1,0:T(8,128)(2,1)S(1)} collective-permute-done((bf16[32,4096]{1,0:T(8,128)(2,1)}, bf16[32,4096]{1,0:T(8,128)(2,1)S(1)}, u32[]{:S(2)}, u32[]{:S(2)}) %collective-permute-start.1) | collective-permute-done | bytes 262176 | tf_op jit(solution)/shard_map/ppermute | solution.py:135
  76.8 1.9 collective-permute-start.4
  78.7 4.6 %collective-permute-start.2 = (bf16[64,4096]{1,0:T(8,128)(2,1)S(1)}, bf16[64,4096]{1,0:T(8,128)(2,1)S(1)}, u32[]{:S(2)}, u32[]{:S(2)}) collective-permute-start(bf16[64,4096]{1,0:T(8,128)(2,1)S(1)} %pad_maximum_fusion), channel_id=1, source_target_pairs={{0,1},{1,0},{2,3},{3,2},{32,35},{33,34},{34,33},{35,32},{4,5},{5,4... | collective-permute-start | bytes 1572872 | tf_op jit(solution)/shard_map/ppermute | solution.py:147
  83.4 0.7 constant_dynamic-update-slice_fusion.2
  84.1 0.7 constant_dynamic-update-slice_fusion.1
  84.8 7.1 %collective-permute-done.4 = bf16[64,4096]{1,0:T(8,128)(2,1)} collective-permute-done((bf16[64,4096]{1,0:T(8,128)(2,1)S(1)}, bf16[64,4096]{1,0:T(8,128)(2,1)}, u32[]{:S(2)}, u32[]{:S(2)}) %collective-permute-start.4) | collective-permute-done | bytes 524320 | tf_op jit(solution)/shard_map/ppermute | solution.py:137
  91.9 4.6 %collective-permute-start.5 = (bf16[64,4096]{1,0:T(8,128)(2,1)}, bf16[64,4096]{1,0:T(8,128)(2,1)}, u32[]{:S(2)}, u32[]{:S(2)}) collective-permute-start(bf16[64,4096]{1,0:T(8,128)(2,1)} %collective-permute-done.4), channel_id=1, source_target_pairs={{0,1},{1,0},{2,3},{3,2},{32,35},{33,34},{34,33},{35,32},{4,5},{5,4... | collective-permute-start | bytes 1572872 | tf_op jit(solution)/shard_map/ppermute | solution.py:147
  96.6 0.0 collective-permute-done.2
  96.6 0.8 constant_dynamic-update-slice_fusion.refs_0_
  97.4 1.9 collective-permute-start.3
  99.3 4.1 %collective-permute-start.7 = (bf16[4,256,896]{2,1,0:T(8,128)(2,1)S(1)}, bf16[4,256,896]{2,1,0:T(8,128)(2,1)}, u32[]{:S(2)}, u32[]{:S(2)}) collective-permute-start(bf16[4,256,896]{2,1,0:T(8,128)(2,1)S(1)} %all-to-all-done.refs_4_), channel_id=1, source_target_pairs={{0,32},{32,0},{1,33},{33,1},{2,34},{34,2},{3,35},{35,3},{4,36},{36... | collective-permute-start | bytes 5505032 | tf_op jit(solution)/shard_map/ppermute | solution.py:159
  103.5 0.0 all-to-all-done.1.refs_6_
  103.5 1.9 collective-permute-start.9
  105.4 1.1 constant_dynamic-update-slice_fusion.6
  106.5 0.0 collective-permute-done.5
  106.5 1.1 constant_dynamic-update-slice_fusion.5.refs_2_
  107.6 2.3 %collective-permute-start.6 = (bf16[128,4096]{1,0:T(8,128)(2,1)S(1)}, bf16[128,4096]{1,0:T(8,128)(2,1)}, u32[]{:S(2)}, u32[]{:S(2)}) collective-permute-start(bf16[128,4096]{1,0:T(8,128)(2,1)S(1)} %constant_dynamic-update-slice_fusion.5.refs_2_), channel_id=1, source_target_pairs={{0,3},{1,2},{2,1},{3,0},{32,33},{33,32},{34,35},{35,34},{4,7},{5,6... | collective-permute-start | bytes 3145736 | tf_op jit(solution)/shard_map/ppermute | solution.py:149
  110.0 0.8 copy.17.refs_8_
  110.8 0.6 stack.191.cols_ref
  111.4 0.6 stack.224.slot_ref
  112.0 3.3 %collective-permute-done.3.refs_1_ = bf16[128,4096]{1,0:T(8,128)(2,1)} collective-permute-done((bf16[128,4096]{1,0:T(8,128)(2,1)}, bf16[128,4096]{1,0:T(8,128)(2,1)}, u32[]{:S(2)}, u32[]{:S(2)}) %collective-permute-start.3) | collective-permute-done | bytes 1048608 | tf_op jit(solution)/shard_map/ppermute | solution.py:149
  115.3 11.3 %collective-permute-done.6.refs_3_ = bf16[128,4096]{1,0:T(8,128)(2,1)} collective-permute-done((bf16[128,4096]{1,0:T(8,128)(2,1)S(1)}, bf16[128,4096]{1,0:T(8,128)(2,1)}, u32[]{:S(2)}, u32[]{:S(2)}) %collective-permute-start.6) | collective-permute-done | bytes 1048608 | tf_op jit(solution)/shard_map/ppermute | solution.py:149
  126.6 0.0 collective-permute-done.7.refs_5_
  126.6 0.0 collective-permute-done.9.refs_7_
  126.6 10.4 %mlp.1 = f32[32,8,128]{2,1,0:T(8,128)} custom-call(s32[16]{0:T(128)} %stack.191.cols_ref, s32[32]{0:T(128)} %stack.224.slot_ref, bf16[128,4096]{1,0:T(8,128)(2,1)} %constant_dynamic-update-slice_fusion.refs_0_, bf16[128,4096]{1,0:T(8,128)(2,1)} %collective-permute-done.3.refs_1_, bf16[128,4096]{1,0:T(8,128)(2,1)} %copy-done.2, ...), custom_call_target="tpu_custom_call" | custom-call | tf_op jit(solution)/shard_map/mlp/pallas_call | solution.py:62
  137.1 9.3 %all-to-all-start.2 = ((f32[32,8,128]{2,1,0:T(8,128)}), f32[32,8,128]{2,1,0:T(8,128)S(1)}, u32[]{:S(2)}, u32[]{:S(2)}) async-start(f32[32,8,128]{2,1,0:T(8,128)} %mlp.1), calls=%async_computation.2 | async-start | bytes 262144 | tf_op jit(solution)/shard_map/all_to_all | solution.py:171
  147.7 0.1 add_bitcast_fusion
  147.7 0.0 copy-done.9
  147.8 0.9 convolution_bitcast_fusion.right_ref
  148.6 0.1 compare_convert_fusion
  148.7 9.8 %all-to-all-done.2.parts_ref = f32[32,8,128]{2,1,0:T(8,128)S(1)} async-done(((f32[32,8,128]{2,1,0:T(8,128)}), f32[32,8,128]{2,1,0:T(8,128)S(1)}, u32[]{:S(2)}, u32[]{:S(2)}) %all-to-all-start.2) | async-done | bytes 131104 | tf_op jit(solution)/shard_map/all_to_all | solution.py:171
  158.5 0.7 broadcast_in_dim.21.live_ref
  159.2 0.0 copy-done.5
  159.2 2.1 norm.1
  161.2 10.8 %collective-permute-start.10 = (f32[8,128]{1,0:T(8,128)}, f32[8,128]{1,0:T(8,128)S(1)}, u32[]{:S(2)}, u32[]{:S(2)}) collective-permute-start(f32[8,128]{1,0:T(8,128)} %get-tuple-element.8), channel_id=1, source_target_pairs={{0,64},{64,0},{1,65},{65,1},{2,66},{66,2},{3,67},{67,3},{4,68},{68... | collective-permute-start | bytes 12296 | tf_op jit(solution)/shard_map/ppermute | solution.py:176
  172.0 2.5 %collective-permute-done.10 = f32[8,128]{1,0:T(8,128)S(1)} collective-permute-done((f32[8,128]{1,0:T(8,128)}, f32[8,128]{1,0:T(8,128)S(1)}, u32[]{:S(2)}, u32[]{:S(2)}) %collective-permute-start.10) | collective-permute-done | bytes 4128 | tf_op jit(solution)/shard_map/ppermute | solution.py:176
  174.5 0.7 maximum_select_fusion
  175.3 13.1 %all_to_all.25 = f32[8,2,8,128]{3,2,1,0:T(8,128)S(1)} all-to-all(f32[8,2,8,128]{3,2,1,0:T(8,128)S(1)} %broadcast_in_dim.23), channel_id=1, replica_groups=mesh['x'=4,'zh'=2,'co'=2,'zl'=8,'y'=4] {'x','co'}, dimensions={0} | all-to-all | bytes 131072 | tf_op jit(solution)/shard_map/all_to_all | solution.py:181
  188.4 1.3 broadcast_in_dim.22
  189.7 4.8 %all-to-all-start.3 = ((f32[32,8,128]{2,1,0:T(8,128)}), f32[32,8,128]{2,1,0:T(8,128)S(1)}, u32[]{:S(2)}, u32[]{:S(2)}) async-start(f32[32,8,128]{2,1,0:T(8,128)} %broadcast_in_dim.22), calls=%async_computation.3 | async-start | bytes 262144 | tf_op jit(solution)/shard_map/all_to_all | solution.py:177
  194.5 0.6 copy.18
  195.1 11.5 %all-to-all-done.3.train_ref = f32[32,8,128]{2,1,0:T(8,128)S(1)} async-done(((f32[32,8,128]{2,1,0:T(8,128)}), f32[32,8,128]{2,1,0:T(8,128)S(1)}, u32[]{:S(2)}, u32[]{:S(2)}) %all-to-all-start.3) | async-done | bytes 131104 | tf_op jit(solution)/shard_map/all_to_all | solution.py:177
  206.6 0.6 copy-done.6
  207.3 2.1 %score.1 = f32[32,16]{1,0:T(8,128)} custom-call(f32[32,8,128]{2,1,0:T(8,128)} %copy-done.6, f32[16,8,128]{2,1,0:T(8,128)} %bitcast.76), custom_call_target="tpu_custom_call" | custom-call | tf_op jit(solution)/shard_map/score/pallas_call | solution.py:186
  209.4 1.4 copy.19
  (18 shorter events, 0.1 us)
Async XLA Ops:
  0.0 147.7 %copy-start = (bf16[4096,64]{0,1:T(8,128)(2,1)S(1)}, bf16[4096,64]{0,1:T(8,128)(2,1)}, u32[]{:S(2)}) copy-start(bf16[4096,64]{0,1:T(8,128)(2,1)} %param.19) | copy-start | bytes 1572868
  0.9 28.6 %collective-permute-start = (bf16[16,4096]{1,0:T(8,128)(2,1)S(1)}, bf16[16,4096]{1,0:T(8,128)(2,1)S(1)}, u32[]{:S(2)}, u32[]{:S(2)}) collective-permute-start(bf16[16,4096]{1,0:T(8,128)(2,1)S(1)} %pad_maximum_fusion.2), channel_id=1, source_target_pairs={{0,16},{4,20},{8,24},{12,28},{16,0},{20,4},{24,8},{28,12},{1,17},{... | collective-permute-start | bytes 393224 | tf_op jit(solution)/shard_map/ppermute | solution.py:135
  12.5 27.1 %collective-permute-start.8 = (bf16[256,896]{0,1:T(8,128)(2,1)S(1)}, bf16[256,896]{0,1:T(8,128)(2,1)}, u32[]{:S(2)}, u32[]{:S(2)}) collective-permute-start(bf16[256,896]{0,1:T(8,128)(2,1)S(1)} %constant_dynamic-update-slice_fusion.7), channel_id=1, source_target_pairs={{0,64},{64,0},{1,65},{65,1},{2,66},{66,2},{3,67},{67,3},{4,68},{68... | collective-permute-start | bytes 1376264 | tf_op jit(solution)/shard_map/ppermute | solution.py:131
  24.8 4.2 %copy-start.3 = (bf16[1,8,4096]{2,1,0:T(8,128)(2,1)S(1)}, bf16[1,8,4096]{2,1,0:T(8,128)(2,1)}, u32[]{:S(2)}) copy-start(bf16[1,8,4096]{2,1,0:T(8,128)(2,1)} %param.10) | copy-start | bytes 196612
  24.8 4.8 %copy-start.4 = (bf16[1,8,4096]{2,1,0:T(8,128)(2,1)S(1)}, bf16[1,8,4096]{2,1,0:T(8,128)(2,1)}, u32[]{:S(2)}) copy-start(bf16[1,8,4096]{2,1,0:T(8,128)(2,1)} %param.13) | copy-start | bytes 196612
  24.8 26.2 %all-to-all-start = ((bf16[4,256,896]{2,1,0:T(8,128)(2,1)}), bf16[4,256,896]{2,1,0:T(8,128)(2,1)S(1)}, u32[]{:S(2)}, u32[]{:S(2)}) async-start(bf16[4,256,896]{2,1,0:T(8,128)(2,1)} %broadcast_in_dim.19), calls=%async_computation | async-start | bytes 3670016 | tf_op jit(solution)/shard_map/all_to_all | solution.py:154
  30.3 46.5 %collective-permute-start.1 = (bf16[32,4096]{1,0:T(8,128)(2,1)}, bf16[32,4096]{1,0:T(8,128)(2,1)S(1)}, u32[]{:S(2)}, u32[]{:S(2)}) collective-permute-start(bf16[32,4096]{1,0:T(8,128)(2,1)} %pad_maximum_fusion.1), channel_id=1, source_target_pairs={{0,8},{4,12},{8,0},{12,4},{16,24},{20,28},{24,16},{28,20},{1,9},{5... | collective-permute-start | bytes 786440 | tf_op jit(solution)/shard_map/ppermute | solution.py:135
  51.0 48.3 %copy-start.1 = (bf16[4,256,896]{2,1,0:T(8,128)(2,1)}, bf16[4,256,896]{2,1,0:T(8,128)(2,1)S(1)}, u32[]{:S(2)}) copy-start(bf16[4,256,896]{2,1,0:T(8,128)(2,1)S(1)} %all-to-all-done.refs_4_) | copy-start | bytes 5505028
  52.5 51.0 %all-to-all-start.1 = ((bf16[4,256,896]{2,1,0:T(8,128)(2,1)}), bf16[4,256,896]{2,1,0:T(8,128)(2,1)}, u32[]{:S(2)}, u32[]{:S(2)}) async-start(bf16[4,256,896]{2,1,0:T(8,128)(2,1)} %broadcast_in_dim.20), calls=%async_computation.1 | async-start | bytes 3670016 | tf_op jit(solution)/shard_map/all_to_all | solution.py:154
  76.8 15.1 %collective-permute-start.4 = (bf16[64,4096]{1,0:T(8,128)(2,1)S(1)}, bf16[64,4096]{1,0:T(8,128)(2,1)}, u32[]{:S(2)}, u32[]{:S(2)}) collective-permute-start(bf16[64,4096]{1,0:T(8,128)(2,1)S(1)} %pad_maximum_fusion), channel_id=1, source_target_pairs={{0,4},{4,0},{8,12},{12,8},{16,20},{20,16},{24,28},{28,24},{1,5},{5... | collective-permute-start | bytes 1572872 | tf_op jit(solution)/shard_map/ppermute | solution.py:137
  78.7 17.8 %collective-permute-start.2 = (bf16[64,4096]{1,0:T(8,128)(2,1)S(1)}, bf16[64,4096]{1,0:T(8,128)(2,1)S(1)}, u32[]{:S(2)}, u32[]{:S(2)}) collective-permute-start(bf16[64,4096]{1,0:T(8,128)(2,1)S(1)} %pad_maximum_fusion), channel_id=1, source_target_pairs={{0,1},{1,0},{2,3},{3,2},{32,35},{33,34},{34,33},{35,32},{4,5},{5,4... | collective-permute-start | bytes 1572872 | tf_op jit(solution)/shard_map/ppermute | solution.py:147
  84.1 25.9 %copy-start.7 = (bf16[448,64]{0,1:T(8,128)(2,1)S(1)}, bf16[448,64]{0,1:T(8,128)(2,1)}, u32[]{:S(2)}) copy-start(bf16[448,64]{0,1:T(8,128)(2,1)} %param.18) | copy-start | bytes 172036
  91.9 14.6 %collective-permute-start.5 = (bf16[64,4096]{1,0:T(8,128)(2,1)}, bf16[64,4096]{1,0:T(8,128)(2,1)}, u32[]{:S(2)}, u32[]{:S(2)}) collective-permute-start(bf16[64,4096]{1,0:T(8,128)(2,1)} %collective-permute-done.4), channel_id=1, source_target_pairs={{0,1},{1,0},{2,3},{3,2},{32,35},{33,34},{34,33},{35,32},{4,5},{5,4... | collective-permute-start | bytes 1572872 | tf_op jit(solution)/shard_map/ppermute | solution.py:147
  97.4 17.9 %collective-permute-start.3 = (bf16[128,4096]{1,0:T(8,128)(2,1)}, bf16[128,4096]{1,0:T(8,128)(2,1)}, u32[]{:S(2)}, u32[]{:S(2)}) collective-permute-start(bf16[128,4096]{1,0:T(8,128)(2,1)} %constant_dynamic-update-slice_fusion.refs_0_), channel_id=1, source_target_pairs={{0,3},{1,2},{2,1},{3,0},{32,33},{33,32},{34,35},{35,34},{4,7},{5,6... | collective-permute-start | bytes 3145736 | tf_op jit(solution)/shard_map/ppermute | solution.py:149
  99.3 27.3 %collective-permute-start.7 = (bf16[4,256,896]{2,1,0:T(8,128)(2,1)S(1)}, bf16[4,256,896]{2,1,0:T(8,128)(2,1)}, u32[]{:S(2)}, u32[]{:S(2)}) collective-permute-start(bf16[4,256,896]{2,1,0:T(8,128)(2,1)S(1)} %all-to-all-done.refs_4_), channel_id=1, source_target_pairs={{0,32},{32,0},{1,33},{33,1},{2,34},{34,2},{3,35},{35,3},{4,36},{36... | collective-permute-start | bytes 5505032 | tf_op jit(solution)/shard_map/ppermute | solution.py:159
  103.5 23.1 %collective-permute-start.9 = (bf16[4,256,896]{2,1,0:T(8,128)(2,1)}, bf16[4,256,896]{2,1,0:T(8,128)(2,1)}, u32[]{:S(2)}, u32[]{:S(2)}) collective-permute-start(bf16[4,256,896]{2,1,0:T(8,128)(2,1)} %all-to-all-done.1.refs_6_), channel_id=1, source_target_pairs={{0,32},{32,0},{1,33},{33,1},{2,34},{34,2},{3,35},{35,3},{4,36},{36... | collective-permute-start | bytes 5505032 | tf_op jit(solution)/shard_map/ppermute | solution.py:159
  107.6 19.0 %copy-start.2 = (bf16[128,4096]{1,0:T(8,128)(2,1)}, bf16[128,4096]{1,0:T(8,128)(2,1)S(1)}, u32[]{:S(2)}) copy-start(bf16[128,4096]{1,0:T(8,128)(2,1)S(1)} %constant_dynamic-update-slice_fusion.5.refs_2_) | copy-start | bytes 3145732
  107.6 19.0 %collective-permute-start.6 = (bf16[128,4096]{1,0:T(8,128)(2,1)S(1)}, bf16[128,4096]{1,0:T(8,128)(2,1)}, u32[]{:S(2)}, u32[]{:S(2)}) collective-permute-start(bf16[128,4096]{1,0:T(8,128)(2,1)S(1)} %constant_dynamic-update-slice_fusion.5.refs_2_), channel_id=1, source_target_pairs={{0,3},{1,2},{2,1},{3,0},{32,33},{33,32},{34,35},{35,34},{4,7},{5,6... | collective-permute-start | bytes 3145736 | tf_op jit(solution)/shard_map/ppermute | solution.py:149
  112.0 35.7 %copy-start.8 = (bf16[1,8,4096]{2,1,0:T(8,128)(2,1)S(1)}, bf16[1,8,4096]{2,1,0:T(8,128)(2,1)}, u32[]{:S(2)}) copy-start(bf16[1,8,4096]{2,1,0:T(8,128)(2,1)} %param.14) | copy-start | bytes 196612
  112.0 35.7 %copy-start.9 = (bf16[1,8,4096]{2,1,0:T(8,128)(2,1)S(1)}, bf16[1,8,4096]{2,1,0:T(8,128)(2,1)}, u32[]{:S(2)}) copy-start(bf16[1,8,4096]{2,1,0:T(8,128)(2,1)} %param.11) | copy-start | bytes 196612
  137.1 21.4 %all-to-all-start.2 = ((f32[32,8,128]{2,1,0:T(8,128)}), f32[32,8,128]{2,1,0:T(8,128)S(1)}, u32[]{:S(2)}, u32[]{:S(2)}) async-start(f32[32,8,128]{2,1,0:T(8,128)} %mlp.1), calls=%async_computation.2 | async-start | bytes 262144 | tf_op jit(solution)/shard_map/all_to_all | solution.py:171
  158.5 0.7 copy-start.5
  161.2 13.3 %collective-permute-start.10 = (f32[8,128]{1,0:T(8,128)}, f32[8,128]{1,0:T(8,128)S(1)}, u32[]{:S(2)}, u32[]{:S(2)}) collective-permute-start(f32[8,128]{1,0:T(8,128)} %get-tuple-element.8), channel_id=1, source_target_pairs={{0,64},{64,0},{1,65},{65,1},{2,66},{66,2},{3,67},{67,3},{4,68},{68... | collective-permute-start | bytes 12296 | tf_op jit(solution)/shard_map/ppermute | solution.py:176
  189.7 16.9 %all-to-all-start.3 = ((f32[32,8,128]{2,1,0:T(8,128)}), f32[32,8,128]{2,1,0:T(8,128)S(1)}, u32[]{:S(2)}, u32[]{:S(2)}) async-start(f32[32,8,128]{2,1,0:T(8,128)} %broadcast_in_dim.22), calls=%async_computation.3 | async-start | bytes 262144 | tf_op jit(solution)/shard_map/all_to_all | solution.py:177
  206.6 0.7 copy-start.6

commit v3 on v2

--- a/solution.py
+++ b/solution.py
@@ -21,22 +21,26 @@
         n = x_ref.shape[0]
         copies.append(pltpu.make_async_copy(x_ref, xv.at[pl.ds(at, n)], xsem.at[i]))
         at += n
-    loads = [pltpu.make_async_copy(w_refs[p], wv.at[p], wsem.at[p]) for p in range(nw)]
+    loads, at = [], 0
+    for p, w_ref in enumerate(w_refs):
+        depth = w_ref.shape[1]
+        loads.append((pltpu.make_async_copy(w_ref, wv.at[pl.ds(at, 4), pl.ds(0, depth)], wsem.at[p]), at, depth))
+        at += 4
     for c in copies:
         c.start()
-    for c in loads:
+    for c, _, _ in loads:
         c.start()
     for c in copies:
         c.wait()
-    for p in range(nw):
-        loads[p].wait()
+    for p, (c, at, depth) in enumerate(loads):
+        c.wait()
         picked = []
         for j in range(4):
-            col = pl.multiple_of(cols_ref[p * 4 + j] * 256, 256)
-            picked.append(xv[:, pl.ds(col, 256)])
+            col = pl.multiple_of(cols_ref[p * 4 + j], 128)
+            picked.append(xv[:, pl.ds(col, depth)])
         part = jnp.dot(
             jnp.concatenate(picked, axis=1),
-            wv[p].reshape(1024, wv.shape[3]),
+            wv[at : at + 4, :depth].reshape(4 * depth, wv.shape[2]),
             preferred_element_type=jnp.float32,
         )
         if p == 0:
@@ -66,7 +70,7 @@
         out_specs=pl.BlockSpec(memory_space=pltpu.VMEM),
         scratch_shapes=[
             pltpu.VMEM((512, xs[0].shape[1]), jnp.bfloat16),
-            pltpu.VMEM((nw,) + ws[0].shape, jnp.bfloat16),
+            pltpu.VMEM((4 * nw,) + ws[0].shape[1:], jnp.bfloat16),
             pltpu.VMEM((512, ws[0].shape[2]), jnp.float32),
             pltpu.SemaphoreType.DMA((nx,)),
             pltpu.SemaphoreType.DMA((nw,)),
@@ -128,13 +132,16 @@
     own = jnp.concatenate([train_hidden[0], roll_hidden[0]], axis=0)
     w = jnp.concatenate([gate_weight, up_weight], axis=1)
 
-    other = lax.ppermute(w, "zh", shift(2, 1))
-
     block, zls = own, [zl]
     for k in (4, 2):
         got = lax.ppermute(block, "zl", [(i, i ^ k) for i in range(NZL)])
         block, zls = jnp.concatenate([block, got], axis=0), zls + [z ^ k for z in zls]
     twin = lax.ppermute(block, "zl", [(i, i ^ 1) for i in range(NZL)])
+
+    far_w, _ = lax.optimization_barrier((w, got))
+    others = [lax.ppermute(far_w[:128], "zh", shift(2, 1))]
+    far_w, _ = lax.optimization_barrier((far_w, twin))
+    others.append(lax.ppermute(far_w[128:], "zh", shift(2, 1)))
 
     first, second = [1, 0, 3, 2], [3, 2, 1, 0]
     step1 = [(c * NY + i, c * NY + (first, second)[c][i]) for c in range(2) for i in range(NY)]
@@ -154,10 +161,16 @@
         return lax.all_to_all(spread, "x", 0, 0, tiled=True)
 
     ws, cols = [], []
-    for a, h in ((w, zh), (other, 1 - zh)):
-        a = over_x(a)
+    starts = [(i * 4 + zh * 2) * 256 for i in range(NX)]
+    a = over_x(w)
+    ws += [a, lax.ppermute(a, "co", shift(2, 1))]
+    cols += [s + c * 256 for c in (co, 1 - co) for s in starts]
+    starts = [(i * 4 + (1 - zh) * 2) * 256 for i in range(NX)]
+    others[0], _ = lax.optimization_barrier((others[0], got))
+    for half, other in enumerate(others):
+        a = over_x(other)
         ws += [a, lax.ppermute(a, "co", shift(2, 1))]
-        cols += [i * 4 + h * 2 + c for c in (co, 1 - co) for i in range(NX)]
+        cols += [s + c * 256 + half * 128 for c in (co, 1 - co) for s in starts]
 
     parts = mlp(
         jnp.stack(cols).astype(jnp.int32), jnp.stack(slots).astype(jnp.int32), xs, ws, in_project
@@ -173,16 +186,12 @@
     train, roll = pl.pallas_call(norm_kernel, out_shape=(small, small), name="norm")(
         parts, right, live
     )
-    far = lax.ppermute(roll, "zh", shift(2, 1))
+    roll_all = lax.all_to_all(
+        jnp.broadcast_to(roll, (16, 8, 2 * RANK)), ("x", "zh", "co"), 0, 0, tiled=True
+    )
     train_all = lax.all_to_all(
         jnp.broadcast_to(train, (32, 8, 2 * RANK)), ("zl", "y"), 0, 0, tiled=True
     )
-    pair = jnp.where(zh == 0, jnp.stack([roll, far]), jnp.stack([far, roll]))
-    roll_all = lax.all_to_all(
-        jnp.broadcast_to(pair, (8, 2, 8, 2 * RANK)), ("x", "co"), 0, 0, tiled=True
-    )
-    roll_all = roll_all.reshape(NX, NCO, NZH, 8, 2 * RANK).transpose(0, 2, 1, 3, 4)
-    roll_all = roll_all.reshape(16, 8, 2 * RANK)
     return pl.pallas_call(
         score_kernel, out_shape=jax.ShapeDtypeStruct((32, 16), jnp.float32), name="score"
     )(train_all, roll_all)

time: 213 us -> 228 us (1.070)
  waiting for transfers between devices: 81.2 us -> 24.8 us
  starting transfers between devices: 78.2 us -> 116 us
  blocking collectives: 13.1 us -> 44.8 us
  local copies, waits for them, and re-layouts: 18.6 us -> 21.4 us
    all_to_all x1 -> x2, blocking collectives: 13.1 us -> 44.8 us  [the longest x1 28.3 us: on_device(): lax.all_to_all(jnp.broadcast_to(roll, (16, 8, 2 * RANK)), ('x', 'zh', 'co...]
    ppermute x2 -> x3, starting transfers between devices: 6.07 us -> 28.3 us  [on_device(): ws += [a, lax.ppermute(a, 'co', shift(2, 1))]]
    ppermute x2, waiting for transfers between devices: 19.9 us -> 3.42 us  [on_device(): got = lax.ppermute(block, 'zl', [(i, i ^ k) for i in range(NZL)])]
    ppermute x2, waiting for transfers between devices: 14.6 us -> 1.17 us  [on_device(): xs += [both, lax.ppermute(both, ('co', 'y'), step2)]]
    all_to_all x1 -> x0, waiting for transfers between devices: 11.5 us -> none  [on_device(): lax.all_to_all(jnp.broadcast_to(train, (32, 8, 2 * RANK)), ('zl', 'y'), 0...]
    ppermute x1, starting transfers between devices: 1.92 us -> 10.7 us  [on_device(): twin = lax.ppermute(block, 'zl', [(i, i ^ 1) for i in range(NZL)])]
    all_to_all x2 -> x3, waiting for transfers between devices: 10.1 us -> 2.03 us  [over_x(): return lax.all_to_all(spread, 'x', 0, 0, tiled=True)]
    all_to_all x1, starting transfers between devices: 9.28 us -> 15 us  [on_device(): parts = lax.all_to_all(parts, ('zl', 'y'), 0, 0, tiled=True)]
  transfers between devices with their start and end apart: 15 -> 16, of which waited for: 9 -> 6; matrix products, arithmetic and copies ran while one was open for 8% -> 9% of each run, Pallas kernels for 0% -> 0%
where the time goes in v3:
time: 228 us; the launch traced here: 226 us
  starting transfers between devices  116 us (51%)
  blocking collectives  44.8 us (20%)
  waiting for transfers between devices  24.8 us (11%)
  local copies, waits for them, and re-layouts  21.4 us (9%)
  Pallas kernels  15.1 us (7%)
    all_to_all x1, blocking collectives, on_device(): lax.all_to_all(jnp.broadcast_to(roll, (16, 8, 2 * RANK)), ('x', 'zh', 'co...  28.3 us
    ppermute x3, starting transfers between devices, on_device(): ws += [a, lax.ppermute(a, 'co', shift(2, 1))]  28.3 us
    ppermute x1, starting transfers between devices, on_device(): others.append(lax.ppermute(far_w[128:], 'zh', shift(2, 1)))  16.8 us
    all_to_all x1, blocking collectives, on_device(): lax.all_to_all(jnp.broadcast_to(train, (32, 8, 2 * RANK)), ('zl', 'y'), 0...  16.5 us
    all_to_all x1, starting transfers between devices, on_device(): parts = lax.all_to_all(parts, ('zl', 'y'), 0, 0, tiled=True)  15 us
    ppermute x2, starting transfers between devices, on_device(): got = lax.ppermute(block, 'zl', [(i, i ^ k) for i in range(NZL)])  14.8 us
    all_to_all x3, starting transfers between devices, over_x(): return lax.all_to_all(spread, 'x', 0, 0, tiled=True)  12.5 us
    ppermute x2, starting transfers between devices, on_device(): got = lax.ppermute(part, ('co', 'y'), step1)  11.2 us
  transfers between devices with their start and end apart: 16, of which 6 were waited for; matrix products, arithmetic and copies ran while one was open for 9% of the time, Pallas kernels for 0%

profile of v3, /device:TPU:1, one launch (start us, length us, event | category | flops | bytes accessed | tf_op | source)
XLA Modules:
  0.0 226.4 jit_solution(9824974091261175537)
XLA Ops:
  0.0 0.9 pad_maximum_fusion.2
  0.9 9.6 %collective-permute-start = (bf16[16,4096]{1,0:T(8,128)(2,1)S(1)}, bf16[16,4096]{1,0:T(8,128)(2,1)S(1)}, u32[]{:S(2)}, u32[]{:S(2)}) collective-permute-start(bf16[16,4096]{1,0:T(8,128)(2,1)S(1)} %pad_maximum_fusion.2), channel_id=1, source_target_pairs={{0,16},{4,20},{8,24},{12,28},{16,0},{20,4},{24,8},{28,12},{1,17},{... | collective-permute-start | bytes 393224 | tf_op jit(solution)/shard_map/ppermute | solution.py:137
  10.6 1.0 constant_dynamic-update-slice_fusion.8
  11.6 1.0 constant_dynamic-update-slice_fusion.7
  12.5 0.2 copy.11
  12.8 1.4 broadcast_in_dim.22
  14.2 4.1 %all-to-all-start = ((bf16[4,256,896]{2,1,0:T(8,128)(2,1)}), bf16[4,256,896]{2,1,0:T(8,128)(2,1)S(1)}, u32[]{:S(2)}, u32[]{:S(2)}) async-start(bf16[4,256,896]{2,1,0:T(8,128)(2,1)} %broadcast_in_dim.22), calls=%async_computation | async-start | bytes 3670016 | tf_op jit(solution)/shard_map/all_to_all | solution.py:161
  18.3 0.0 collective-permute-done
  18.4 5.1 %collective-permute-start.1 = (bf16[32,4096]{1,0:T(8,128)(2,1)S(1)}, bf16[32,4096]{1,0:T(8,128)(2,1)S(1)}, u32[]{:S(2)}, u32[]{:S(2)}) collective-permute-start(bf16[32,4096]{1,0:T(8,128)(2,1)S(1)} %pad_maximum_fusion.1), channel_id=1, source_target_pairs={{0,8},{4,12},{8,0},{12,4},{16,24},{20,28},{24,16},{28,20},{1,9},{5... | collective-permute-start | bytes 786440 | tf_op jit(solution)/shard_map/ppermute | solution.py:137
  23.5 0.6 constant_dynamic-update-slice_fusion.4
  24.1 3.4 %collective-permute-done.1 = bf16[32,4096]{1,0:T(8,128)(2,1)S(1)} collective-permute-done((bf16[32,4096]{1,0:T(8,128)(2,1)S(1)}, bf16[32,4096]{1,0:T(8,128)(2,1)S(1)}, u32[]{:S(2)}, u32[]{:S(2)}) %collective-permute-start.1) | collective-permute-done | bytes 262176 | tf_op jit(solution)/shard_map/ppermute | solution.py:137
  27.5 0.8 pad_maximum_fusion
  28.4 10.7 %collective-permute-start.4 = (bf16[64,4096]{1,0:T(8,128)(2,1)}, bf16[64,4096]{1,0:T(8,128)(2,1)}, u32[]{:S(2)}, u32[]{:S(2)}) collective-permute-start(bf16[64,4096]{1,0:T(8,128)(2,1)} %pad_maximum_fusion), channel_id=1, source_target_pairs={{0,4},{4,0},{8,12},{12,8},{16,20},{20,16},{24,28},{28,24},{1,5},{5... | collective-permute-start | bytes 1572872 | tf_op jit(solution)/shard_map/ppermute | solution.py:139
  39.0 0.6 constant_dynamic-update-slice_fusion.3
  39.7 6.6 %collective-permute-start.2 = (bf16[64,4096]{1,0:T(8,128)(2,1)}, bf16[64,4096]{1,0:T(8,128)(2,1)}, u32[]{:S(2)}, u32[]{:S(2)}) collective-permute-start(bf16[64,4096]{1,0:T(8,128)(2,1)} %pad_maximum_fusion), channel_id=1, source_target_pairs={{0,1},{1,0},{2,3},{3,2},{32,35},{33,34},{34,33},{35,32},{4,5},{5,4... | collective-permute-start | bytes 1572872 | tf_op jit(solution)/shard_map/ppermute | solution.py:154
  46.2 3.7 %collective-permute-done.4 = bf16[64,4096]{1,0:T(8,128)(2,1)} collective-permute-done((bf16[64,4096]{1,0:T(8,128)(2,1)}, bf16[64,4096]{1,0:T(8,128)(2,1)}, u32[]{:S(2)}, u32[]{:S(2)}) %collective-permute-start.4) | collective-permute-done | bytes 524320 | tf_op jit(solution)/shard_map/ppermute | solution.py:139
  50.0 16.8 %collective-permute-start.10 = (bf16[128,896]{0,1:T(8,128)(2,1)S(1)}, bf16[128,896]{0,1:T(8,128)(2,1)S(1)}, u32[]{:S(2)}, u32[]{:S(2)}) collective-permute-start(bf16[128,896]{0,1:T(8,128)(2,1)S(1)} %slice.7), channel_id=1, source_target_pairs={{0,64},{64,0},{1,65},{65,1},{2,66},{66,2},{3,67},{67,3},{4,68},{68... | collective-permute-start | bytes 688136 | tf_op jit(solution)/shard_map/ppermute | solution.py:144
  66.8 0.7 constant_dynamic-update-slice_fusion.2
  67.5 0.7 slice.6
  68.2 1.9 collective-permute-start.8
  70.1 4.6 %collective-permute-start.5 = (bf16[64,4096]{1,0:T(8,128)(2,1)}, bf16[64,4096]{1,0:T(8,128)(2,1)}, u32[]{:S(2)}, u32[]{:S(2)}) collective-permute-start(bf16[64,4096]{1,0:T(8,128)(2,1)} %collective-permute-done.4), channel_id=1, source_target_pairs={{0,1},{1,0},{2,3},{3,2},{32,35},{33,34},{34,33},{35,32},{4,5},{5,4... | collective-permute-start | bytes 1572872 | tf_op jit(solution)/shard_map/ppermute | solution.py:154
  74.7 0.0 collective-permute-done.10
  74.8 0.2 copy.13
  74.9 0.0 all-to-all-done.refs_4_
  74.9 1.1 broadcast_in_dim.24
  76.0 4.0 %all-to-all-start.2 = ((bf16[4,128,896]{2,1,0:T(8,128)(2,1)}), bf16[4,128,896]{2,1,0:T(8,128)(2,1)S(1)}, u32[]{:S(2)}, u32[]{:S(2)}) async-start(bf16[4,128,896]{2,1,0:T(8,128)(2,1)} %broadcast_in_dim.24), calls=%async_computation.2 | async-start | bytes 1835008 | tf_op jit(solution)/shard_map/all_to_all | solution.py:161
  80.0 0.7 constant_dynamic-update-slice_fusion.1
  80.8 0.0 collective-permute-done.2
  80.8 1.9 constant_dynamic-update-slice_fusion.refs_0_
  82.7 1.9 collective-permute-start.3
  84.6 20.3 %collective-permute-start.7 = (bf16[4,256,896]{2,1,0:T(8,128)(2,1)S(1)}, bf16[4,256,896]{2,1,0:T(8,128)(2,1)}, u32[]{:S(2)}, u32[]{:S(2)}) collective-permute-start(bf16[4,256,896]{2,1,0:T(8,128)(2,1)S(1)} %all-to-all-done.refs_4_), channel_id=1, source_target_pairs={{0,32},{32,0},{1,33},{33,1},{2,34},{34,2},{3,35},{35,3},{4,36},{36... | collective-permute-start | bytes 5505032 | tf_op jit(solution)/shard_map/ppermute | solution.py:166
  104.9 4.6 %collective-permute-done.8 = bf16[128,896]{0,1:T(8,128)(2,1)} collective-permute-done((bf16[128,896]{0,1:T(8,128)(2,1)}, bf16[128,896]{0,1:T(8,128)(2,1)}, u32[]{:S(2)}, u32[]{:S(2)}) %collective-permute-start.8) | collective-permute-done | bytes 229408 | tf_op jit(solution)/shard_map/ppermute | solution.py:142
  109.5 0.0 collective-permute-done.5
  109.5 1.1 copy.12
  110.6 0.0 all-to-all-done.2.refs_8_
  110.6 1.1 broadcast_in_dim.23
  111.7 4.4 %all-to-all-start.1 = ((bf16[4,128,896]{2,1,0:T(8,128)(2,1)}), bf16[4,128,896]{2,1,0:T(8,128)(2,1)}, u32[]{:S(2)}, u32[]{:S(2)}) async-start(bf16[4,128,896]{2,1,0:T(8,128)(2,1)} %broadcast_in_dim.23), calls=%async_computation.1 | async-start | bytes 1835008 | tf_op jit(solution)/shard_map/all_to_all | solution.py:161
  116.1 1.9 constant_dynamic-update-slice_fusion.6
  118.0 1.9 constant_dynamic-update-slice_fusion.5.refs_2_
  119.8 2.8 %collective-permute-start.6 = (bf16[128,4096]{1,0:T(8,128)(2,1)}, bf16[128,4096]{1,0:T(8,128)(2,1)}, u32[]{:S(2)}, u32[]{:S(2)}) collective-permute-start(bf16[128,4096]{1,0:T(8,128)(2,1)} %constant_dynamic-update-slice_fusion.5.refs_2_), channel_id=1, source_target_pairs={{0,3},{1,2},{2,1},{3,0},{32,33},{33,32},{34,35},{35,34},{4,7},{5,6... | collective-permute-start | bytes 3145736 | tf_op jit(solution)/shard_map/ppermute | solution.py:156
  122.7 4.6 %collective-permute-start.11 = (bf16[4,128,896]{2,1,0:T(8,128)(2,1)S(1)}, bf16[4,128,896]{2,1,0:T(8,128)(2,1)}, u32[]{:S(2)}, u32[]{:S(2)}) collective-permute-start(bf16[4,128,896]{2,1,0:T(8,128)(2,1)S(1)} %all-to-all-done.2.refs_8_), channel_id=1, source_target_pairs={{0,32},{32,0},{1,33},{33,1},{2,34},{34,2},{3,35},{35,3},{4,36},{36... | collective-permute-start | bytes 2752520 | tf_op jit(solution)/shard_map/ppermute | solution.py:172
  127.3 2.0 all-to-all-done.1.refs_6_
  129.3 3.4 %collective-permute-start.9 = (bf16[4,128,896]{2,1,0:T(8,128)(2,1)}, bf16[4,128,896]{2,1,0:T(8,128)(2,1)}, u32[]{:S(2)}, u32[]{:S(2)}) collective-permute-start(bf16[4,128,896]{2,1,0:T(8,128)(2,1)} %all-to-all-done.1.refs_6_), channel_id=1, source_target_pairs={{0,32},{32,0},{1,33},{33,1},{2,34},{34,2},{3,35},{35,3},{4,36},{36... | collective-permute-start | bytes 2752520 | tf_op jit(solution)/shard_map/ppermute | solution.py:172
  132.8 0.8 copy.14.refs_10_
  133.5 0.6 stack.209.cols_ref
  134.2 0.6 stack.242.slot_ref
  134.8 0.0 collective-permute-done.3.refs_1_
  134.8 1.2 collective-permute-done.6.refs_3_
  136.0 0.0 collective-permute-done.11.refs_9_
  136.0 0.0 collective-permute-done.9.refs_7_
  136.0 10.8 %mlp.1 = f32[32,8,128]{2,1,0:T(8,128)} custom-call(s32[24]{0:T(128)} %stack.209.cols_ref, s32[32]{0:T(128)} %stack.242.slot_ref, bf16[128,4096]{1,0:T(8,128)(2,1)} %constant_dynamic-update-slice_fusion.refs_0_, bf16[128,4096]{1,0:T(8,128)(2,1)} %collective-permute-done.3.refs_1_, bf16[128,4096]{1,0:T(8,128)(2,1)} %constant_dynamic-update-slice_fusion.5.refs_2_, ...), custom_call_target="tpu_custom_call" | custom-call | tf_op jit(solution)/shard_map/mlp/pallas_call | solution.py:66
  146.9 15.0 %all-to-all-start.3 = ((f32[32,8,128]{2,1,0:T(8,128)}), f32[32,8,128]{2,1,0:T(8,128)S(1)}, u32[]{:S(2)}, u32[]{:S(2)}) async-start(f32[32,8,128]{2,1,0:T(8,128)} %mlp.1), calls=%async_computation.3 | async-start | bytes 262144 | tf_op jit(solution)/shard_map/all_to_all | solution.py:184
  163.2 0.1 add_bitcast_fusion
  163.3 0.9 convolution_bitcast_fusion.right_ref
  164.1 0.1 compare_convert_fusion
  164.2 9.8 %all-to-all-done.3.parts_ref = f32[32,8,128]{2,1,0:T(8,128)S(1)} async-done(((f32[32,8,128]{2,1,0:T(8,128)}), f32[32,8,128]{2,1,0:T(8,128)S(1)}, u32[]{:S(2)}, u32[]{:S(2)}) %all-to-all-start.3) | async-done | bytes 131104 | tf_op jit(solution)/shard_map/all_to_all | solution.py:184
  174.0 0.7 broadcast_in_dim.25.live_ref
  174.7 2.1 norm.1
  176.8 0.7 broadcast_in_dim.27
  177.5 28.3 %all_to_all.30.roll_ref = f32[16,8,128]{2,1,0:T(8,128)} all-to-all(f32[16,8,128]{2,1,0:T(8,128)S(1)} %broadcast_in_dim.27), channel_id=1, replica_groups=mesh['x'=4,'zh'=2,'co'=2,'zl'=8,'y'=4] {'x','zh','co'}, dimensions={0} | all-to-all | bytes 131072 | tf_op jit(solution)/shard_map/all_to_all | solution.py:189
  205.8 0.7 broadcast_in_dim.26
  206.5 16.5 %all_to_all.31.train_ref = f32[32,8,128]{2,1,0:T(8,128)} all-to-all(f32[32,8,128]{2,1,0:T(8,128)S(1)} %broadcast_in_dim.26), channel_id=1, replica_groups=mesh['x'=4,'zh'=2,'co'=2,'zl'=8,'y'=4] {'zl','y'}, dimensions={0} | all-to-all | bytes 262144 | tf_op jit(solution)/shard_map/all_to_all | solution.py:192
  222.9 2.1 score.1
  225.1 1.4 copy.15
  (21 shorter events, 0.1 us)
Async XLA Ops:
  0.0 163.3 %copy-start = (bf16[4096,64]{0,1:T(8,128)(2,1)S(1)}, bf16[4096,64]{0,1:T(8,128)(2,1)}, u32[]{:S(2)}) copy-start(bf16[4096,64]{0,1:T(8,128)(2,1)} %param.19) | copy-start | bytes 1572868
  0.9 17.4 %collective-permute-start = (bf16[16,4096]{1,0:T(8,128)(2,1)S(1)}, bf16[16,4096]{1,0:T(8,128)(2,1)S(1)}, u32[]{:S(2)}, u32[]{:S(2)}) collective-permute-start(bf16[16,4096]{1,0:T(8,128)(2,1)S(1)} %pad_maximum_fusion.2), channel_id=1, source_target_pairs={{0,16},{4,20},{8,24},{12,28},{16,0},{20,4},{24,8},{28,12},{1,17},{... | collective-permute-start | bytes 393224 | tf_op jit(solution)/shard_map/ppermute | solution.py:137
  14.2 4.2 %copy-start.3 = (bf16[1,8,4096]{2,1,0:T(8,128)(2,1)S(1)}, bf16[1,8,4096]{2,1,0:T(8,128)(2,1)}, u32[]{:S(2)}) copy-start(bf16[1,8,4096]{2,1,0:T(8,128)(2,1)} %param.10) | copy-start | bytes 196612
  14.2 4.2 %copy-start.4 = (bf16[1,8,4096]{2,1,0:T(8,128)(2,1)S(1)}, bf16[1,8,4096]{2,1,0:T(8,128)(2,1)}, u32[]{:S(2)}) copy-start(bf16[1,8,4096]{2,1,0:T(8,128)(2,1)} %param.13) | copy-start | bytes 196612
  14.2 60.8 %all-to-all-start = ((bf16[4,256,896]{2,1,0:T(8,128)(2,1)}), bf16[4,256,896]{2,1,0:T(8,128)(2,1)S(1)}, u32[]{:S(2)}, u32[]{:S(2)}) async-start(bf16[4,256,896]{2,1,0:T(8,128)(2,1)} %broadcast_in_dim.22), calls=%async_computation | async-start | bytes 3670016 | tf_op jit(solution)/shard_map/all_to_all | solution.py:161
  18.4 9.2 %collective-permute-start.1 = (bf16[32,4096]{1,0:T(8,128)(2,1)S(1)}, bf16[32,4096]{1,0:T(8,128)(2,1)S(1)}, u32[]{:S(2)}, u32[]{:S(2)}) collective-permute-start(bf16[32,4096]{1,0:T(8,128)(2,1)S(1)} %pad_maximum_fusion.1), channel_id=1, source_target_pairs={{0,8},{4,12},{8,0},{12,4},{16,24},{20,28},{24,16},{28,20},{1,9},{5... | collective-permute-start | bytes 786440 | tf_op jit(solution)/shard_map/ppermute | solution.py:137
  28.4 21.6 %collective-permute-start.4 = (bf16[64,4096]{1,0:T(8,128)(2,1)}, bf16[64,4096]{1,0:T(8,128)(2,1)}, u32[]{:S(2)}, u32[]{:S(2)}) collective-permute-start(bf16[64,4096]{1,0:T(8,128)(2,1)} %pad_maximum_fusion), channel_id=1, source_target_pairs={{0,4},{4,0},{8,12},{12,8},{16,20},{20,16},{24,28},{28,24},{1,5},{5... | collective-permute-start | bytes 1572872 | tf_op jit(solution)/shard_map/ppermute | solution.py:139
  39.7 41.1 %collective-permute-start.2 = (bf16[64,4096]{1,0:T(8,128)(2,1)}, bf16[64,4096]{1,0:T(8,128)(2,1)}, u32[]{:S(2)}, u32[]{:S(2)}) collective-permute-start(bf16[64,4096]{1,0:T(8,128)(2,1)} %pad_maximum_fusion), channel_id=1, source_target_pairs={{0,1},{1,0},{2,3},{3,2},{32,35},{33,34},{34,33},{35,32},{4,5},{5,4... | collective-permute-start | bytes 1572872 | tf_op jit(solution)/shard_map/ppermute | solution.py:154
  50.0 24.8 %collective-permute-start.10 = (bf16[128,896]{0,1:T(8,128)(2,1)S(1)}, bf16[128,896]{0,1:T(8,128)(2,1)S(1)}, u32[]{:S(2)}, u32[]{:S(2)}) collective-permute-start(bf16[128,896]{0,1:T(8,128)(2,1)S(1)} %slice.7), channel_id=1, source_target_pairs={{0,64},{64,0},{1,65},{65,1},{2,66},{66,2},{3,67},{67,3},{4,68},{68... | collective-permute-start | bytes 688136 | tf_op jit(solution)/shard_map/ppermute | solution.py:144
  68.2 41.3 %collective-permute-start.8 = (bf16[128,896]{0,1:T(8,128)(2,1)}, bf16[128,896]{0,1:T(8,128)(2,1)}, u32[]{:S(2)}, u32[]{:S(2)}) collective-permute-start(bf16[128,896]{0,1:T(8,128)(2,1)} %slice.6), channel_id=1, source_target_pairs={{0,64},{64,0},{1,65},{65,1},{2,66},{66,2},{3,67},{67,3},{4,68},{68... | collective-permute-start | bytes 688136 | tf_op jit(solution)/shard_map/ppermute | solution.py:142
  70.1 39.4 %collective-permute-start.5 = (bf16[64,4096]{1,0:T(8,128)(2,1)}, bf16[64,4096]{1,0:T(8,128)(2,1)}, u32[]{:S(2)}, u32[]{:S(2)}) collective-permute-start(bf16[64,4096]{1,0:T(8,128)(2,1)} %collective-permute-done.4), channel_id=1, source_target_pairs={{0,1},{1,0},{2,3},{3,2},{32,35},{33,34},{34,33},{35,32},{4,5},{5,4... | collective-permute-start | bytes 1572872 | tf_op jit(solution)/shard_map/ppermute | solution.py:154
  74.9 9.6 %copy-start.1 = (bf16[4,256,896]{2,1,0:T(8,128)(2,1)}, bf16[4,256,896]{2,1,0:T(8,128)(2,1)S(1)}, u32[]{:S(2)}) copy-start(bf16[4,256,896]{2,1,0:T(8,128)(2,1)S(1)} %all-to-all-done.refs_4_) | copy-start | bytes 5505028
  76.0 34.6 %all-to-all-start.2 = ((bf16[4,128,896]{2,1,0:T(8,128)(2,1)}), bf16[4,128,896]{2,1,0:T(8,128)(2,1)S(1)}, u32[]{:S(2)}, u32[]{:S(2)}) async-start(bf16[4,128,896]{2,1,0:T(8,128)(2,1)} %broadcast_in_dim.24), calls=%async_computation.2 | async-start | bytes 1835008 | tf_op jit(solution)/shard_map/all_to_all | solution.py:161
  82.7 52.2 %collective-permute-start.3 = (bf16[128,4096]{1,0:T(8,128)(2,1)}, bf16[128,4096]{1,0:T(8,128)(2,1)}, u32[]{:S(2)}, u32[]{:S(2)}) collective-permute-start(bf16[128,4096]{1,0:T(8,128)(2,1)} %constant_dynamic-update-slice_fusion.refs_0_), channel_id=1, source_target_pairs={{0,3},{1,2},{2,1},{3,0},{32,33},{33,32},{34,35},{35,34},{4,7},{5,6... | collective-permute-start | bytes 3145736 | tf_op jit(solution)/shard_map/ppermute | solution.py:156
  84.6 51.4 %collective-permute-start.7 = (bf16[4,256,896]{2,1,0:T(8,128)(2,1)S(1)}, bf16[4,256,896]{2,1,0:T(8,128)(2,1)}, u32[]{:S(2)}, u32[]{:S(2)}) collective-permute-start(bf16[4,256,896]{2,1,0:T(8,128)(2,1)S(1)} %all-to-all-done.refs_4_), channel_id=1, source_target_pairs={{0,32},{32,0},{1,33},{33,1},{2,34},{34,2},{3,35},{35,3},{4,36},{36... | collective-permute-start | bytes 5505032 | tf_op jit(solution)/shard_map/ppermute | solution.py:166
  110.6 12.1 %copy-start.2 = (bf16[4,128,896]{2,1,0:T(8,128)(2,1)}, bf16[4,128,896]{2,1,0:T(8,128)(2,1)S(1)}, u32[]{:S(2)}) copy-start(bf16[4,128,896]{2,1,0:T(8,128)(2,1)S(1)} %all-to-all-done.2.refs_8_) | copy-start | bytes 2752516
  111.7 21.1 %copy-start.6 = (bf16[448,64]{0,1:T(8,128)(2,1)S(1)}, bf16[448,64]{0,1:T(8,128)(2,1)}, u32[]{:S(2)}) copy-start(bf16[448,64]{0,1:T(8,128)(2,1)} %param.18) | copy-start | bytes 172036
  111.7 17.6 %all-to-all-start.1 = ((bf16[4,128,896]{2,1,0:T(8,128)(2,1)}), bf16[4,128,896]{2,1,0:T(8,128)(2,1)}, u32[]{:S(2)}, u32[]{:S(2)}) async-start(bf16[4,128,896]{2,1,0:T(8,128)(2,1)} %broadcast_in_dim.23), calls=%async_computation.1 | async-start | bytes 1835008 | tf_op jit(solution)/shard_map/all_to_all | solution.py:161
  119.8 16.1 %collective-permute-start.6 = (bf16[128,4096]{1,0:T(8,128)(2,1)}, bf16[128,4096]{1,0:T(8,128)(2,1)}, u32[]{:S(2)}, u32[]{:S(2)}) collective-permute-start(bf16[128,4096]{1,0:T(8,128)(2,1)} %constant_dynamic-update-slice_fusion.5.refs_2_), channel_id=1, source_target_pairs={{0,3},{1,2},{2,1},{3,0},{32,33},{33,32},{34,35},{35,34},{4,7},{5,6... | collective-permute-start | bytes 3145736 | tf_op jit(solution)/shard_map/ppermute | solution.py:156
  122.7 13.3 %collective-permute-start.11 = (bf16[4,128,896]{2,1,0:T(8,128)(2,1)S(1)}, bf16[4,128,896]{2,1,0:T(8,128)(2,1)}, u32[]{:S(2)}, u32[]{:S(2)}) collective-permute-start(bf16[4,128,896]{2,1,0:T(8,128)(2,1)S(1)} %all-to-all-done.2.refs_8_), channel_id=1, source_target_pairs={{0,32},{32,0},{1,33},{33,1},{2,34},{34,2},{3,35},{35,3},{4,36},{36... | collective-permute-start | bytes 2752520 | tf_op jit(solution)/shard_map/ppermute | solution.py:172
  129.3 6.7 %collective-permute-start.9 = (bf16[4,128,896]{2,1,0:T(8,128)(2,1)}, bf16[4,128,896]{2,1,0:T(8,128)(2,1)}, u32[]{:S(2)}, u32[]{:S(2)}) collective-permute-start(bf16[4,128,896]{2,1,0:T(8,128)(2,1)} %all-to-all-done.1.refs_6_), channel_id=1, source_target_pairs={{0,32},{32,0},{1,33},{33,1},{2,34},{34,2},{3,35},{35,3},{4,36},{36... | collective-permute-start | bytes 2752520 | tf_op jit(solution)/shard_map/ppermute | solution.py:172
  134.8 28.5 %copy-start.7 = (bf16[1,8,4096]{2,1,0:T(8,128)(2,1)S(1)}, bf16[1,8,4096]{2,1,0:T(8,128)(2,1)}, u32[]{:S(2)}) copy-start(bf16[1,8,4096]{2,1,0:T(8,128)(2,1)} %param.14) | copy-start | bytes 196612
  134.8 28.5 %copy-start.8 = (bf16[1,8,4096]{2,1,0:T(8,128)(2,1)S(1)}, bf16[1,8,4096]{2,1,0:T(8,128)(2,1)}, u32[]{:S(2)}) copy-start(bf16[1,8,4096]{2,1,0:T(8,128)(2,1)} %param.11) | copy-start | bytes 196612
  146.9 27.2 %all-to-all-start.3 = ((f32[32,8,128]{2,1,0:T(8,128)}), f32[32,8,128]{2,1,0:T(8,128)S(1)}, u32[]{:S(2)}, u32[]{:S(2)}) async-start(f32[32,8,128]{2,1,0:T(8,128)} %mlp.1), calls=%async_computation.3 | async-start | bytes 262144 | tf_op jit(solution)/shard_map/all_to_all | solution.py:184
  174.0 0.7 copy-start.5

commit v4 on v3

--- a/solution.py
+++ b/solution.py
@@ -52,7 +52,9 @@
         rows = acc[m * 128 : (m + 1) * 128, :]
         gate, up = rows[:, :half], rows[:, half:]
         act = (gate / (1.0 + jnp.exp(-gate)) * up).astype(jnp.bfloat16)
-        left = jnp.dot(act, ip_ref[...], preferred_element_type=jnp.float32)
+        left = lax.dot_general(
+            act, ip_ref[...], (((1,), (1,)), ((), ())), preferred_element_type=jnp.float32
+        )
         left = left.reshape(8, 2, 8, RANK)
         left = jnp.concatenate([left[:, 0], left[:, 1]], axis=-1)
         for i in range(8):
@@ -80,10 +82,11 @@
     )(cols, slots, *xs, *ws, ip)
 
 
-def norm_kernel(parts_ref, right_ref, live_ref, train_ref, roll_ref):
+def norm_kernel(parts_ref, right_ref, train_len_ref, roll_len_ref, train_ref, roll_ref):
     left = jnp.sum(parts_ref[...], axis=0)
-    for s, ref in ((0, train_ref), (1, roll_ref)):
-        one = left[:, s * RANK : (s + 1) * RANK] * live_ref[s]
+    token = lax.broadcasted_iota(jnp.int32, (8, RANK), 0)
+    for s, (len_ref, ref) in enumerate(((train_len_ref, train_ref), (roll_len_ref, roll_ref))):
+        one = jnp.where(token < len_ref[0], left[:, s * RANK : (s + 1) * RANK], 0.0)
         right = right_ref[s]
         grad = lax.dot_general(
             one, right, (((0,), (0,)), ((), ())), precision=HIGH, preferred_element_type=jnp.float32
@@ -98,15 +101,15 @@
     r = roll_ref[...].reshape(-1, 2 * RANK)
     dims = (((1,), (1,)), ((), ()))
     a = lax.dot_general(
-        t[:, :RANK], r[:, :RANK], dims, precision=HIGH, preferred_element_type=jnp.float32
+        r[:, :RANK], t[:, :RANK], dims, precision=HIGH, preferred_element_type=jnp.float32
     )
     b = lax.dot_general(
-        t[:, RANK:], r[:, RANK:], dims, precision=HIGH, preferred_element_type=jnp.float32
-    )
-    both = jnp.sum((a * b).reshape(32, 8, 128), axis=1)
+        r[:, RANK:], t[:, RANK:], dims, precision=HIGH, preferred_element_type=jnp.float32
+    )
+    both = jnp.sum((a * b).reshape(16, 8, 256), axis=1)
     pick = (
-        lax.broadcasted_iota(jnp.int32, (128, 16), 0) // 8
-        == lax.broadcasted_iota(jnp.int32, (128, 16), 1)
+        lax.broadcasted_iota(jnp.int32, (256, 32), 0) // 8
+        == lax.broadcasted_iota(jnp.int32, (256, 32), 1)
     ).astype(jnp.float32)
     out_ref[...] = jnp.dot(both, pick, precision=HIGH, preferred_element_type=jnp.float32) / RANK
 
@@ -135,13 +138,11 @@
     block, zls = own, [zl]
     for k in (4, 2):
         got = lax.ppermute(block, "zl", [(i, i ^ k) for i in range(NZL)])
+        if k == 4:
+            far_w, _ = lax.optimization_barrier((w, got))
+            other = lax.ppermute(far_w, "zh", shift(2, 1))
         block, zls = jnp.concatenate([block, got], axis=0), zls + [z ^ k for z in zls]
     twin = lax.ppermute(block, "zl", [(i, i ^ 1) for i in range(NZL)])
-
-    far_w, _ = lax.optimization_barrier((w, got))
-    others = [lax.ppermute(far_w[:128], "zh", shift(2, 1))]
-    far_w, _ = lax.optimization_barrier((far_w, twin))
-    others.append(lax.ppermute(far_w[128:], "zh", shift(2, 1)))
 
     first, second = [1, 0, 3, 2], [3, 2, 1, 0]
     step1 = [(c * NY + i, c * NY + (first, second)[c][i]) for c in range(2) for i in range(NY)]
@@ -161,40 +162,33 @@
         return lax.all_to_all(spread, "x", 0, 0, tiled=True)
 
     ws, cols = [], []
-    starts = [(i * 4 + zh * 2) * 256 for i in range(NX)]
-    a = over_x(w)
-    ws += [a, lax.ppermute(a, "co", shift(2, 1))]
-    cols += [s + c * 256 for c in (co, 1 - co) for s in starts]
-    starts = [(i * 4 + (1 - zh) * 2) * 256 for i in range(NX)]
-    others[0], _ = lax.optimization_barrier((others[0], got))
-    for half, other in enumerate(others):
-        a = over_x(other)
+    other, _ = lax.optimization_barrier((other, got))
+    for a, h in ((w, zh), (other, 1 - zh)):
+        a = over_x(a)
         ws += [a, lax.ppermute(a, "co", shift(2, 1))]
-        cols += [s + c * 256 + half * 128 for c in (co, 1 - co) for s in starts]
+        cols += [(i * 4 + h * 2 + c) * 256 for c in (co, 1 - co) for i in range(NX)]
 
     parts = mlp(
-        jnp.stack(cols).astype(jnp.int32), jnp.stack(slots).astype(jnp.int32), xs, ws, in_project
+        jnp.stack(cols).astype(jnp.int32), jnp.stack(slots).astype(jnp.int32), xs, ws, in_project.T
     )
     cot = jnp.concatenate([train_cotangent[0], roll_cotangent[0]], axis=0)
     right = jnp.dot(cot, out_project, preferred_element_type=jnp.float32).reshape(2, 8, RANK)
-    lengths = jnp.stack([train_lengths, roll_lengths])
-    live = (jnp.arange(8, dtype=jnp.int32)[None, :] < lengths).astype(jnp.float32)[:, :, None]
-    live = jnp.broadcast_to(live, (2, 8, RANK))
-
     parts = lax.all_to_all(parts, ("zl", "y"), 0, 0, tiled=True)
     small = jax.ShapeDtypeStruct((8, 2 * RANK), jnp.float32)
-    train, roll = pl.pallas_call(norm_kernel, out_shape=(small, small), name="norm")(
-        parts, right, live
-    )
+    vmem, smem = pl.BlockSpec(memory_space=pltpu.VMEM), pl.BlockSpec(memory_space=pltpu.SMEM)
+    train, roll = pl.pallas_call(
+        norm_kernel, out_shape=(small, small), in_specs=[vmem, vmem, smem, smem], name="norm"
+    )(parts, right, train_lengths, roll_lengths)
     roll_all = lax.all_to_all(
         jnp.broadcast_to(roll, (16, 8, 2 * RANK)), ("x", "zh", "co"), 0, 0, tiled=True
     )
     train_all = lax.all_to_all(
         jnp.broadcast_to(train, (32, 8, 2 * RANK)), ("zl", "y"), 0, 0, tiled=True
     )
-    return pl.pallas_call(
-        score_kernel, out_shape=jax.ShapeDtypeStruct((32, 16), jnp.float32), name="score"
+    scores = pl.pallas_call(
+        score_kernel, out_shape=jax.ShapeDtypeStruct((16, 32), jnp.float32), name="score"
     )(train_all, roll_all)
+    return scores.T
 
 
 def solution(mesh):

time: 228 us -> 239 us (1.048)
  waiting for transfers between devices: 24.8 us -> 64.4 us
  starting transfers between devices: 116 us -> 93.7 us
  local copies, waits for them, and re-layouts: 21.4 us -> 15.1 us
    ppermute x2 -> x1, waiting for transfers between devices: 4.59 us -> 31.3 us  [on_device(): other = lax.ppermute(far_w, 'zh', shift(2, 1))]
    ppermute x3 -> x2, starting transfers between devices: 28.3 us -> 10.5 us  [on_device(): ws += [a, lax.ppermute(a, 'co', shift(2, 1))]]
    ppermute x2, waiting for transfers between devices: 1.17 us -> 11.4 us  [on_device(): xs += [both, lax.ppermute(both, ('co', 'y'), step2)]]
    ppermute x2 -> x1, starting transfers between devices: 18.7 us -> 12.5 us  [on_device(): other = lax.ppermute(far_w, 'zh', shift(2, 1))]
    ppermute x2, waiting for transfers between devices: 0.01 us -> 5.77 us  [on_device(): got = lax.ppermute(part, ('co', 'y'), step1)]
    ppermute x2, starting transfers between devices: 14.8 us -> 20.1 us  [on_device(): got = lax.ppermute(block, 'zl', [(i, i ^ k) for i in range(NZL)])]
    ppermute x1, waiting for transfers between devices: 3.73 us -> 0.01 us  [on_device(): twin = lax.ppermute(block, 'zl', [(i, i ^ 1) for i in range(NZL)])]
    all_to_all x3 -> x2, starting transfers between devices: 12.5 us -> 10.6 us  [over_x(): return lax.all_to_all(spread, 'x', 0, 0, tiled=True)]
  transfers between devices with their start and end apart: 16 -> 13, of which waited for: 6 -> 7; matrix products, arithmetic and copies ran while one was open for 9% -> 5% of each run, Pallas kernels for 0% -> 0%
where the time goes in v4:
time: 239 us; the launch traced here: 237 us
  starting transfers between devices  93.7 us (39%)
  waiting for transfers between devices  64.4 us (27%)
  blocking collectives  43 us (18%)
  local copies, waits for them, and re-layouts  15.1 us (6%)
  Pallas kernels  14.6 us (6%)
  other arithmetic  3.54 us (1%)
    ppermute x1, waiting for transfers between devices, on_device(): other = lax.ppermute(far_w, 'zh', shift(2, 1))  31.3 us
    all_to_all x1, blocking collectives, on_device(): lax.all_to_all(jnp.broadcast_to(roll, (16, 8, 2 * RANK)), ('x', 'zh', 'co...  26.5 us
    ppermute x2, starting transfers between devices, on_device(): got = lax.ppermute(block, 'zl', [(i, i ^ k) for i in range(NZL)])  20.1 us
    all_to_all x1, blocking collectives, on_device(): lax.all_to_all(jnp.broadcast_to(train, (32, 8, 2 * RANK)), ('zl', 'y'), 0...  16.6 us
    all_to_all x1, starting transfers between devices, on_device(): parts = lax.all_to_all(parts, ('zl', 'y'), 0, 0, tiled=True)  14.7 us
    ppermute x1, starting transfers between devices, on_device(): other = lax.ppermute(far_w, 'zh', shift(2, 1))  12.5 us
    ppermute x2, waiting for transfers between devices, on_device(): xs += [both, lax.ppermute(both, ('co', 'y'), step2)]  11.4 us
    ppermute x1, starting transfers between devices, on_device(): twin = lax.ppermute(block, 'zl', [(i, i ^ 1) for i in range(NZL)])  10.8 us
  transfers between devices with their start and end apart: 13, of which 7 were waited for; matrix products, arithmetic and copies ran while one was open for 5% of the time, Pallas kernels for 0%

profile of v4, /device:TPU:1, one launch (start us, length us, event | category | flops | bytes accessed | tf_op | source)
XLA Modules:
  0.0 236.9 jit_solution(12546603742643951865)
XLA Ops:
  0.0 0.0 copy-start
  0.0 1.0 pad_maximum_fusion.2
  1.0 9.6 %collective-permute-start = (bf16[16,4096]{1,0:T(8,128)(2,1)S(1)}, bf16[16,4096]{1,0:T(8,128)(2,1)S(1)}, u32[]{:S(2)}, u32[]{:S(2)}) collective-permute-start(bf16[16,4096]{1,0:T(8,128)(2,1)S(1)} %pad_maximum_fusion.2), channel_id=1, source_target_pairs={{0,16},{4,20},{8,24},{12,28},{16,0},{20,4},{24,8},{28,12},{1,17},{... | collective-permute-start | bytes 393224 | tf_op jit(solution)/shard_map/ppermute | solution.py:140
  10.6 2.4 collective-permute-done
  13.0 0.9 pad_maximum_fusion.1
  13.9 10.5 %collective-permute-start.1 = (bf16[32,4096]{1,0:T(8,128)(2,1)S(1)}, bf16[32,4096]{1,0:T(8,128)(2,1)S(1)}, u32[]{:S(2)}, u32[]{:S(2)}) collective-permute-start(bf16[32,4096]{1,0:T(8,128)(2,1)S(1)} %pad_maximum_fusion.1), channel_id=1, source_target_pairs={{0,8},{4,12},{8,0},{12,4},{16,24},{20,28},{24,16},{28,20},{1,9},{5... | collective-permute-start | bytes 786440 | tf_op jit(solution)/shard_map/ppermute | solution.py:140
  24.4 1.0 constant_dynamic-update-slice_fusion.8
  25.3 3.0 %collective-permute-done.1 = bf16[32,4096]{1,0:T(8,128)(2,1)S(1)} collective-permute-done((bf16[32,4096]{1,0:T(8,128)(2,1)S(1)}, bf16[32,4096]{1,0:T(8,128)(2,1)S(1)}, u32[]{:S(2)}, u32[]{:S(2)}) %collective-permute-start.1) | collective-permute-done | bytes 262176 | tf_op jit(solution)/shard_map/ppermute | solution.py:140
  28.3 1.7 pad_maximum_fusion
  30.0 10.8 %collective-permute-start.4 = (bf16[64,4096]{1,0:T(8,128)(2,1)}, bf16[64,4096]{1,0:T(8,128)(2,1)}, u32[]{:S(2)}, u32[]{:S(2)}) collective-permute-start(bf16[64,4096]{1,0:T(8,128)(2,1)} %pad_maximum_fusion), channel_id=1, source_target_pairs={{0,4},{4,0},{8,12},{12,8},{16,20},{20,16},{24,28},{28,24},{1,5},{5... | collective-permute-start | bytes 1572872 | tf_op jit(solution)/shard_map/ppermute | solution.py:145
  40.8 0.0 copy-done.8
  40.8 0.0 copy-start.5
  40.8 0.2 copy.11
  41.1 1.4 broadcast_in_dim.12
  42.5 0.0 copy-done.5
  42.5 6.1 %all-to-all-start = ((bf16[4,256,896]{2,1,0:T(8,128)(2,1)}), bf16[4,256,896]{2,1,0:T(8,128)(2,1)S(1)}, u32[]{:S(2)}, u32[]{:S(2)}) async-start(bf16[4,256,896]{2,1,0:T(8,128)(2,1)} %broadcast_in_dim.12), calls=%async_computation | async-start | bytes 3670016 | tf_op jit(solution)/shard_map/all_to_all | solution.py:162
  48.6 12.5 %collective-permute-start.8 = (bf16[256,896]{0,1:T(8,128)(2,1)}, bf16[256,896]{0,1:T(8,128)(2,1)S(1)}, u32[]{:S(2)}, u32[]{:S(2)}) collective-permute-start(bf16[256,896]{0,1:T(8,128)(2,1)} %copy-done.5), channel_id=1, source_target_pairs={{0,64},{64,0},{1,65},{65,1},{2,66},{66,2},{3,67},{67,3},{4,68},{68... | collective-permute-start | bytes 1376264 | tf_op jit(solution)/shard_map/ppermute | solution.py:143
  61.1 0.0 collective-permute-done.4
  61.1 4.6 %collective-permute-start.5 = (bf16[64,4096]{1,0:T(8,128)(2,1)}, bf16[64,4096]{1,0:T(8,128)(2,1)}, u32[]{:S(2)}, u32[]{:S(2)}) collective-permute-start(bf16[64,4096]{1,0:T(8,128)(2,1)} %collective-permute-done.4), channel_id=1, source_target_pairs={{0,1},{1,0},{2,3},{3,2},{32,35},{33,34},{34,33},{35,32},{4,5},{5,4... | collective-permute-start | bytes 1572872 | tf_op jit(solution)/shard_map/ppermute | solution.py:155
  65.8 0.6 constant_dynamic-update-slice_fusion.4
  66.4 31.3 %collective-permute-done.8 = bf16[256,896]{0,1:T(8,128)(2,1)S(1)} collective-permute-done((bf16[256,896]{0,1:T(8,128)(2,1)}, bf16[256,896]{0,1:T(8,128)(2,1)S(1)}, u32[]{:S(2)}, u32[]{:S(2)}) %collective-permute-start.8) | collective-permute-done | bytes 458784 | tf_op jit(solution)/shard_map/ppermute | solution.py:143
  97.7 0.8 copy-done.7
  98.5 0.0 collective-permute-done.5
  98.5 1.3 copy.12
  99.8 0.0 all-to-all-done.refs_4_
  99.8 1.5 broadcast_in_dim.13
  101.3 4.5 %all-to-all-start.1 = ((bf16[4,256,896]{2,1,0:T(8,128)(2,1)}), bf16[4,256,896]{2,1,0:T(8,128)(2,1)}, u32[]{:S(2)}, u32[]{:S(2)}) async-start(bf16[4,256,896]{2,1,0:T(8,128)(2,1)} %broadcast_in_dim.13), calls=%async_computation.1 | async-start | bytes 3670016 | tf_op jit(solution)/shard_map/all_to_all | solution.py:162
  105.8 0.0 copy-done.4
  105.8 0.6 constant_dynamic-update-slice_fusion.3
  106.5 4.6 %collective-permute-start.2 = (bf16[64,4096]{1,0:T(8,128)(2,1)}, bf16[64,4096]{1,0:T(8,128)(2,1)S(1)}, u32[]{:S(2)}, u32[]{:S(2)}) collective-permute-start(bf16[64,4096]{1,0:T(8,128)(2,1)} %pad_maximum_fusion), channel_id=1, source_target_pairs={{0,1},{1,0},{2,3},{3,2},{32,35},{33,34},{34,33},{35,32},{4,5},{5,4... | collective-permute-start | bytes 1572872 | tf_op jit(solution)/shard_map/ppermute | solution.py:155
  111.1 0.7 constant_dynamic-update-slice_fusion.2
  111.8 0.7 constant_dynamic-update-slice_fusion.1
  112.5 5.8 %collective-permute-done.2 = bf16[64,4096]{1,0:T(8,128)(2,1)S(1)} collective-permute-done((bf16[64,4096]{1,0:T(8,128)(2,1)}, bf16[64,4096]{1,0:T(8,128)(2,1)S(1)}, u32[]{:S(2)}, u32[]{:S(2)}) %collective-permute-start.2) | collective-permute-done | bytes 524320 | tf_op jit(solution)/shard_map/ppermute | solution.py:155
  118.3 0.8 constant_dynamic-update-slice_fusion.refs_0_
  119.1 1.9 collective-permute-start.3
  121.0 6.0 %collective-permute-start.7 = (bf16[4,256,896]{2,1,0:T(8,128)(2,1)S(1)}, bf16[4,256,896]{2,1,0:T(8,128)(2,1)}, u32[]{:S(2)}, u32[]{:S(2)}) collective-permute-start(bf16[4,256,896]{2,1,0:T(8,128)(2,1)S(1)} %all-to-all-done.refs_4_), channel_id=1, source_target_pairs={{0,32},{32,0},{1,33},{33,1},{2,34},{34,2},{3,35},{35,3},{4,36},{36... | collective-permute-start | bytes 5505032 | tf_op jit(solution)/shard_map/ppermute | solution.py:168
  127.1 0.7 all-to-all-done.1.refs_6_
  127.8 4.5 %collective-permute-start.9 = (bf16[4,256,896]{2,1,0:T(8,128)(2,1)}, bf16[4,256,896]{2,1,0:T(8,128)(2,1)}, u32[]{:S(2)}, u32[]{:S(2)}) collective-permute-start(bf16[4,256,896]{2,1,0:T(8,128)(2,1)} %all-to-all-done.1.refs_6_), channel_id=1, source_target_pairs={{0,32},{32,0},{1,33},{33,1},{2,34},{34,2},{3,35},{35,3},{4,36},{36... | collective-permute-start | bytes 5505032 | tf_op jit(solution)/shard_map/ppermute | solution.py:168
  132.3 1.1 constant_dynamic-update-slice_fusion.6
  133.3 1.1 constant_dynamic-update-slice_fusion.5.refs_2_
  134.4 3.2 %collective-permute-start.6 = (bf16[128,4096]{1,0:T(8,128)(2,1)S(1)}, bf16[128,4096]{1,0:T(8,128)(2,1)}, u32[]{:S(2)}, u32[]{:S(2)}) collective-permute-start(bf16[128,4096]{1,0:T(8,128)(2,1)S(1)} %constant_dynamic-update-slice_fusion.5.refs_2_), channel_id=1, source_target_pairs={{0,3},{1,2},{2,1},{3,0},{32,33},{33,32},{34,35},{35,34},{4,7},{5,6... | collective-permute-start | bytes 3145736 | tf_op jit(solution)/shard_map/ppermute | solution.py:157
  137.7 0.6 stack.166.cols_ref
  138.3 0.6 stack.199.slot_ref
  139.0 0.0 collective-permute-done.3.refs_1_
  139.0 11.4 %collective-permute-done.6.refs_3_ = bf16[128,4096]{1,0:T(8,128)(2,1)} collective-permute-done((bf16[128,4096]{1,0:T(8,128)(2,1)S(1)}, bf16[128,4096]{1,0:T(8,128)(2,1)}, u32[]{:S(2)}, u32[]{:S(2)}) %collective-permute-start.6) | collective-permute-done | bytes 1048608 | tf_op jit(solution)/shard_map/ppermute | solution.py:157
  150.4 0.0 collective-permute-done.7.refs_5_
  150.4 0.0 collective-permute-done.9.refs_7_
  150.4 0.0 copy-done.2
  150.4 0.0 copy-start.9
  150.4 0.0 copy-start.10
  150.4 10.4 %mlp.1 = f32[32,8,128]{2,1,0:T(8,128)} custom-call(s32[16]{0:T(128)} %stack.166.cols_ref, s32[32]{0:T(128)} %stack.199.slot_ref, bf16[128,4096]{1,0:T(8,128)(2,1)} %constant_dynamic-update-slice_fusion.refs_0_, bf16[128,4096]{1,0:T(8,128)(2,1)} %collective-permute-done.3.refs_1_, bf16[128,4096]{1,0:T(8,128)(2,1)} %copy-done.2, ...), custom_call_target="tpu_custom_call" | custom-call | tf_op jit(solution)/shard_map/mlp/pallas_call | solution.py:68
  160.9 14.7 %all-to-all-start.2 = ((f32[32,8,128]{2,1,0:T(8,128)}), f32[32,8,128]{2,1,0:T(8,128)S(1)}, u32[]{:S(2)}, u32[]{:S(2)}) async-start(f32[32,8,128]{2,1,0:T(8,128)} %mlp.1), calls=%async_computation.2 | async-start | bytes 262144 | tf_op jit(solution)/shard_map/all_to_all | solution.py:176
  176.9 0.0 copy-done
  176.9 0.0 copy-done.9
  176.9 0.0 copy-done.10
  176.9 0.9 convolution_bitcast_fusion.right_ref
  177.8 9.9 %all-to-all-done.2.parts_ref = f32[32,8,128]{2,1,0:T(8,128)S(1)} async-done(((f32[32,8,128]{2,1,0:T(8,128)}), f32[32,8,128]{2,1,0:T(8,128)S(1)}, u32[]{:S(2)}, u32[]{:S(2)}) %all-to-all-start.2) | async-done | bytes 131104 | tf_op jit(solution)/shard_map/all_to_all | solution.py:176
  187.7 0.6 copy-done.6
  188.4 2.1 norm.1
  190.4 0.7 broadcast_in_dim.15
  191.1 26.5 %all_to_all.25.roll_ref = f32[16,8,128]{2,1,0:T(8,128)} all-to-all(f32[16,8,128]{2,1,0:T(8,128)S(1)} %broadcast_in_dim.15), channel_id=1, replica_groups=mesh['x'=4,'zh'=2,'co'=2,'zl'=8,'y'=4] {'x','zh','co'}, dimensions={0} | all-to-all | bytes 131072 | tf_op jit(solution)/shard_map/all_to_all | solution.py:182
  217.6 0.7 broadcast_in_dim.14
  218.3 16.6 %all_to_all.26.train_ref = f32[32,8,128]{2,1,0:T(8,128)} all-to-all(f32[32,8,128]{2,1,0:T(8,128)S(1)} %broadcast_in_dim.14), channel_id=1, replica_groups=mesh['x'=4,'zh'=2,'co'=2,'zl'=8,'y'=4] {'zl','y'}, dimensions={0} | all-to-all | bytes 262144 | tf_op jit(solution)/shard_map/all_to_all | solution.py:185
  234.8 2.1 score.1
  (10 shorter events, 0.0 us)
Async XLA Ops:
  0.0 176.9 %copy-start = (bf16[4096,64]{0,1:T(8,128)(2,1)S(1)}, bf16[4096,64]{0,1:T(8,128)(2,1)}, u32[]{:S(2)}) copy-start(bf16[4096,64]{0,1:T(8,128)(2,1)} %param.19) | copy-start | bytes 1572868
  0.0 40.8 %copy-start.8 = (bf16[256,448]{0,1:T(8,128)(2,1)S(1)}, bf16[256,448]{0,1:T(8,128)(2,1)}, u32[]{:S(2)}) copy-start(bf16[256,448]{0,1:T(8,128)(2,1)} %param.17) | copy-start | bytes 688132
  1.0 12.0 %collective-permute-start = (bf16[16,4096]{1,0:T(8,128)(2,1)S(1)}, bf16[16,4096]{1,0:T(8,128)(2,1)S(1)}, u32[]{:S(2)}, u32[]{:S(2)}) collective-permute-start(bf16[16,4096]{1,0:T(8,128)(2,1)S(1)} %pad_maximum_fusion.2), channel_id=1, source_target_pairs={{0,16},{4,20},{8,24},{12,28},{16,0},{20,4},{24,8},{28,12},{1,17},{... | collective-permute-start | bytes 393224 | tf_op jit(solution)/shard_map/ppermute | solution.py:140
  13.9 14.4 %collective-permute-start.1 = (bf16[32,4096]{1,0:T(8,128)(2,1)S(1)}, bf16[32,4096]{1,0:T(8,128)(2,1)S(1)}, u32[]{:S(2)}, u32[]{:S(2)}) collective-permute-start(bf16[32,4096]{1,0:T(8,128)(2,1)S(1)} %pad_maximum_fusion.1), channel_id=1, source_target_pairs={{0,8},{4,12},{8,0},{12,4},{16,24},{20,28},{24,16},{28,20},{1,9},{5... | collective-permute-start | bytes 786440 | tf_op jit(solution)/shard_map/ppermute | solution.py:140
  30.0 31.1 %collective-permute-start.4 = (bf16[64,4096]{1,0:T(8,128)(2,1)}, bf16[64,4096]{1,0:T(8,128)(2,1)}, u32[]{:S(2)}, u32[]{:S(2)}) collective-permute-start(bf16[64,4096]{1,0:T(8,128)(2,1)} %pad_maximum_fusion), channel_id=1, source_target_pairs={{0,4},{4,0},{8,12},{12,8},{16,20},{20,16},{24,28},{28,24},{1,5},{5... | collective-permute-start | bytes 1572872 | tf_op jit(solution)/shard_map/ppermute | solution.py:145
  40.8 1.7 copy-start.5
  42.5 23.3 %copy-start.3 = (bf16[1,8,4096]{2,1,0:T(8,128)(2,1)S(1)}, bf16[1,8,4096]{2,1,0:T(8,128)(2,1)}, u32[]{:S(2)}) copy-start(bf16[1,8,4096]{2,1,0:T(8,128)(2,1)} %param.10) | copy-start | bytes 196612
  42.5 57.3 %all-to-all-start = ((bf16[4,256,896]{2,1,0:T(8,128)(2,1)}), bf16[4,256,896]{2,1,0:T(8,128)(2,1)S(1)}, u32[]{:S(2)}, u32[]{:S(2)}) async-start(bf16[4,256,896]{2,1,0:T(8,128)(2,1)} %broadcast_in_dim.12), calls=%async_computation | async-start | bytes 3670016 | tf_op jit(solution)/shard_map/all_to_all | solution.py:162
  48.6 49.1 %collective-permute-start.8 = (bf16[256,896]{0,1:T(8,128)(2,1)}, bf16[256,896]{0,1:T(8,128)(2,1)S(1)}, u32[]{:S(2)}, u32[]{:S(2)}) collective-permute-start(bf16[256,896]{0,1:T(8,128)(2,1)} %copy-done.5), channel_id=1, source_target_pairs={{0,64},{64,0},{1,65},{65,1},{2,66},{66,2},{3,67},{67,3},{4,68},{68... | collective-permute-start | bytes 1376264 | tf_op jit(solution)/shard_map/ppermute | solution.py:143
  61.1 37.4 %collective-permute-start.5 = (bf16[64,4096]{1,0:T(8,128)(2,1)}, bf16[64,4096]{1,0:T(8,128)(2,1)}, u32[]{:S(2)}, u32[]{:S(2)}) collective-permute-start(bf16[64,4096]{1,0:T(8,128)(2,1)} %collective-permute-done.4), channel_id=1, source_target_pairs={{0,1},{1,0},{2,3},{3,2},{32,35},{33,34},{34,33},{35,32},{4,5},{5,4... | collective-permute-start | bytes 1572872 | tf_op jit(solution)/shard_map/ppermute | solution.py:155
  97.7 0.8 copy-start.7
  99.8 21.2 %copy-start.1 = (bf16[4,256,896]{2,1,0:T(8,128)(2,1)}, bf16[4,256,896]{2,1,0:T(8,128)(2,1)S(1)}, u32[]{:S(2)}) copy-start(bf16[4,256,896]{2,1,0:T(8,128)(2,1)S(1)} %all-to-all-done.refs_4_) | copy-start | bytes 5505028
  101.3 4.5 %copy-start.4 = (bf16[1,8,4096]{2,1,0:T(8,128)(2,1)S(1)}, bf16[1,8,4096]{2,1,0:T(8,128)(2,1)}, u32[]{:S(2)}) copy-start(bf16[1,8,4096]{2,1,0:T(8,128)(2,1)} %param.13) | copy-start | bytes 196612
  101.3 26.5 %all-to-all-start.1 = ((bf16[4,256,896]{2,1,0:T(8,128)(2,1)}), bf16[4,256,896]{2,1,0:T(8,128)(2,1)}, u32[]{:S(2)}, u32[]{:S(2)}) async-start(bf16[4,256,896]{2,1,0:T(8,128)(2,1)} %broadcast_in_dim.13), calls=%async_computation.1 | async-start | bytes 3670016 | tf_op jit(solution)/shard_map/all_to_all | solution.py:162
  106.5 11.8 %collective-permute-start.2 = (bf16[64,4096]{1,0:T(8,128)(2,1)}, bf16[64,4096]{1,0:T(8,128)(2,1)S(1)}, u32[]{:S(2)}, u32[]{:S(2)}) collective-permute-start(bf16[64,4096]{1,0:T(8,128)(2,1)} %pad_maximum_fusion), channel_id=1, source_target_pairs={{0,1},{1,0},{2,3},{3,2},{32,35},{33,34},{34,33},{35,32},{4,5},{5,4... | collective-permute-start | bytes 1572872 | tf_op jit(solution)/shard_map/ppermute | solution.py:155
  119.1 19.9 %collective-permute-start.3 = (bf16[128,4096]{1,0:T(8,128)(2,1)}, bf16[128,4096]{1,0:T(8,128)(2,1)}, u32[]{:S(2)}, u32[]{:S(2)}) collective-permute-start(bf16[128,4096]{1,0:T(8,128)(2,1)} %constant_dynamic-update-slice_fusion.refs_0_), channel_id=1, source_target_pairs={{0,3},{1,2},{2,1},{3,0},{32,33},{33,32},{34,35},{35,34},{4,7},{5,6... | collective-permute-start | bytes 3145736 | tf_op jit(solution)/shard_map/ppermute | solution.py:157
  121.0 29.4 %collective-permute-start.7 = (bf16[4,256,896]{2,1,0:T(8,128)(2,1)S(1)}, bf16[4,256,896]{2,1,0:T(8,128)(2,1)}, u32[]{:S(2)}, u32[]{:S(2)}) collective-permute-start(bf16[4,256,896]{2,1,0:T(8,128)(2,1)S(1)} %all-to-all-done.refs_4_), channel_id=1, source_target_pairs={{0,32},{32,0},{1,33},{33,1},{2,34},{34,2},{3,35},{35,3},{4,36},{36... | collective-permute-start | bytes 5505032 | tf_op jit(solution)/shard_map/ppermute | solution.py:168
  127.8 22.6 %collective-permute-start.9 = (bf16[4,256,896]{2,1,0:T(8,128)(2,1)}, bf16[4,256,896]{2,1,0:T(8,128)(2,1)}, u32[]{:S(2)}, u32[]{:S(2)}) collective-permute-start(bf16[4,256,896]{2,1,0:T(8,128)(2,1)} %all-to-all-done.1.refs_6_), channel_id=1, source_target_pairs={{0,32},{32,0},{1,33},{33,1},{2,34},{34,2},{3,35},{35,3},{4,36},{36... | collective-permute-start | bytes 5505032 | tf_op jit(solution)/shard_map/ppermute | solution.py:168
  134.4 16.0 %copy-start.2 = (bf16[128,4096]{1,0:T(8,128)(2,1)}, bf16[128,4096]{1,0:T(8,128)(2,1)S(1)}, u32[]{:S(2)}) copy-start(bf16[128,4096]{1,0:T(8,128)(2,1)S(1)} %constant_dynamic-update-slice_fusion.5.refs_2_) | copy-start | bytes 3145732
  134.4 15.9 %collective-permute-start.6 = (bf16[128,4096]{1,0:T(8,128)(2,1)S(1)}, bf16[128,4096]{1,0:T(8,128)(2,1)}, u32[]{:S(2)}, u32[]{:S(2)}) collective-permute-start(bf16[128,4096]{1,0:T(8,128)(2,1)S(1)} %constant_dynamic-update-slice_fusion.5.refs_2_), channel_id=1, source_target_pairs={{0,3},{1,2},{2,1},{3,0},{32,33},{33,32},{34,35},{35,34},{4,7},{5,6... | collective-permute-start | bytes 3145736 | tf_op jit(solution)/shard_map/ppermute | solution.py:157
  150.4 26.5 %copy-start.9 = (bf16[1,8,4096]{2,1,0:T(8,128)(2,1)S(1)}, bf16[1,8,4096]{2,1,0:T(8,128)(2,1)}, u32[]{:S(2)}) copy-start(bf16[1,8,4096]{2,1,0:T(8,128)(2,1)} %param.14) | copy-start | bytes 196612
  150.4 26.5 %copy-start.10 = (bf16[1,8,4096]{2,1,0:T(8,128)(2,1)S(1)}, bf16[1,8,4096]{2,1,0:T(8,128)(2,1)}, u32[]{:S(2)}) copy-start(bf16[1,8,4096]{2,1,0:T(8,128)(2,1)} %param.11) | copy-start | bytes 196612
  160.9 26.9 %all-to-all-start.2 = ((f32[32,8,128]{2,1,0:T(8,128)}), f32[32,8,128]{2,1,0:T(8,128)S(1)}, u32[]{:S(2)}, u32[]{:S(2)}) async-start(f32[32,8,128]{2,1,0:T(8,128)} %mlp.1), calls=%async_computation.2 | async-start | bytes 262144 | tf_op jit(solution)/shard_map/all_to_all | solution.py:176
  187.7 0.6 copy-start.6

commit v5 on v4

--- a/solution.py
+++ b/solution.py
@@ -16,41 +16,36 @@
     x_refs = refs[:nx]
     w_refs = refs[nx : nx + nw]
     ip_ref, out_ref, xv, wv, acc, xsem, wsem = refs[nx + nw :]
-    copies, at = [], 0
-    for i, x_ref in enumerate(x_refs):
-        n = x_ref.shape[0]
-        copies.append(pltpu.make_async_copy(x_ref, xv.at[pl.ds(at, n)], xsem.at[i]))
-        at += n
-    loads, at = [], 0
-    for p, w_ref in enumerate(w_refs):
-        depth = w_ref.shape[1]
-        loads.append((pltpu.make_async_copy(w_ref, wv.at[pl.ds(at, 4), pl.ds(0, depth)], wsem.at[p]), at, depth))
-        at += 4
-    for c in copies:
-        c.start()
-    for c, _, _ in loads:
-        c.start()
-    for c in copies:
+    half_k = xv.shape[1] // 2
+    xcopies, wcopies = [[], []], [[], []]
+    for h in range(2):
+        at = 0
+        for i, x_ref in enumerate(x_refs):
+            n = x_ref.shape[0]
+            cut = pl.ds(h * half_k, half_k)
+            xcopies[h].append(
+                pltpu.make_async_copy(x_ref.at[:, cut], xv.at[pl.ds(at, n), cut], xsem.at[h * nx + i])
+            )
+            at += n
+    for p in range(nw):
+        for j in range(4):
+            row = pl.multiple_of(cols_ref[p * 4 + j], 256)
+            wcopies[j // 2].append(
+                pltpu.make_async_copy(w_refs[p].at[j], wv.at[pl.ds(row, 256)], wsem.at[p * 4 + j])
+            )
+    for h in range(2):
+        for c in xcopies[h] + wcopies[h]:
+            c.start()
+    for c in xcopies[0] + wcopies[0]:
         c.wait()
-    for p, (c, at, depth) in enumerate(loads):
+    acc[...] = jnp.dot(xv[:, :half_k], wv[:half_k], preferred_element_type=jnp.float32)
+    for c in xcopies[1] + wcopies[1]:
         c.wait()
-        picked = []
-        for j in range(4):
-            col = pl.multiple_of(cols_ref[p * 4 + j], 128)
-            picked.append(xv[:, pl.ds(col, depth)])
-        part = jnp.dot(
-            jnp.concatenate(picked, axis=1),
-            wv[at : at + 4, :depth].reshape(4 * depth, wv.shape[2]),
-            preferred_element_type=jnp.float32,
-        )
-        if p == 0:
-            acc[...] = part
-        else:
-            acc[...] += part
+    acc[...] += jnp.dot(xv[:, half_k:], wv[half_k:], preferred_element_type=jnp.float32)
     half = acc.shape[1] // 2
     for m in range(4):
-        rows = acc[m * 128 : (m + 1) * 128, :]
-        gate, up = rows[:, :half], rows[:, half:]
+        both = acc[m * 128 : (m + 1) * 128]
+        gate, up = both[:, :half], both[:, half:]
         act = (gate / (1.0 + jnp.exp(-gate)) * up).astype(jnp.bfloat16)
         left = lax.dot_general(
             act, ip_ref[...], (((1,), (1,)), ((), ())), preferred_element_type=jnp.float32
@@ -72,10 +67,10 @@
         out_specs=pl.BlockSpec(memory_space=pltpu.VMEM),
         scratch_shapes=[
             pltpu.VMEM((512, xs[0].shape[1]), jnp.bfloat16),
-            pltpu.VMEM((4 * nw,) + ws[0].shape[1:], jnp.bfloat16),
+            pltpu.VMEM((4096, ws[0].shape[2]), jnp.bfloat16),
             pltpu.VMEM((512, ws[0].shape[2]), jnp.float32),
-            pltpu.SemaphoreType.DMA((nx,)),
-            pltpu.SemaphoreType.DMA((nw,)),
+            pltpu.SemaphoreType.DMA((2 * nx,)),
+            pltpu.SemaphoreType.DMA((4 * nw,)),
         ],
         compiler_params=pltpu.CompilerParams(vmem_limit_bytes=60 << 20),
         name="mlp",
@@ -96,7 +91,7 @@
         ref[...] = jnp.concatenate([one * inv, right], axis=-1)
 
 
-def score_kernel(train_ref, roll_ref, out_ref):
+def score_kernel(train_ref, roll_ref, y_ref, out_ref):
     t = train_ref[...].reshape(-1, 2 * RANK)
     r = roll_ref[...].reshape(-1, 2 * RANK)
     dims = (((1,), (1,)), ((), ()))
@@ -107,10 +102,11 @@
         r[:, RANK:], t[:, RANK:], dims, precision=HIGH, preferred_element_type=jnp.float32
     )
     both = jnp.sum((a * b).reshape(16, 8, 256), axis=1)
-    pick = (
-        lax.broadcasted_iota(jnp.int32, (256, 32), 0) // 8
-        == lax.broadcasted_iota(jnp.int32, (256, 32), 1)
-    ).astype(jnp.float32)
+    group = lax.broadcasted_iota(jnp.int32, (256, 32), 0) // 8
+    step = group & 3
+    step = step ^ (step >> 1)
+    column = (group & 28) + ((y_ref[0] - step) & 3)
+    pick = (column == lax.broadcasted_iota(jnp.int32, (256, 32), 1)).astype(jnp.float32)
     out_ref[...] = jnp.dot(both, pick, precision=HIGH, preferred_element_type=jnp.float32) / RANK
 
 
@@ -135,12 +131,11 @@
     own = jnp.concatenate([train_hidden[0], roll_hidden[0]], axis=0)
     w = jnp.concatenate([gate_weight, up_weight], axis=1)
 
+    other = lax.ppermute(w, "zh", shift(2, 1))
+
     block, zls = own, [zl]
     for k in (4, 2):
         got = lax.ppermute(block, "zl", [(i, i ^ k) for i in range(NZL)])
-        if k == 4:
-            far_w, _ = lax.optimization_barrier((w, got))
-            other = lax.ppermute(far_w, "zh", shift(2, 1))
         block, zls = jnp.concatenate([block, got], axis=0), zls + [z ^ k for z in zls]
     twin = lax.ppermute(block, "zl", [(i, i ^ 1) for i in range(NZL)])
 
@@ -162,7 +157,6 @@
         return lax.all_to_all(spread, "x", 0, 0, tiled=True)
 
     ws, cols = [], []
-    other, _ = lax.optimization_barrier((other, got))
     for a, h in ((w, zh), (other, 1 - zh)):
         a = over_x(a)
         ws += [a, lax.ppermute(a, "co", shift(2, 1))]
@@ -182,12 +176,16 @@
     roll_all = lax.all_to_all(
         jnp.broadcast_to(roll, (16, 8, 2 * RANK)), ("x", "zh", "co"), 0, 0, tiled=True
     )
+    near = [train] + [lax.ppermute(train, "y", shift(NY, k)) for k in (1, 3, 2)]
     train_all = lax.all_to_all(
-        jnp.broadcast_to(train, (32, 8, 2 * RANK)), ("zl", "y"), 0, 0, tiled=True
+        jnp.broadcast_to(jnp.stack(near), (NZL, NY, 8, 2 * RANK)), "zl", 0, 0, tiled=True
     )
     scores = pl.pallas_call(
-        score_kernel, out_shape=jax.ShapeDtypeStruct((16, 32), jnp.float32), name="score"
-    )(train_all, roll_all)
+        score_kernel,
+        out_shape=jax.ShapeDtypeStruct((16, 32), jnp.float32),
+        in_specs=[vmem, vmem, smem],
+        name="score",
+    )(train_all, roll_all, y.astype(jnp.int32).reshape(1))
     return scores.T
 
 

time: 239 us -> 210 us (0.88)
  blocking collectives: 43 us -> 13.8 us
  waiting for transfers between devices: 64.4 us -> 73.3 us
  starting transfers between devices: 93.7 us -> 87.1 us
    all_to_all x2 -> x1, blocking collectives: 43 us -> 13.8 us  [on_device(): lax.all_to_all(jnp.broadcast_to(jnp.stack(near), (NZL, NY, 8, 2 * RANK)),...]
    ppermute x1 -> x4, waiting for transfers between devices: 31.3 us -> 9.9 us  [the longest x1 5.6 us: on_device(): other = lax.ppermute(w, 'zh', shift(2, 1))]
    all_to_all x0 -> x1, starting transfers between devices: none -> 15.8 us  [on_device(): lax.all_to_all(jnp.broadcast_to(roll, (16, 8, 2 * RANK)), ('x', 'zh', 'co...]
    ppermute x2, waiting for transfers between devices: 5.31 us -> 19.9 us  [on_device(): got = lax.ppermute(block, 'zl', [(i, i ^ k) for i in range(NZL)])]
    all_to_all x2, waiting for transfers between devices: 0.69 us -> 10.1 us  [over_x(): return lax.all_to_all(spread, 'x', 0, 0, tiled=True)]
    ppermute x1, starting transfers between devices: 10.8 us -> 1.92 us  [on_device(): twin = lax.ppermute(block, 'zl', [(i, i ^ 1) for i in range(NZL)])]
    ppermute x2, starting transfers between devices: 20.1 us -> 12.7 us  [on_device(): got = lax.ppermute(block, 'zl', [(i, i ^ k) for i in range(NZL)])]
    ppermute x1, waiting for transfers between devices: 0.01 us -> 7.13 us  [on_device(): twin = lax.ppermute(block, 'zl', [(i, i ^ 1) for i in range(NZL)])]
  transfers between devices with their start and end apart: 13 -> 17, of which waited for: 7 -> 9; matrix products, arithmetic and copies ran while one was open for 5% -> 7% of each run, Pallas kernels for 0% -> 0%
where the time goes in v5:
time: 210 us; the launch traced here: 208 us
  starting transfers between devices  87.1 us (41%)
  waiting for transfers between devices  73.3 us (35%)
  local copies, waits for them, and re-layouts  15.2 us (7%)
  Pallas kernels  13.9 us (7%)
  blocking collectives  13.8 us (7%)
  other arithmetic  2.36 us (1%)
    ppermute x2, waiting for transfers between devices, on_device(): got = lax.ppermute(block, 'zl', [(i, i ^ k) for i in range(NZL)])  19.9 us
    all_to_all x1, starting transfers between devices, on_device(): lax.all_to_all(jnp.broadcast_to(roll, (16, 8, 2 * RANK)), ('x', 'zh', 'co...  15.8 us
    ppermute x2, waiting for transfers between devices, on_device(): xs += [both, lax.ppermute(both, ('co', 'y'), step2)]  15.3 us
    all_to_all x1, blocking collectives, on_device(): lax.all_to_all(jnp.broadcast_to(jnp.stack(near), (NZL, NY, 8, 2 * RANK)),...  13.8 us
    ppermute x2, starting transfers between devices, on_device(): got = lax.ppermute(block, 'zl', [(i, i ^ k) for i in range(NZL)])  12.7 us
    ppermute x1, starting transfers between devices, on_device(): other = lax.ppermute(w, 'zh', shift(2, 1))  10.6 us
    all_to_all x2, waiting for transfers between devices, over_x(): return lax.all_to_all(spread, 'x', 0, 0, tiled=True)  10.1 us
    all_to_all x1, waiting for transfers between devices, on_device(): parts = lax.all_to_all(parts, ('zl', 'y'), 0, 0, tiled=True)  9.99 us
  transfers between devices with their start and end apart: 17, of which 9 were waited for; matrix products, arithmetic and copies ran while one was open for 7% of the time, Pallas kernels for 0%

profile of v5, /device:TPU:1, one launch (start us, length us, event | category | flops | bytes accessed | tf_op | source)
XLA Modules:
  0.0 208.2 jit_solution(15325701206988149332)
XLA Ops:
  0.0 0.0 copy-start
  0.0 0.9 pad_maximum_fusion.2
  0.9 9.6 %collective-permute-start = (bf16[16,4096]{1,0:T(8,128)(2,1)S(1)}, bf16[16,4096]{1,0:T(8,128)(2,1)S(1)}, u32[]{:S(2)}, u32[]{:S(2)}) collective-permute-start(bf16[16,4096]{1,0:T(8,128)(2,1)S(1)} %pad_maximum_fusion.2), channel_id=1, source_target_pairs={{0,16},{4,20},{8,24},{12,28},{16,0},{20,4},{24,8},{28,12},{1,17},{... | collective-permute-start | bytes 393224 | tf_op jit(solution)/shard_map/ppermute | solution.py:138
  10.6 1.0 constant_dynamic-update-slice_fusion.8
  11.6 1.0 constant_dynamic-update-slice_fusion.7
  12.5 10.6 %collective-permute-start.8 = (bf16[256,896]{0,1:T(8,128)(2,1)S(1)}, bf16[256,896]{0,1:T(8,128)(2,1)}, u32[]{:S(2)}, u32[]{:S(2)}) collective-permute-start(bf16[256,896]{0,1:T(8,128)(2,1)S(1)} %constant_dynamic-update-slice_fusion.7), channel_id=1, source_target_pairs={{0,64},{64,0},{1,65},{65,1},{2,66},{66,2},{3,67},{67,3},{4,68},{68... | collective-permute-start | bytes 1376264 | tf_op jit(solution)/shard_map/ppermute | solution.py:134
  23.2 0.2 copy.11
  23.4 1.4 broadcast_in_dim.12
  24.8 4.1 %all-to-all-start = ((bf16[4,256,896]{2,1,0:T(8,128)(2,1)}), bf16[4,256,896]{2,1,0:T(8,128)(2,1)S(1)}, u32[]{:S(2)}, u32[]{:S(2)}) async-start(bf16[4,256,896]{2,1,0:T(8,128)(2,1)} %broadcast_in_dim.12), calls=%async_computation | async-start | bytes 3670016 | tf_op jit(solution)/shard_map/all_to_all | solution.py:157
  29.0 0.0 copy-done.3
  29.0 0.6 constant_dynamic-update-slice_fusion.4
  29.6 0.0 collective-permute-done
  29.6 0.7 pad_maximum_fusion.1
  30.3 3.1 %collective-permute-start.1 = (bf16[32,4096]{1,0:T(8,128)(2,1)}, bf16[32,4096]{1,0:T(8,128)(2,1)S(1)}, u32[]{:S(2)}, u32[]{:S(2)}) collective-permute-start(bf16[32,4096]{1,0:T(8,128)(2,1)} %pad_maximum_fusion.1), channel_id=1, source_target_pairs={{0,8},{4,12},{8,0},{12,4},{16,24},{20,28},{24,16},{28,20},{1,9},{5... | collective-permute-start | bytes 786440 | tf_op jit(solution)/shard_map/ppermute | solution.py:138
  33.4 0.6 constant_dynamic-update-slice_fusion.3
  34.0 5.6 %collective-permute-done.8 = bf16[256,896]{0,1:T(8,128)(2,1)} collective-permute-done((bf16[256,896]{0,1:T(8,128)(2,1)S(1)}, bf16[256,896]{0,1:T(8,128)(2,1)}, u32[]{:S(2)}, u32[]{:S(2)}) %collective-permute-start.8) | collective-permute-done | bytes 458784 | tf_op jit(solution)/shard_map/ppermute | solution.py:134
  39.6 1.3 copy.12
  40.9 10.1 %all-to-all-done.refs_4_ = bf16[4,256,896]{2,1,0:T(8,128)(2,1)S(1)} async-done(((bf16[4,256,896]{2,1,0:T(8,128)(2,1)}), bf16[4,256,896]{2,1,0:T(8,128)(2,1)S(1)}, u32[]{:S(2)}, u32[]{:S(2)}) %all-to-all-start) | async-done | bytes 1835040 | tf_op jit(solution)/shard_map/all_to_all | solution.py:157
  51.0 1.5 broadcast_in_dim.13
  52.5 4.4 %all-to-all-start.1 = ((bf16[4,256,896]{2,1,0:T(8,128)(2,1)}), bf16[4,256,896]{2,1,0:T(8,128)(2,1)}, u32[]{:S(2)}, u32[]{:S(2)}) async-start(bf16[4,256,896]{2,1,0:T(8,128)(2,1)} %broadcast_in_dim.13), calls=%async_computation.1 | async-start | bytes 3670016 | tf_op jit(solution)/shard_map/all_to_all | solution.py:157
  56.9 19.9 %collective-permute-done.1 = bf16[32,4096]{1,0:T(8,128)(2,1)S(1)} collective-permute-done((bf16[32,4096]{1,0:T(8,128)(2,1)}, bf16[32,4096]{1,0:T(8,128)(2,1)S(1)}, u32[]{:S(2)}, u32[]{:S(2)}) %collective-permute-start.1) | collective-permute-done | bytes 262176 | tf_op jit(solution)/shard_map/ppermute | solution.py:138
  76.8 1.9 collective-permute-start.4
  78.7 4.6 %collective-permute-start.2 = (bf16[64,4096]{1,0:T(8,128)(2,1)S(1)}, bf16[64,4096]{1,0:T(8,128)(2,1)S(1)}, u32[]{:S(2)}, u32[]{:S(2)}) collective-permute-start(bf16[64,4096]{1,0:T(8,128)(2,1)S(1)} %pad_maximum_fusion), channel_id=1, source_target_pairs={{0,1},{1,0},{2,3},{3,2},{32,35},{33,34},{34,33},{35,32},{4,5},{5,4... | collective-permute-start | bytes 1572872 | tf_op jit(solution)/shard_map/ppermute | solution.py:150
  83.4 0.7 constant_dynamic-update-slice_fusion.2
  84.1 0.7 constant_dynamic-update-slice_fusion.1
  84.8 7.1 %collective-permute-done.4 = bf16[64,4096]{1,0:T(8,128)(2,1)} collective-permute-done((bf16[64,4096]{1,0:T(8,128)(2,1)S(1)}, bf16[64,4096]{1,0:T(8,128)(2,1)}, u32[]{:S(2)}, u32[]{:S(2)}) %collective-permute-start.4) | collective-permute-done | bytes 524320 | tf_op jit(solution)/shard_map/ppermute | solution.py:140
  91.9 4.6 %collective-permute-start.5 = (bf16[64,4096]{1,0:T(8,128)(2,1)}, bf16[64,4096]{1,0:T(8,128)(2,1)}, u32[]{:S(2)}, u32[]{:S(2)}) collective-permute-start(bf16[64,4096]{1,0:T(8,128)(2,1)} %collective-permute-done.4), channel_id=1, source_target_pairs={{0,1},{1,0},{2,3},{3,2},{32,35},{33,34},{34,33},{35,32},{4,5},{5,4... | collective-permute-start | bytes 1572872 | tf_op jit(solution)/shard_map/ppermute | solution.py:150
  96.6 0.0 collective-permute-done.2
  96.6 0.8 constant_dynamic-update-slice_fusion.refs_0_
  97.4 1.9 collective-permute-start.3
  99.3 0.0 copy-done.1
  99.3 4.1 %collective-permute-start.7 = (bf16[4,256,896]{2,1,0:T(8,128)(2,1)S(1)}, bf16[4,256,896]{2,1,0:T(8,128)(2,1)}, u32[]{:S(2)}, u32[]{:S(2)}) collective-permute-start(bf16[4,256,896]{2,1,0:T(8,128)(2,1)S(1)} %all-to-all-done.refs_4_), channel_id=1, source_target_pairs={{0,32},{32,0},{1,33},{33,1},{2,34},{34,2},{3,35},{35,3},{4,36},{36... | collective-permute-start | bytes 5505032 | tf_op jit(solution)/shard_map/ppermute | solution.py:162
  103.5 0.0 all-to-all-done.1.refs_6_
  103.5 1.9 collective-permute-start.9
  105.4 1.1 constant_dynamic-update-slice_fusion.6
  106.5 0.0 collective-permute-done.5
  106.5 1.1 constant_dynamic-update-slice_fusion.5.refs_2_
  107.6 2.3 %collective-permute-start.6 = (bf16[128,4096]{1,0:T(8,128)(2,1)S(1)}, bf16[128,4096]{1,0:T(8,128)(2,1)}, u32[]{:S(2)}, u32[]{:S(2)}) collective-permute-start(bf16[128,4096]{1,0:T(8,128)(2,1)S(1)} %constant_dynamic-update-slice_fusion.5.refs_2_), channel_id=1, source_target_pairs={{0,3},{1,2},{2,1},{3,0},{32,33},{33,32},{34,35},{35,34},{4,7},{5,6... | collective-permute-start | bytes 3145736 | tf_op jit(solution)/shard_map/ppermute | solution.py:152
  110.0 0.6 stack.181.cols_ref
  110.6 0.6 stack.214.slot_ref
  111.3 4.0 %collective-permute-done.3.refs_1_ = bf16[128,4096]{1,0:T(8,128)(2,1)} collective-permute-done((bf16[128,4096]{1,0:T(8,128)(2,1)}, bf16[128,4096]{1,0:T(8,128)(2,1)}, u32[]{:S(2)}, u32[]{:S(2)}) %collective-permute-start.3) | collective-permute-done | bytes 1048608 | tf_op jit(solution)/shard_map/ppermute | solution.py:152
  115.3 11.3 %collective-permute-done.6.refs_3_ = bf16[128,4096]{1,0:T(8,128)(2,1)} collective-permute-done((bf16[128,4096]{1,0:T(8,128)(2,1)S(1)}, bf16[128,4096]{1,0:T(8,128)(2,1)}, u32[]{:S(2)}, u32[]{:S(2)}) %collective-permute-start.6) | collective-permute-done | bytes 1048608 | tf_op jit(solution)/shard_map/ppermute | solution.py:152
  126.6 0.0 collective-permute-done.7.refs_5_
  126.6 0.0 collective-permute-done.9.refs_7_
  126.6 0.0 copy-start.7
  126.6 0.0 copy-start.8
  126.7 9.7 %mlp.1 = f32[32,8,128]{2,1,0:T(8,128)} custom-call(s32[16]{0:T(128)} %stack.181.cols_ref, s32[32]{0:T(128)} %stack.214.slot_ref, bf16[128,4096]{1,0:T(8,128)(2,1)} %constant_dynamic-update-slice_fusion.refs_0_, bf16[128,4096]{1,0:T(8,128)(2,1)} %collective-permute-done.3.refs_1_, bf16[128,4096]{1,0:T(8,128)(2,1)} %copy-done.2, ...), custom_call_target="tpu_custom_call" | custom-call | tf_op jit(solution)/shard_map/mlp/pallas_call | solution.py:63
  136.4 9.3 %all-to-all-start.2 = ((f32[32,8,128]{2,1,0:T(8,128)}), f32[32,8,128]{2,1,0:T(8,128)S(1)}, u32[]{:S(2)}, u32[]{:S(2)}) async-start(f32[32,8,128]{2,1,0:T(8,128)} %mlp.1), calls=%async_computation.2 | async-start | bytes 262144 | tf_op jit(solution)/shard_map/all_to_all | solution.py:170
  147.0 0.9 convolution_bitcast_fusion.right_ref
  147.9 10.0 %all-to-all-done.2.parts_ref = f32[32,8,128]{2,1,0:T(8,128)S(1)} async-done(((f32[32,8,128]{2,1,0:T(8,128)}), f32[32,8,128]{2,1,0:T(8,128)S(1)}, u32[]{:S(2)}, u32[]{:S(2)}) %all-to-all-start.2) | async-done | bytes 131104 | tf_op jit(solution)/shard_map/all_to_all | solution.py:170
  157.9 0.6 copy-done.5
  158.5 2.0 norm.1
  160.5 1.3 broadcast_in_dim.15
  161.8 15.8 %all-to-all-start.4 = ((f32[16,8,128]{2,1,0:T(8,128)}), f32[16,8,128]{2,1,0:T(8,128)S(1)}, u32[]{:S(2)}, u32[]{:S(2)}) async-start(f32[16,8,128]{2,1,0:T(8,128)} %broadcast_in_dim.15), calls=%async_computation.4 | async-start | bytes 131072 | tf_op jit(solution)/shard_map/all_to_all | solution.py:176
  177.7 2.3 %collective-permute-start.10 = (f32[8,128]{1,0:T(8,128)}, f32[8,128]{1,0:T(8,128)S(1)}, u32[]{:S(2)}, u32[]{:S(2)}) collective-permute-start(f32[8,128]{1,0:T(8,128)} %get-tuple-element.7), channel_id=1, source_target_pairs={{0,1},{1,2},{2,3},{3,0},{4,5},{5,6},{6,7},{7,4},{8,9},{9,10},{10,1... | collective-permute-start | bytes 12296 | tf_op jit(solution)/shard_map/ppermute | solution.py:179
  180.0 4.2 %collective-permute-start.11 = (f32[8,128]{1,0:T(8,128)}, f32[8,128]{1,0:T(8,128)S(1)}, u32[]{:S(2)}, u32[]{:S(2)}) collective-permute-start(f32[8,128]{1,0:T(8,128)} %get-tuple-element.7), channel_id=1, source_target_pairs={{0,3},{1,0},{2,1},{3,2},{4,7},{5,4},{6,5},{7,6},{8,11},{9,8},{10,9... | collective-permute-start | bytes 12296 | tf_op jit(solution)/shard_map/ppermute | solution.py:179
  184.2 2.0 collective-permute-start.12
  186.3 0.0 collective-permute-done.10
  186.3 0.0 collective-permute-done.11
  186.3 4.3 %collective-permute-done.12 = f32[8,128]{1,0:T(8,128)S(1)} collective-permute-done((f32[8,128]{1,0:T(8,128)}, f32[8,128]{1,0:T(8,128)S(1)}, u32[]{:S(2)}, u32[]{:S(2)}) %collective-permute-start.12) | collective-permute-done | bytes 4128 | tf_op jit(solution)/shard_map/ppermute | solution.py:179
  190.6 0.7 pad_maximum_fusion.3
  191.2 1.0 all-to-all-done.4.roll_ref
  192.2 13.8 %all_to_all.25.train_ref = f32[8,4,8,128]{3,2,1,0:T(8,128)} all-to-all(f32[8,4,8,128]{3,2,1,0:T(8,128)S(1)} %broadcast_in_dim.14), channel_id=1, replica_groups=mesh['x'=4,'zh'=2,'co'=2,'zl'=8,'y'=4] {'zl'}, dimensions={0} | all-to-all | bytes 262144 | tf_op jit(solution)/shard_map/all_to_all | solution.py:180
  206.1 2.1 %score.1 = f32[16,32]{1,0:T(8,128)} custom-call(f32[8,4,8,128]{3,2,1,0:T(8,128)} %all_to_all.25.train_ref, f32[16,8,128]{2,1,0:T(8,128)} %copy-done.6, s32[1]{0:T(128)} %bitcast.58.y_ref), custom_call_target="tpu_custom_call" | custom-call | tf_op jit(solution)/shard_map/score/pallas_call | solution.py:183
  (14 shorter events, 0.1 us)
Async XLA Ops:
  0.0 147.0 %copy-start = (bf16[4096,64]{0,1:T(8,128)(2,1)S(1)}, bf16[4096,64]{0,1:T(8,128)(2,1)}, u32[]{:S(2)}) copy-start(bf16[4096,64]{0,1:T(8,128)(2,1)} %param.19) | copy-start | bytes 1572868
  0.9 28.7 %collective-permute-start = (bf16[16,4096]{1,0:T(8,128)(2,1)S(1)}, bf16[16,4096]{1,0:T(8,128)(2,1)S(1)}, u32[]{:S(2)}, u32[]{:S(2)}) collective-permute-start(bf16[16,4096]{1,0:T(8,128)(2,1)S(1)} %pad_maximum_fusion.2), channel_id=1, source_target_pairs={{0,16},{4,20},{8,24},{12,28},{16,0},{20,4},{24,8},{28,12},{1,17},{... | collective-permute-start | bytes 393224 | tf_op jit(solution)/shard_map/ppermute | solution.py:138
  12.5 27.1 %collective-permute-start.8 = (bf16[256,896]{0,1:T(8,128)(2,1)S(1)}, bf16[256,896]{0,1:T(8,128)(2,1)}, u32[]{:S(2)}, u32[]{:S(2)}) collective-permute-start(bf16[256,896]{0,1:T(8,128)(2,1)S(1)} %constant_dynamic-update-slice_fusion.7), channel_id=1, source_target_pairs={{0,64},{64,0},{1,65},{65,1},{2,66},{66,2},{3,67},{67,3},{4,68},{68... | collective-permute-start | bytes 1376264 | tf_op jit(solution)/shard_map/ppermute | solution.py:134
  24.8 4.2 %copy-start.3 = (bf16[1,8,4096]{2,1,0:T(8,128)(2,1)S(1)}, bf16[1,8,4096]{2,1,0:T(8,128)(2,1)}, u32[]{:S(2)}) copy-start(bf16[1,8,4096]{2,1,0:T(8,128)(2,1)} %param.10) | copy-start | bytes 196612
  24.8 4.8 %copy-start.4 = (bf16[1,8,4096]{2,1,0:T(8,128)(2,1)S(1)}, bf16[1,8,4096]{2,1,0:T(8,128)(2,1)}, u32[]{:S(2)}) copy-start(bf16[1,8,4096]{2,1,0:T(8,128)(2,1)} %param.13) | copy-start | bytes 196612
  24.8 26.2 %all-to-all-start = ((bf16[4,256,896]{2,1,0:T(8,128)(2,1)}), bf16[4,256,896]{2,1,0:T(8,128)(2,1)S(1)}, u32[]{:S(2)}, u32[]{:S(2)}) async-start(bf16[4,256,896]{2,1,0:T(8,128)(2,1)} %broadcast_in_dim.12), calls=%async_computation | async-start | bytes 3670016 | tf_op jit(solution)/shard_map/all_to_all | solution.py:157
  30.3 46.5 %collective-permute-start.1 = (bf16[32,4096]{1,0:T(8,128)(2,1)}, bf16[32,4096]{1,0:T(8,128)(2,1)S(1)}, u32[]{:S(2)}, u32[]{:S(2)}) collective-permute-start(bf16[32,4096]{1,0:T(8,128)(2,1)} %pad_maximum_fusion.1), channel_id=1, source_target_pairs={{0,8},{4,12},{8,0},{12,4},{16,24},{20,28},{24,16},{28,20},{1,9},{5... | collective-permute-start | bytes 786440 | tf_op jit(solution)/shard_map/ppermute | solution.py:138
  51.0 48.3 %copy-start.1 = (bf16[4,256,896]{2,1,0:T(8,128)(2,1)}, bf16[4,256,896]{2,1,0:T(8,128)(2,1)S(1)}, u32[]{:S(2)}) copy-start(bf16[4,256,896]{2,1,0:T(8,128)(2,1)S(1)} %all-to-all-done.refs_4_) | copy-start | bytes 5505028
  52.5 51.0 %all-to-all-start.1 = ((bf16[4,256,896]{2,1,0:T(8,128)(2,1)}), bf16[4,256,896]{2,1,0:T(8,128)(2,1)}, u32[]{:S(2)}, u32[]{:S(2)}) async-start(bf16[4,256,896]{2,1,0:T(8,128)(2,1)} %broadcast_in_dim.13), calls=%async_computation.1 | async-start | bytes 3670016 | tf_op jit(solution)/shard_map/all_to_all | solution.py:157
  76.8 15.1 %collective-permute-start.4 = (bf16[64,4096]{1,0:T(8,128)(2,1)S(1)}, bf16[64,4096]{1,0:T(8,128)(2,1)}, u32[]{:S(2)}, u32[]{:S(2)}) collective-permute-start(bf16[64,4096]{1,0:T(8,128)(2,1)S(1)} %pad_maximum_fusion), channel_id=1, source_target_pairs={{0,4},{4,0},{8,12},{12,8},{16,20},{20,16},{24,28},{28,24},{1,5},{5... | collective-permute-start | bytes 1572872 | tf_op jit(solution)/shard_map/ppermute | solution.py:140
  78.7 17.8 %collective-permute-start.2 = (bf16[64,4096]{1,0:T(8,128)(2,1)S(1)}, bf16[64,4096]{1,0:T(8,128)(2,1)S(1)}, u32[]{:S(2)}, u32[]{:S(2)}) collective-permute-start(bf16[64,4096]{1,0:T(8,128)(2,1)S(1)} %pad_maximum_fusion), channel_id=1, source_target_pairs={{0,1},{1,0},{2,3},{3,2},{32,35},{33,34},{34,33},{35,32},{4,5},{5,4... | collective-permute-start | bytes 1572872 | tf_op jit(solution)/shard_map/ppermute | solution.py:150
  91.9 14.6 %collective-permute-start.5 = (bf16[64,4096]{1,0:T(8,128)(2,1)}, bf16[64,4096]{1,0:T(8,128)(2,1)}, u32[]{:S(2)}, u32[]{:S(2)}) collective-permute-start(bf16[64,4096]{1,0:T(8,128)(2,1)} %collective-permute-done.4), channel_id=1, source_target_pairs={{0,1},{1,0},{2,3},{3,2},{32,35},{33,34},{34,33},{35,32},{4,5},{5,4... | collective-permute-start | bytes 1572872 | tf_op jit(solution)/shard_map/ppermute | solution.py:150
  97.4 17.9 %collective-permute-start.3 = (bf16[128,4096]{1,0:T(8,128)(2,1)}, bf16[128,4096]{1,0:T(8,128)(2,1)}, u32[]{:S(2)}, u32[]{:S(2)}) collective-permute-start(bf16[128,4096]{1,0:T(8,128)(2,1)} %constant_dynamic-update-slice_fusion.refs_0_), channel_id=1, source_target_pairs={{0,3},{1,2},{2,1},{3,0},{32,33},{33,32},{34,35},{35,34},{4,7},{5,6... | collective-permute-start | bytes 3145736 | tf_op jit(solution)/shard_map/ppermute | solution.py:152
  99.3 27.3 %collective-permute-start.7 = (bf16[4,256,896]{2,1,0:T(8,128)(2,1)S(1)}, bf16[4,256,896]{2,1,0:T(8,128)(2,1)}, u32[]{:S(2)}, u32[]{:S(2)}) collective-permute-start(bf16[4,256,896]{2,1,0:T(8,128)(2,1)S(1)} %all-to-all-done.refs_4_), channel_id=1, source_target_pairs={{0,32},{32,0},{1,33},{33,1},{2,34},{34,2},{3,35},{35,3},{4,36},{36... | collective-permute-start | bytes 5505032 | tf_op jit(solution)/shard_map/ppermute | solution.py:162
  103.5 23.1 %collective-permute-start.9 = (bf16[4,256,896]{2,1,0:T(8,128)(2,1)}, bf16[4,256,896]{2,1,0:T(8,128)(2,1)}, u32[]{:S(2)}, u32[]{:S(2)}) collective-permute-start(bf16[4,256,896]{2,1,0:T(8,128)(2,1)} %all-to-all-done.1.refs_6_), channel_id=1, source_target_pairs={{0,32},{32,0},{1,33},{33,1},{2,34},{34,2},{3,35},{35,3},{4,36},{36... | collective-permute-start | bytes 5505032 | tf_op jit(solution)/shard_map/ppermute | solution.py:162
  107.6 19.0 %copy-start.2 = (bf16[128,4096]{1,0:T(8,128)(2,1)}, bf16[128,4096]{1,0:T(8,128)(2,1)S(1)}, u32[]{:S(2)}) copy-start(bf16[128,4096]{1,0:T(8,128)(2,1)S(1)} %constant_dynamic-update-slice_fusion.5.refs_2_) | copy-start | bytes 3145732
  107.6 19.0 %collective-permute-start.6 = (bf16[128,4096]{1,0:T(8,128)(2,1)S(1)}, bf16[128,4096]{1,0:T(8,128)(2,1)}, u32[]{:S(2)}, u32[]{:S(2)}) collective-permute-start(bf16[128,4096]{1,0:T(8,128)(2,1)S(1)} %constant_dynamic-update-slice_fusion.5.refs_2_), channel_id=1, source_target_pairs={{0,3},{1,2},{2,1},{3,0},{32,33},{33,32},{34,35},{35,34},{4,7},{5,6... | collective-permute-start | bytes 3145736 | tf_op jit(solution)/shard_map/ppermute | solution.py:152
  126.6 20.4 %copy-start.7 = (bf16[1,8,4096]{2,1,0:T(8,128)(2,1)S(1)}, bf16[1,8,4096]{2,1,0:T(8,128)(2,1)}, u32[]{:S(2)}) copy-start(bf16[1,8,4096]{2,1,0:T(8,128)(2,1)} %param.14) | copy-start | bytes 196612
  126.6 20.4 %copy-start.8 = (bf16[1,8,4096]{2,1,0:T(8,128)(2,1)S(1)}, bf16[1,8,4096]{2,1,0:T(8,128)(2,1)}, u32[]{:S(2)}) copy-start(bf16[1,8,4096]{2,1,0:T(8,128)(2,1)} %param.11) | copy-start | bytes 196612
  136.4 21.5 %all-to-all-start.2 = ((f32[32,8,128]{2,1,0:T(8,128)}), f32[32,8,128]{2,1,0:T(8,128)S(1)}, u32[]{:S(2)}, u32[]{:S(2)}) async-start(f32[32,8,128]{2,1,0:T(8,128)} %mlp.1), calls=%async_computation.2 | async-start | bytes 262144 | tf_op jit(solution)/shard_map/all_to_all | solution.py:170
  157.9 0.7 copy-start.5
  161.8 30.4 %all-to-all-start.4 = ((f32[16,8,128]{2,1,0:T(8,128)}), f32[16,8,128]{2,1,0:T(8,128)S(1)}, u32[]{:S(2)}, u32[]{:S(2)}) async-start(f32[16,8,128]{2,1,0:T(8,128)} %broadcast_in_dim.15), calls=%async_computation.4 | async-start | bytes 131072 | tf_op jit(solution)/shard_map/all_to_all | solution.py:176
  177.7 8.6 %collective-permute-start.10 = (f32[8,128]{1,0:T(8,128)}, f32[8,128]{1,0:T(8,128)S(1)}, u32[]{:S(2)}, u32[]{:S(2)}) collective-permute-start(f32[8,128]{1,0:T(8,128)} %get-tuple-element.7), channel_id=1, source_target_pairs={{0,1},{1,2},{2,3},{3,0},{4,5},{5,6},{6,7},{7,4},{8,9},{9,10},{10,1... | collective-permute-start | bytes 12296 | tf_op jit(solution)/shard_map/ppermute | solution.py:179
  180.0 6.2 %collective-permute-start.11 = (f32[8,128]{1,0:T(8,128)}, f32[8,128]{1,0:T(8,128)S(1)}, u32[]{:S(2)}, u32[]{:S(2)}) collective-permute-start(f32[8,128]{1,0:T(8,128)} %get-tuple-element.7), channel_id=1, source_target_pairs={{0,3},{1,0},{2,1},{3,2},{4,7},{5,4},{6,5},{7,6},{8,11},{9,8},{10,9... | collective-permute-start | bytes 12296 | tf_op jit(solution)/shard_map/ppermute | solution.py:179
  184.2 6.4 %collective-permute-start.12 = (f32[8,128]{1,0:T(8,128)}, f32[8,128]{1,0:T(8,128)S(1)}, u32[]{:S(2)}, u32[]{:S(2)}) collective-permute-start(f32[8,128]{1,0:T(8,128)} %get-tuple-element.7), channel_id=1, source_target_pairs={{0,2},{1,3},{2,0},{3,1},{4,6},{5,7},{6,4},{7,5},{8,10},{9,11},{10,... | collective-permute-start | bytes 12296 | tf_op jit(solution)/shard_map/ppermute | solution.py:179
  192.2 13.9 %copy-start.6 = (f32[16,8,128]{2,1,0:T(8,128)}, f32[16,8,128]{2,1,0:T(8,128)S(1)}, u32[]{:S(2)}) copy-start(f32[16,8,128]{2,1,0:T(8,128)S(1)} %all-to-all-done.4.roll_ref) | copy-start | bytes 196612

commit v6 on v5

--- a/solution.py
+++ b/solution.py
@@ -88,7 +88,7 @@
         )
         mean = jnp.sum(grad * grad) / (RANK * RANK)
         inv = 1.0 / jnp.sqrt(jnp.full((8, RANK), mean + 1e-6))
-        ref[...] = jnp.concatenate([one * inv, right], axis=-1)
+        ref[...] = jnp.broadcast_to(jnp.concatenate([one * inv, right], axis=-1), ref.shape)
 
 
 def score_kernel(train_ref, roll_ref, y_ref, out_ref):
@@ -171,10 +171,13 @@
     small = jax.ShapeDtypeStruct((8, 2 * RANK), jnp.float32)
     vmem, smem = pl.BlockSpec(memory_space=pltpu.VMEM), pl.BlockSpec(memory_space=pltpu.SMEM)
     train, roll = pl.pallas_call(
-        norm_kernel, out_shape=(small, small), in_specs=[vmem, vmem, smem, smem], name="norm"
+        norm_kernel,
+        out_shape=[small, jax.ShapeDtypeStruct((16, 8, 2 * RANK), jnp.float32)],
+        in_specs=[vmem, vmem, smem, smem],
+        name="norm",
     )(parts, right, train_lengths, roll_lengths)
     roll_all = lax.all_to_all(
-        jnp.broadcast_to(roll, (16, 8, 2 * RANK)), ("x", "zh", "co"), 0, 0, tiled=True
+        roll, ("x", "zh", "co"), 0, 0, tiled=True
     )
     near = [train] + [lax.ppermute(train, "y", shift(NY, k)) for k in (1, 3, 2)]
     train_all = lax.all_to_all(

time: 210 us -> 209 us (level)
  transfers between devices with their start and end apart: 17 -> 17, of which waited for: 9 -> 9; matrix products, arithmetic and copies ran while one was open for 7% -> 8% of each run, Pallas kernels for 0% -> 0%
where the time goes in v6:
time: 209 us; the launch traced here: 207 us
  starting transfers between devices  87.1 us (42%)
  waiting for transfers between devices  73.3 us (35%)
  local copies, waits for them, and re-layouts  13.9 us (7%)
  Pallas kernels  13.9 us (7%)
  blocking collectives  13.8 us (7%)
  other arithmetic  2.37 us (1%)
    ppermute x2, waiting for transfers between devices, on_device(): got = lax.ppermute(block, 'zl', [(i, i ^ k) for i in range(NZL)])  19.9 us
    all_to_all x1, starting transfers between devices, on_device(): roll_all = lax.all_to_all(roll, ('x', 'zh', 'co'), 0, 0, tiled=True)  15.8 us
    ppermute x2, waiting for transfers between devices, on_device(): xs += [both, lax.ppermute(both, ('co', 'y'), step2)]  15.3 us
    all_to_all x1, blocking collectives, on_device(): lax.all_to_all(jnp.broadcast_to(jnp.stack(near), (NZL, NY, 8, 2 * RANK)),...  13.8 us
    ppermute x2, starting transfers between devices, on_device(): got = lax.ppermute(block, 'zl', [(i, i ^ k) for i in range(NZL)])  12.7 us
    ppermute x1, starting transfers between devices, on_device(): other = lax.ppermute(w, 'zh', shift(2, 1))  10.6 us
    all_to_all x2, waiting for transfers between devices, over_x(): return lax.all_to_all(spread, 'x', 0, 0, tiled=True)  10.1 us
    all_to_all x1, waiting for transfers between devices, on_device(): parts = lax.all_to_all(parts, ('zl', 'y'), 0, 0, tiled=True)  9.99 us
  transfers between devices with their start and end apart: 17, of which 9 were waited for; matrix products, arithmetic and copies ran while one was open for 8% of the time, Pallas kernels for 0%

profile of v6, /device:TPU:1, one launch (start us, length us, event | category | flops | bytes accessed | tf_op | source)
XLA Modules:
  0.0 206.9 jit_solution(3107834958976213610)
XLA Ops:
  0.0 0.0 copy-start
  0.0 0.9 pad_maximum_fusion.2
  0.9 9.6 %collective-permute-start = (bf16[16,4096]{1,0:T(8,128)(2,1)S(1)}, bf16[16,4096]{1,0:T(8,128)(2,1)S(1)}, u32[]{:S(2)}, u32[]{:S(2)}) collective-permute-start(bf16[16,4096]{1,0:T(8,128)(2,1)S(1)} %pad_maximum_fusion.2), channel_id=1, source_target_pairs={{0,16},{4,20},{8,24},{12,28},{16,0},{20,4},{24,8},{28,12},{1,17},{... | collective-permute-start | bytes 393224 | tf_op jit(solution)/shard_map/ppermute | solution.py:138
  10.6 1.0 constant_dynamic-update-slice_fusion.8
  11.6 1.0 constant_dynamic-update-slice_fusion.7
  12.5 10.6 %collective-permute-start.8 = (bf16[256,896]{0,1:T(8,128)(2,1)S(1)}, bf16[256,896]{0,1:T(8,128)(2,1)}, u32[]{:S(2)}, u32[]{:S(2)}) collective-permute-start(bf16[256,896]{0,1:T(8,128)(2,1)S(1)} %constant_dynamic-update-slice_fusion.7), channel_id=1, source_target_pairs={{0,64},{64,0},{1,65},{65,1},{2,66},{66,2},{3,67},{67,3},{4,68},{68... | collective-permute-start | bytes 1376264 | tf_op jit(solution)/shard_map/ppermute | solution.py:134
  23.2 0.2 copy.11
  23.4 1.4 broadcast_in_dim.9
  24.8 4.1 %all-to-all-start = ((bf16[4,256,896]{2,1,0:T(8,128)(2,1)}), bf16[4,256,896]{2,1,0:T(8,128)(2,1)S(1)}, u32[]{:S(2)}, u32[]{:S(2)}) async-start(bf16[4,256,896]{2,1,0:T(8,128)(2,1)} %broadcast_in_dim.9), calls=%async_computation | async-start | bytes 3670016 | tf_op jit(solution)/shard_map/all_to_all | solution.py:157
  29.0 0.0 copy-done.3
  29.0 0.6 constant_dynamic-update-slice_fusion.4
  29.6 0.0 collective-permute-done
  29.6 0.0 copy-done.4
  29.6 0.7 pad_maximum_fusion.1
  30.3 3.1 %collective-permute-start.1 = (bf16[32,4096]{1,0:T(8,128)(2,1)}, bf16[32,4096]{1,0:T(8,128)(2,1)S(1)}, u32[]{:S(2)}, u32[]{:S(2)}) collective-permute-start(bf16[32,4096]{1,0:T(8,128)(2,1)} %pad_maximum_fusion.1), channel_id=1, source_target_pairs={{0,8},{4,12},{8,0},{12,4},{16,24},{20,28},{24,16},{28,20},{1,9},{5... | collective-permute-start | bytes 786440 | tf_op jit(solution)/shard_map/ppermute | solution.py:138
  33.4 0.6 constant_dynamic-update-slice_fusion.3
  34.0 5.6 %collective-permute-done.8 = bf16[256,896]{0,1:T(8,128)(2,1)} collective-permute-done((bf16[256,896]{0,1:T(8,128)(2,1)S(1)}, bf16[256,896]{0,1:T(8,128)(2,1)}, u32[]{:S(2)}, u32[]{:S(2)}) %collective-permute-start.8) | collective-permute-done | bytes 458784 | tf_op jit(solution)/shard_map/ppermute | solution.py:134
  39.6 1.3 copy.12
  40.9 10.1 %all-to-all-done.refs_4_ = bf16[4,256,896]{2,1,0:T(8,128)(2,1)S(1)} async-done(((bf16[4,256,896]{2,1,0:T(8,128)(2,1)}), bf16[4,256,896]{2,1,0:T(8,128)(2,1)S(1)}, u32[]{:S(2)}, u32[]{:S(2)}) %all-to-all-start) | async-done | bytes 1835040 | tf_op jit(solution)/shard_map/all_to_all | solution.py:157
  51.0 1.5 broadcast_in_dim.10
  52.5 4.4 %all-to-all-start.1 = ((bf16[4,256,896]{2,1,0:T(8,128)(2,1)}), bf16[4,256,896]{2,1,0:T(8,128)(2,1)}, u32[]{:S(2)}, u32[]{:S(2)}) async-start(bf16[4,256,896]{2,1,0:T(8,128)(2,1)} %broadcast_in_dim.10), calls=%async_computation.1 | async-start | bytes 3670016 | tf_op jit(solution)/shard_map/all_to_all | solution.py:157
  56.9 19.9 %collective-permute-done.1 = bf16[32,4096]{1,0:T(8,128)(2,1)S(1)} collective-permute-done((bf16[32,4096]{1,0:T(8,128)(2,1)}, bf16[32,4096]{1,0:T(8,128)(2,1)S(1)}, u32[]{:S(2)}, u32[]{:S(2)}) %collective-permute-start.1) | collective-permute-done | bytes 262176 | tf_op jit(solution)/shard_map/ppermute | solution.py:138
  76.8 1.9 collective-permute-start.4
  78.7 4.6 %collective-permute-start.2 = (bf16[64,4096]{1,0:T(8,128)(2,1)S(1)}, bf16[64,4096]{1,0:T(8,128)(2,1)S(1)}, u32[]{:S(2)}, u32[]{:S(2)}) collective-permute-start(bf16[64,4096]{1,0:T(8,128)(2,1)S(1)} %pad_maximum_fusion), channel_id=1, source_target_pairs={{0,1},{1,0},{2,3},{3,2},{32,35},{33,34},{34,33},{35,32},{4,5},{5,4... | collective-permute-start | bytes 1572872 | tf_op jit(solution)/shard_map/ppermute | solution.py:150
  83.4 0.7 constant_dynamic-update-slice_fusion.2
  84.1 0.7 constant_dynamic-update-slice_fusion.1
  84.8 7.1 %collective-permute-done.4 = bf16[64,4096]{1,0:T(8,128)(2,1)} collective-permute-done((bf16[64,4096]{1,0:T(8,128)(2,1)S(1)}, bf16[64,4096]{1,0:T(8,128)(2,1)}, u32[]{:S(2)}, u32[]{:S(2)}) %collective-permute-start.4) | collective-permute-done | bytes 524320 | tf_op jit(solution)/shard_map/ppermute | solution.py:140
  91.9 4.6 %collective-permute-start.5 = (bf16[64,4096]{1,0:T(8,128)(2,1)}, bf16[64,4096]{1,0:T(8,128)(2,1)}, u32[]{:S(2)}, u32[]{:S(2)}) collective-permute-start(bf16[64,4096]{1,0:T(8,128)(2,1)} %collective-permute-done.4), channel_id=1, source_target_pairs={{0,1},{1,0},{2,3},{3,2},{32,35},{33,34},{34,33},{35,32},{4,5},{5,4... | collective-permute-start | bytes 1572872 | tf_op jit(solution)/shard_map/ppermute | solution.py:150
  96.6 0.0 collective-permute-done.2
  96.6 0.8 constant_dynamic-update-slice_fusion.refs_0_
  97.4 1.9 collective-permute-start.3
  99.3 0.0 copy-done.1
  99.3 4.1 %collective-permute-start.7 = (bf16[4,256,896]{2,1,0:T(8,128)(2,1)S(1)}, bf16[4,256,896]{2,1,0:T(8,128)(2,1)}, u32[]{:S(2)}, u32[]{:S(2)}) collective-permute-start(bf16[4,256,896]{2,1,0:T(8,128)(2,1)S(1)} %all-to-all-done.refs_4_), channel_id=1, source_target_pairs={{0,32},{32,0},{1,33},{33,1},{2,34},{34,2},{3,35},{35,3},{4,36},{36... | collective-permute-start | bytes 5505032 | tf_op jit(solution)/shard_map/ppermute | solution.py:162
  103.5 0.0 all-to-all-done.1.refs_6_
  103.5 1.9 collective-permute-start.9
  105.4 1.1 constant_dynamic-update-slice_fusion.6
  106.5 0.0 collective-permute-done.5
  106.5 1.1 constant_dynamic-update-slice_fusion.5.refs_2_
  107.6 2.3 %collective-permute-start.6 = (bf16[128,4096]{1,0:T(8,128)(2,1)S(1)}, bf16[128,4096]{1,0:T(8,128)(2,1)}, u32[]{:S(2)}, u32[]{:S(2)}) collective-permute-start(bf16[128,4096]{1,0:T(8,128)(2,1)S(1)} %constant_dynamic-update-slice_fusion.5.refs_2_), channel_id=1, source_target_pairs={{0,3},{1,2},{2,1},{3,0},{32,33},{33,32},{34,35},{35,34},{4,7},{5,6... | collective-permute-start | bytes 3145736 | tf_op jit(solution)/shard_map/ppermute | solution.py:152
  110.0 0.6 stack.181.cols_ref
  110.6 0.6 stack.214.slot_ref
  111.3 4.0 %collective-permute-done.3.refs_1_ = bf16[128,4096]{1,0:T(8,128)(2,1)} collective-permute-done((bf16[128,4096]{1,0:T(8,128)(2,1)}, bf16[128,4096]{1,0:T(8,128)(2,1)}, u32[]{:S(2)}, u32[]{:S(2)}) %collective-permute-start.3) | collective-permute-done | bytes 1048608 | tf_op jit(solution)/shard_map/ppermute | solution.py:152
  115.3 11.3 %collective-permute-done.6.refs_3_ = bf16[128,4096]{1,0:T(8,128)(2,1)} collective-permute-done((bf16[128,4096]{1,0:T(8,128)(2,1)S(1)}, bf16[128,4096]{1,0:T(8,128)(2,1)}, u32[]{:S(2)}, u32[]{:S(2)}) %collective-permute-start.6) | collective-permute-done | bytes 1048608 | tf_op jit(solution)/shard_map/ppermute | solution.py:152
  126.6 0.0 collective-permute-done.7.refs_5_
  126.6 0.0 collective-permute-done.9.refs_7_
  126.6 0.0 copy-start.7
  126.6 0.0 copy-start.8
  126.7 9.7 %mlp.1 = f32[32,8,128]{2,1,0:T(8,128)} custom-call(s32[16]{0:T(128)} %stack.181.cols_ref, s32[32]{0:T(128)} %stack.214.slot_ref, bf16[128,4096]{1,0:T(8,128)(2,1)} %constant_dynamic-update-slice_fusion.refs_0_, bf16[128,4096]{1,0:T(8,128)(2,1)} %collective-permute-done.3.refs_1_, bf16[128,4096]{1,0:T(8,128)(2,1)} %copy-done.2, ...), custom_call_target="tpu_custom_call" | custom-call | tf_op jit(solution)/shard_map/mlp/pallas_call | solution.py:63
  136.4 9.3 %all-to-all-start.2 = ((f32[32,8,128]{2,1,0:T(8,128)}), f32[32,8,128]{2,1,0:T(8,128)S(1)}, u32[]{:S(2)}, u32[]{:S(2)}) async-start(f32[32,8,128]{2,1,0:T(8,128)} %mlp.1), calls=%async_computation.2 | async-start | bytes 262144 | tf_op jit(solution)/shard_map/all_to_all | solution.py:170
  147.0 0.9 convolution_bitcast_fusion.right_ref
  147.9 10.0 %all-to-all-done.2.parts_ref = f32[32,8,128]{2,1,0:T(8,128)S(1)} async-done(((f32[32,8,128]{2,1,0:T(8,128)}), f32[32,8,128]{2,1,0:T(8,128)S(1)}, u32[]{:S(2)}, u32[]{:S(2)}) %all-to-all-start.2) | async-done | bytes 131104 | tf_op jit(solution)/shard_map/all_to_all | solution.py:170
  157.9 0.6 copy-done.5
  158.5 2.1 %norm.1 = (f32[8,128]{1,0:T(8,128)}, f32[16,8,128]{2,1,0:T(8,128)}) custom-call(f32[32,8,128]{2,1,0:T(8,128)} %copy-done.5, f32[2,8,64]{2,1,0:T(8,128)} %convolution_bitcast_fusion.right_ref, s32[1]{0:T(128)S(6)} %copy.19.train_len_ref, s32[1]{0:T(128)S(6)} %copy.20.roll_len_ref), custom_call_target="tpu_custom_call" | custom-call | tf_op jit(solution)/shard_map/norm/pallas_call | solution.py:173
  160.6 15.8 %all-to-all-start.4 = ((f32[16,8,128]{2,1,0:T(8,128)}), f32[16,8,128]{2,1,0:T(8,128)S(1)}, u32[]{:S(2)}, u32[]{:S(2)}) async-start(f32[16,8,128]{2,1,0:T(8,128)} %get-tuple-element.8), calls=%async_computation.4 | async-start | bytes 131072 | tf_op jit(solution)/shard_map/all_to_all | solution.py:179
  176.4 2.3 %collective-permute-start.10 = (f32[8,128]{1,0:T(8,128)}, f32[8,128]{1,0:T(8,128)S(1)}, u32[]{:S(2)}, u32[]{:S(2)}) collective-permute-start(f32[8,128]{1,0:T(8,128)} %get-tuple-element.7), channel_id=1, source_target_pairs={{0,1},{1,2},{2,3},{3,0},{4,5},{5,6},{6,7},{7,4},{8,9},{9,10},{10,1... | collective-permute-start | bytes 12296 | tf_op jit(solution)/shard_map/ppermute | solution.py:182
  178.8 4.2 %collective-permute-start.11 = (f32[8,128]{1,0:T(8,128)}, f32[8,128]{1,0:T(8,128)S(1)}, u32[]{:S(2)}, u32[]{:S(2)}) collective-permute-start(f32[8,128]{1,0:T(8,128)} %get-tuple-element.7), channel_id=1, source_target_pairs={{0,3},{1,0},{2,1},{3,2},{4,7},{5,4},{6,5},{7,6},{8,11},{9,8},{10,9... | collective-permute-start | bytes 12296 | tf_op jit(solution)/shard_map/ppermute | solution.py:182
  183.0 2.0 collective-permute-start.12
  185.0 0.0 collective-permute-done.10
  185.0 0.0 collective-permute-done.11
  185.0 4.3 %collective-permute-done.12 = f32[8,128]{1,0:T(8,128)S(1)} collective-permute-done((f32[8,128]{1,0:T(8,128)}, f32[8,128]{1,0:T(8,128)S(1)}, u32[]{:S(2)}, u32[]{:S(2)}) %collective-permute-start.12) | collective-permute-done | bytes 4128 | tf_op jit(solution)/shard_map/ppermute | solution.py:182
  189.3 0.7 pad_maximum_fusion.3
  190.0 1.0 all-to-all-done.4.roll_ref
  191.0 13.8 %all_to_all.25.train_ref = f32[8,4,8,128]{3,2,1,0:T(8,128)} all-to-all(f32[8,4,8,128]{3,2,1,0:T(8,128)S(1)} %broadcast_in_dim.11), channel_id=1, replica_groups=mesh['x'=4,'zh'=2,'co'=2,'zl'=8,'y'=4] {'zl'}, dimensions={0} | all-to-all | bytes 262144 | tf_op jit(solution)/shard_map/all_to_all | solution.py:183
  204.8 2.1 %score.1 = f32[16,32]{1,0:T(8,128)} custom-call(f32[8,4,8,128]{3,2,1,0:T(8,128)} %all_to_all.25.train_ref, f32[16,8,128]{2,1,0:T(8,128)} %copy-done.6, s32[1]{0:T(128)} %bitcast.58.y_ref), custom_call_target="tpu_custom_call" | custom-call | tf_op jit(solution)/shard_map/score/pallas_call | solution.py:186
  (13 shorter events, 0.1 us)
Async XLA Ops:
  0.0 147.0 %copy-start = (bf16[4096,64]{0,1:T(8,128)(2,1)S(1)}, bf16[4096,64]{0,1:T(8,128)(2,1)}, u32[]{:S(2)}) copy-start(bf16[4096,64]{0,1:T(8,128)(2,1)} %param.19) | copy-start | bytes 1572868
  0.9 28.7 %collective-permute-start = (bf16[16,4096]{1,0:T(8,128)(2,1)S(1)}, bf16[16,4096]{1,0:T(8,128)(2,1)S(1)}, u32[]{:S(2)}, u32[]{:S(2)}) collective-permute-start(bf16[16,4096]{1,0:T(8,128)(2,1)S(1)} %pad_maximum_fusion.2), channel_id=1, source_target_pairs={{0,16},{4,20},{8,24},{12,28},{16,0},{20,4},{24,8},{28,12},{1,17},{... | collective-permute-start | bytes 393224 | tf_op jit(solution)/shard_map/ppermute | solution.py:138
  12.5 27.1 %collective-permute-start.8 = (bf16[256,896]{0,1:T(8,128)(2,1)S(1)}, bf16[256,896]{0,1:T(8,128)(2,1)}, u32[]{:S(2)}, u32[]{:S(2)}) collective-permute-start(bf16[256,896]{0,1:T(8,128)(2,1)S(1)} %constant_dynamic-update-slice_fusion.7), channel_id=1, source_target_pairs={{0,64},{64,0},{1,65},{65,1},{2,66},{66,2},{3,67},{67,3},{4,68},{68... | collective-permute-start | bytes 1376264 | tf_op jit(solution)/shard_map/ppermute | solution.py:134
  24.8 4.2 %copy-start.3 = (bf16[1,8,4096]{2,1,0:T(8,128)(2,1)S(1)}, bf16[1,8,4096]{2,1,0:T(8,128)(2,1)}, u32[]{:S(2)}) copy-start(bf16[1,8,4096]{2,1,0:T(8,128)(2,1)} %param.10) | copy-start | bytes 196612
  24.8 4.8 %copy-start.4 = (bf16[1,8,4096]{2,1,0:T(8,128)(2,1)S(1)}, bf16[1,8,4096]{2,1,0:T(8,128)(2,1)}, u32[]{:S(2)}) copy-start(bf16[1,8,4096]{2,1,0:T(8,128)(2,1)} %param.13) | copy-start | bytes 196612
  24.8 26.2 %all-to-all-start = ((bf16[4,256,896]{2,1,0:T(8,128)(2,1)}), bf16[4,256,896]{2,1,0:T(8,128)(2,1)S(1)}, u32[]{:S(2)}, u32[]{:S(2)}) async-start(bf16[4,256,896]{2,1,0:T(8,128)(2,1)} %broadcast_in_dim.9), calls=%async_computation | async-start | bytes 3670016 | tf_op jit(solution)/shard_map/all_to_all | solution.py:157
  30.3 46.5 %collective-permute-start.1 = (bf16[32,4096]{1,0:T(8,128)(2,1)}, bf16[32,4096]{1,0:T(8,128)(2,1)S(1)}, u32[]{:S(2)}, u32[]{:S(2)}) collective-permute-start(bf16[32,4096]{1,0:T(8,128)(2,1)} %pad_maximum_fusion.1), channel_id=1, source_target_pairs={{0,8},{4,12},{8,0},{12,4},{16,24},{20,28},{24,16},{28,20},{1,9},{5... | collective-permute-start | bytes 786440 | tf_op jit(solution)/shard_map/ppermute | solution.py:138
  51.0 48.3 %copy-start.1 = (bf16[4,256,896]{2,1,0:T(8,128)(2,1)}, bf16[4,256,896]{2,1,0:T(8,128)(2,1)S(1)}, u32[]{:S(2)}) copy-start(bf16[4,256,896]{2,1,0:T(8,128)(2,1)S(1)} %all-to-all-done.refs_4_) | copy-start | bytes 5505028
  52.5 51.0 %all-to-all-start.1 = ((bf16[4,256,896]{2,1,0:T(8,128)(2,1)}), bf16[4,256,896]{2,1,0:T(8,128)(2,1)}, u32[]{:S(2)}, u32[]{:S(2)}) async-start(bf16[4,256,896]{2,1,0:T(8,128)(2,1)} %broadcast_in_dim.10), calls=%async_computation.1 | async-start | bytes 3670016 | tf_op jit(solution)/shard_map/all_to_all | solution.py:157
  76.8 15.1 %collective-permute-start.4 = (bf16[64,4096]{1,0:T(8,128)(2,1)S(1)}, bf16[64,4096]{1,0:T(8,128)(2,1)}, u32[]{:S(2)}, u32[]{:S(2)}) collective-permute-start(bf16[64,4096]{1,0:T(8,128)(2,1)S(1)} %pad_maximum_fusion), channel_id=1, source_target_pairs={{0,4},{4,0},{8,12},{12,8},{16,20},{20,16},{24,28},{28,24},{1,5},{5... | collective-permute-start | bytes 1572872 | tf_op jit(solution)/shard_map/ppermute | solution.py:140
  78.7 17.8 %collective-permute-start.2 = (bf16[64,4096]{1,0:T(8,128)(2,1)S(1)}, bf16[64,4096]{1,0:T(8,128)(2,1)S(1)}, u32[]{:S(2)}, u32[]{:S(2)}) collective-permute-start(bf16[64,4096]{1,0:T(8,128)(2,1)S(1)} %pad_maximum_fusion), channel_id=1, source_target_pairs={{0,1},{1,0},{2,3},{3,2},{32,35},{33,34},{34,33},{35,32},{4,5},{5,4... | collective-permute-start | bytes 1572872 | tf_op jit(solution)/shard_map/ppermute | solution.py:150
  91.9 14.6 %collective-permute-start.5 = (bf16[64,4096]{1,0:T(8,128)(2,1)}, bf16[64,4096]{1,0:T(8,128)(2,1)}, u32[]{:S(2)}, u32[]{:S(2)}) collective-permute-start(bf16[64,4096]{1,0:T(8,128)(2,1)} %collective-permute-done.4), channel_id=1, source_target_pairs={{0,1},{1,0},{2,3},{3,2},{32,35},{33,34},{34,33},{35,32},{4,5},{5,4... | collective-permute-start | bytes 1572872 | tf_op jit(solution)/shard_map/ppermute | solution.py:150
  97.4 17.9 %collective-permute-start.3 = (bf16[128,4096]{1,0:T(8,128)(2,1)}, bf16[128,4096]{1,0:T(8,128)(2,1)}, u32[]{:S(2)}, u32[]{:S(2)}) collective-permute-start(bf16[128,4096]{1,0:T(8,128)(2,1)} %constant_dynamic-update-slice_fusion.refs_0_), channel_id=1, source_target_pairs={{0,3},{1,2},{2,1},{3,0},{32,33},{33,32},{34,35},{35,34},{4,7},{5,6... | collective-permute-start | bytes 3145736 | tf_op jit(solution)/shard_map/ppermute | solution.py:152
  99.3 27.3 %collective-permute-start.7 = (bf16[4,256,896]{2,1,0:T(8,128)(2,1)S(1)}, bf16[4,256,896]{2,1,0:T(8,128)(2,1)}, u32[]{:S(2)}, u32[]{:S(2)}) collective-permute-start(bf16[4,256,896]{2,1,0:T(8,128)(2,1)S(1)} %all-to-all-done.refs_4_), channel_id=1, source_target_pairs={{0,32},{32,0},{1,33},{33,1},{2,34},{34,2},{3,35},{35,3},{4,36},{36... | collective-permute-start | bytes 5505032 | tf_op jit(solution)/shard_map/ppermute | solution.py:162
  103.5 23.1 %collective-permute-start.9 = (bf16[4,256,896]{2,1,0:T(8,128)(2,1)}, bf16[4,256,896]{2,1,0:T(8,128)(2,1)}, u32[]{:S(2)}, u32[]{:S(2)}) collective-permute-start(bf16[4,256,896]{2,1,0:T(8,128)(2,1)} %all-to-all-done.1.refs_6_), channel_id=1, source_target_pairs={{0,32},{32,0},{1,33},{33,1},{2,34},{34,2},{3,35},{35,3},{4,36},{36... | collective-permute-start | bytes 5505032 | tf_op jit(solution)/shard_map/ppermute | solution.py:162
  107.6 19.0 %copy-start.2 = (bf16[128,4096]{1,0:T(8,128)(2,1)}, bf16[128,4096]{1,0:T(8,128)(2,1)S(1)}, u32[]{:S(2)}) copy-start(bf16[128,4096]{1,0:T(8,128)(2,1)S(1)} %constant_dynamic-update-slice_fusion.5.refs_2_) | copy-start | bytes 3145732
  107.6 19.0 %collective-permute-start.6 = (bf16[128,4096]{1,0:T(8,128)(2,1)S(1)}, bf16[128,4096]{1,0:T(8,128)(2,1)}, u32[]{:S(2)}, u32[]{:S(2)}) collective-permute-start(bf16[128,4096]{1,0:T(8,128)(2,1)S(1)} %constant_dynamic-update-slice_fusion.5.refs_2_), channel_id=1, source_target_pairs={{0,3},{1,2},{2,1},{3,0},{32,33},{33,32},{34,35},{35,34},{4,7},{5,6... | collective-permute-start | bytes 3145736 | tf_op jit(solution)/shard_map/ppermute | solution.py:152
  126.6 20.4 %copy-start.7 = (bf16[1,8,4096]{2,1,0:T(8,128)(2,1)S(1)}, bf16[1,8,4096]{2,1,0:T(8,128)(2,1)}, u32[]{:S(2)}) copy-start(bf16[1,8,4096]{2,1,0:T(8,128)(2,1)} %param.14) | copy-start | bytes 196612
  126.6 20.4 %copy-start.8 = (bf16[1,8,4096]{2,1,0:T(8,128)(2,1)S(1)}, bf16[1,8,4096]{2,1,0:T(8,128)(2,1)}, u32[]{:S(2)}) copy-start(bf16[1,8,4096]{2,1,0:T(8,128)(2,1)} %param.11) | copy-start | bytes 196612
  136.4 21.5 %all-to-all-start.2 = ((f32[32,8,128]{2,1,0:T(8,128)}), f32[32,8,128]{2,1,0:T(8,128)S(1)}, u32[]{:S(2)}, u32[]{:S(2)}) async-start(f32[32,8,128]{2,1,0:T(8,128)} %mlp.1), calls=%async_computation.2 | async-start | bytes 262144 | tf_op jit(solution)/shard_map/all_to_all | solution.py:170
  157.9 0.7 copy-start.5
  160.6 30.4 %all-to-all-start.4 = ((f32[16,8,128]{2,1,0:T(8,128)}), f32[16,8,128]{2,1,0:T(8,128)S(1)}, u32[]{:S(2)}, u32[]{:S(2)}) async-start(f32[16,8,128]{2,1,0:T(8,128)} %get-tuple-element.8), calls=%async_computation.4 | async-start | bytes 131072 | tf_op jit(solution)/shard_map/all_to_all | solution.py:179
  176.4 8.6 %collective-permute-start.10 = (f32[8,128]{1,0:T(8,128)}, f32[8,128]{1,0:T(8,128)S(1)}, u32[]{:S(2)}, u32[]{:S(2)}) collective-permute-start(f32[8,128]{1,0:T(8,128)} %get-tuple-element.7), channel_id=1, source_target_pairs={{0,1},{1,2},{2,3},{3,0},{4,5},{5,6},{6,7},{7,4},{8,9},{9,10},{10,1... | collective-permute-start | bytes 12296 | tf_op jit(solution)/shard_map/ppermute | solution.py:182
  178.8 6.2 %collective-permute-start.11 = (f32[8,128]{1,0:T(8,128)}, f32[8,128]{1,0:T(8,128)S(1)}, u32[]{:S(2)}, u32[]{:S(2)}) collective-permute-start(f32[8,128]{1,0:T(8,128)} %get-tuple-element.7), channel_id=1, source_target_pairs={{0,3},{1,0},{2,1},{3,2},{4,7},{5,4},{6,5},{7,6},{8,11},{9,8},{10,9... | collective-permute-start | bytes 12296 | tf_op jit(solution)/shard_map/ppermute | solution.py:182
  183.0 6.4 %collective-permute-start.12 = (f32[8,128]{1,0:T(8,128)}, f32[8,128]{1,0:T(8,128)S(1)}, u32[]{:S(2)}, u32[]{:S(2)}) collective-permute-start(f32[8,128]{1,0:T(8,128)} %get-tuple-element.7), channel_id=1, source_target_pairs={{0,2},{1,3},{2,0},{3,1},{4,6},{5,7},{6,4},{7,5},{8,10},{9,11},{10,... | collective-permute-start | bytes 12296 | tf_op jit(solution)/shard_map/ppermute | solution.py:182
  191.0 13.9 %copy-start.6 = (f32[16,8,128]{2,1,0:T(8,128)}, f32[16,8,128]{2,1,0:T(8,128)S(1)}, u32[]{:S(2)}) copy-start(f32[16,8,128]{2,1,0:T(8,128)S(1)} %all-to-all-done.4.roll_ref) | copy-start | bytes 196612

commit v7 on v6

--- a/solution.py
+++ b/solution.py
@@ -16,32 +16,35 @@
     x_refs = refs[:nx]
     w_refs = refs[nx : nx + nw]
     ip_ref, out_ref, xv, wv, acc, xsem, wsem = refs[nx + nw :]
-    half_k = xv.shape[1] // 2
-    xcopies, wcopies = [[], []], [[], []]
-    for h in range(2):
-        at = 0
+    part_k = xv.shape[1] // 4
+    groups = []
+    for h in range(4):
+        at, copies = 0, []
         for i, x_ref in enumerate(x_refs):
             n = x_ref.shape[0]
-            cut = pl.ds(h * half_k, half_k)
-            xcopies[h].append(
+            cut = pl.ds(h * part_k, part_k)
+            copies.append(
                 pltpu.make_async_copy(x_ref.at[:, cut], xv.at[pl.ds(at, n), cut], xsem.at[h * nx + i])
             )
             at += n
-    for p in range(nw):
-        for j in range(4):
-            row = pl.multiple_of(cols_ref[p * 4 + j], 256)
-            wcopies[j // 2].append(
-                pltpu.make_async_copy(w_refs[p].at[j], wv.at[pl.ds(row, 256)], wsem.at[p * 4 + j])
+        for p in range(nw):
+            row = pl.multiple_of(cols_ref[p * 4 + h], 256)
+            copies.append(
+                pltpu.make_async_copy(w_refs[p].at[h], wv.at[pl.ds(row, 256)], wsem.at[p * 4 + h])
             )
-    for h in range(2):
-        for c in xcopies[h] + wcopies[h]:
+        groups.append(copies)
+    for copies in groups:
+        for c in copies:
             c.start()
-    for c in xcopies[0] + wcopies[0]:
-        c.wait()
-    acc[...] = jnp.dot(xv[:, :half_k], wv[:half_k], preferred_element_type=jnp.float32)
-    for c in xcopies[1] + wcopies[1]:
-        c.wait()
-    acc[...] += jnp.dot(xv[:, half_k:], wv[half_k:], preferred_element_type=jnp.float32)
+    for h, copies in enumerate(groups):
+        for c in copies:
+            c.wait()
+        k = slice(h * part_k, (h + 1) * part_k)
+        part = jnp.dot(xv[:, k], wv[k], preferred_element_type=jnp.float32)
+        if h:
+            acc[...] += part
+        else:
+            acc[...] = part
     half = acc.shape[1] // 2
     for m in range(4):
         both = acc[m * 128 : (m + 1) * 128]
@@ -69,7 +72,7 @@
             pltpu.VMEM((512, xs[0].shape[1]), jnp.bfloat16),
             pltpu.VMEM((4096, ws[0].shape[2]), jnp.bfloat16),
             pltpu.VMEM((512, ws[0].shape[2]), jnp.float32),
-            pltpu.SemaphoreType.DMA((2 * nx,)),
+            pltpu.SemaphoreType.DMA((4 * nx,)),
             pltpu.SemaphoreType.DMA((4 * nw,)),
         ],
         compiler_params=pltpu.CompilerParams(vmem_limit_bytes=60 << 20),

time: 209 us -> 208 us (level)
  no operation moved by 1% of the time
where the time goes in v7:
time: 208 us; the launch traced here: 206 us
  starting transfers between devices  87.1 us (42%)
  waiting for transfers between devices  73.3 us (35%)
  local copies, waits for them, and re-layouts  13.9 us (7%)
  blocking collectives  13.8 us (7%)
  Pallas kernels  12.9 us (6%)
  other arithmetic  2.37 us (1%)
    ppermute x2, waiting for transfers between devices, on_device(): got = lax.ppermute(block, 'zl', [(i, i ^ k) for i in range(NZL)])  19.9 us
    all_to_all x1, starting transfers between devices, on_device(): roll_all = lax.all_to_all(roll, ('x', 'zh', 'co'), 0, 0, tiled=True)  15.8 us
    ppermute x2, waiting for transfers between devices, on_device(): xs += [both, lax.ppermute(both, ('co', 'y'), step2)]  15.3 us
    all_to_all x1, blocking collectives, on_device(): lax.all_to_all(jnp.broadcast_to(jnp.stack(near), (NZL, NY, 8, 2 * RANK)),...  13.8 us
    ppermute x2, starting transfers between devices, on_device(): got = lax.ppermute(block, 'zl', [(i, i ^ k) for i in range(NZL)])  12.7 us
    ppermute x1, starting transfers between devices, on_device(): other = lax.ppermute(w, 'zh', shift(2, 1))  10.6 us
    all_to_all x2, waiting for transfers between devices, over_x(): return lax.all_to_all(spread, 'x', 0, 0, tiled=True)  10.1 us
    all_to_all x1, waiting for transfers between devices, on_device(): parts = lax.all_to_all(parts, ('zl', 'y'), 0, 0, tiled=True)  9.99 us
  transfers between devices with their start and end apart: 17, of which 9 were waited for; matrix products, arithmetic and copies ran while one was open for 8% of the time, Pallas kernels for 0%

profile of v7, /device:TPU:1, one launch (start us, length us, event | category | flops | bytes accessed | tf_op | source)
XLA Modules:
  0.0 205.9 jit_solution(5466604671065931052)
XLA Ops:
  0.0 0.0 copy-start
  0.0 0.9 pad_maximum_fusion.2
  0.9 9.6 %collective-permute-start = (bf16[16,4096]{1,0:T(8,128)(2,1)S(1)}, bf16[16,4096]{1,0:T(8,128)(2,1)S(1)}, u32[]{:S(2)}, u32[]{:S(2)}) collective-permute-start(bf16[16,4096]{1,0:T(8,128)(2,1)S(1)} %pad_maximum_fusion.2), channel_id=1, source_target_pairs={{0,16},{4,20},{8,24},{12,28},{16,0},{20,4},{24,8},{28,12},{1,17},{... | collective-permute-start | bytes 393224 | tf_op jit(solution)/shard_map/ppermute | solution.py:141
  10.6 1.0 constant_dynamic-update-slice_fusion.8
  11.6 1.0 constant_dynamic-update-slice_fusion.7
  12.5 10.6 %collective-permute-start.8 = (bf16[256,896]{0,1:T(8,128)(2,1)S(1)}, bf16[256,896]{0,1:T(8,128)(2,1)}, u32[]{:S(2)}, u32[]{:S(2)}) collective-permute-start(bf16[256,896]{0,1:T(8,128)(2,1)S(1)} %constant_dynamic-update-slice_fusion.7), channel_id=1, source_target_pairs={{0,64},{64,0},{1,65},{65,1},{2,66},{66,2},{3,67},{67,3},{4,68},{68... | collective-permute-start | bytes 1376264 | tf_op jit(solution)/shard_map/ppermute | solution.py:137
  23.2 0.2 copy.11
  23.4 1.4 broadcast_in_dim.9
  24.8 4.1 %all-to-all-start = ((bf16[4,256,896]{2,1,0:T(8,128)(2,1)}), bf16[4,256,896]{2,1,0:T(8,128)(2,1)S(1)}, u32[]{:S(2)}, u32[]{:S(2)}) async-start(bf16[4,256,896]{2,1,0:T(8,128)(2,1)} %broadcast_in_dim.9), calls=%async_computation | async-start | bytes 3670016 | tf_op jit(solution)/shard_map/all_to_all | solution.py:160
  29.0 0.0 copy-done.3
  29.0 0.6 constant_dynamic-update-slice_fusion.4
  29.6 0.0 collective-permute-done
  29.6 0.0 copy-done.4
  29.6 0.7 pad_maximum_fusion.1
  30.3 3.1 %collective-permute-start.1 = (bf16[32,4096]{1,0:T(8,128)(2,1)}, bf16[32,4096]{1,0:T(8,128)(2,1)S(1)}, u32[]{:S(2)}, u32[]{:S(2)}) collective-permute-start(bf16[32,4096]{1,0:T(8,128)(2,1)} %pad_maximum_fusion.1), channel_id=1, source_target_pairs={{0,8},{4,12},{8,0},{12,4},{16,24},{20,28},{24,16},{28,20},{1,9},{5... | collective-permute-start | bytes 786440 | tf_op jit(solution)/shard_map/ppermute | solution.py:141
  33.4 0.6 constant_dynamic-update-slice_fusion.3
  34.0 5.6 %collective-permute-done.8 = bf16[256,896]{0,1:T(8,128)(2,1)} collective-permute-done((bf16[256,896]{0,1:T(8,128)(2,1)S(1)}, bf16[256,896]{0,1:T(8,128)(2,1)}, u32[]{:S(2)}, u32[]{:S(2)}) %collective-permute-start.8) | collective-permute-done | bytes 458784 | tf_op jit(solution)/shard_map/ppermute | solution.py:137
  39.6 1.3 copy.12
  40.9 10.1 %all-to-all-done.refs_4_ = bf16[4,256,896]{2,1,0:T(8,128)(2,1)S(1)} async-done(((bf16[4,256,896]{2,1,0:T(8,128)(2,1)}), bf16[4,256,896]{2,1,0:T(8,128)(2,1)S(1)}, u32[]{:S(2)}, u32[]{:S(2)}) %all-to-all-start) | async-done | bytes 1835040 | tf_op jit(solution)/shard_map/all_to_all | solution.py:160
  51.0 1.5 broadcast_in_dim.10
  52.5 4.4 %all-to-all-start.1 = ((bf16[4,256,896]{2,1,0:T(8,128)(2,1)}), bf16[4,256,896]{2,1,0:T(8,128)(2,1)}, u32[]{:S(2)}, u32[]{:S(2)}) async-start(bf16[4,256,896]{2,1,0:T(8,128)(2,1)} %broadcast_in_dim.10), calls=%async_computation.1 | async-start | bytes 3670016 | tf_op jit(solution)/shard_map/all_to_all | solution.py:160
  56.9 19.9 %collective-permute-done.1 = bf16[32,4096]{1,0:T(8,128)(2,1)S(1)} collective-permute-done((bf16[32,4096]{1,0:T(8,128)(2,1)}, bf16[32,4096]{1,0:T(8,128)(2,1)S(1)}, u32[]{:S(2)}, u32[]{:S(2)}) %collective-permute-start.1) | collective-permute-done | bytes 262176 | tf_op jit(solution)/shard_map/ppermute | solution.py:141
  76.8 1.9 collective-permute-start.4
  78.7 4.6 %collective-permute-start.2 = (bf16[64,4096]{1,0:T(8,128)(2,1)S(1)}, bf16[64,4096]{1,0:T(8,128)(2,1)S(1)}, u32[]{:S(2)}, u32[]{:S(2)}) collective-permute-start(bf16[64,4096]{1,0:T(8,128)(2,1)S(1)} %pad_maximum_fusion), channel_id=1, source_target_pairs={{0,1},{1,0},{2,3},{3,2},{32,35},{33,34},{34,33},{35,32},{4,5},{5,4... | collective-permute-start | bytes 1572872 | tf_op jit(solution)/shard_map/ppermute | solution.py:153
  83.4 0.7 constant_dynamic-update-slice_fusion.2
  84.1 0.7 constant_dynamic-update-slice_fusion.1
  84.8 7.1 %collective-permute-done.4 = bf16[64,4096]{1,0:T(8,128)(2,1)} collective-permute-done((bf16[64,4096]{1,0:T(8,128)(2,1)S(1)}, bf16[64,4096]{1,0:T(8,128)(2,1)}, u32[]{:S(2)}, u32[]{:S(2)}) %collective-permute-start.4) | collective-permute-done | bytes 524320 | tf_op jit(solution)/shard_map/ppermute | solution.py:143
  91.9 4.6 %collective-permute-start.5 = (bf16[64,4096]{1,0:T(8,128)(2,1)}, bf16[64,4096]{1,0:T(8,128)(2,1)}, u32[]{:S(2)}, u32[]{:S(2)}) collective-permute-start(bf16[64,4096]{1,0:T(8,128)(2,1)} %collective-permute-done.4), channel_id=1, source_target_pairs={{0,1},{1,0},{2,3},{3,2},{32,35},{33,34},{34,33},{35,32},{4,5},{5,4... | collective-permute-start | bytes 1572872 | tf_op jit(solution)/shard_map/ppermute | solution.py:153
  96.6 0.0 collective-permute-done.2
  96.6 0.8 constant_dynamic-update-slice_fusion.refs_0_
  97.4 1.9 collective-permute-start.3
  99.3 4.1 %collective-permute-start.7 = (bf16[4,256,896]{2,1,0:T(8,128)(2,1)S(1)}, bf16[4,256,896]{2,1,0:T(8,128)(2,1)}, u32[]{:S(2)}, u32[]{:S(2)}) collective-permute-start(bf16[4,256,896]{2,1,0:T(8,128)(2,1)S(1)} %all-to-all-done.refs_4_), channel_id=1, source_target_pairs={{0,32},{32,0},{1,33},{33,1},{2,34},{34,2},{3,35},{35,3},{4,36},{36... | collective-permute-start | bytes 5505032 | tf_op jit(solution)/shard_map/ppermute | solution.py:165
  103.5 0.0 all-to-all-done.1.refs_6_
  103.5 1.9 collective-permute-start.9
  105.4 1.1 constant_dynamic-update-slice_fusion.6
  106.5 0.0 collective-permute-done.5
  106.5 1.1 constant_dynamic-update-slice_fusion.5.refs_2_
  107.6 2.3 %collective-permute-start.6 = (bf16[128,4096]{1,0:T(8,128)(2,1)S(1)}, bf16[128,4096]{1,0:T(8,128)(2,1)}, u32[]{:S(2)}, u32[]{:S(2)}) collective-permute-start(bf16[128,4096]{1,0:T(8,128)(2,1)S(1)} %constant_dynamic-update-slice_fusion.5.refs_2_), channel_id=1, source_target_pairs={{0,3},{1,2},{2,1},{3,0},{32,33},{33,32},{34,35},{35,34},{4,7},{5,6... | collective-permute-start | bytes 3145736 | tf_op jit(solution)/shard_map/ppermute | solution.py:155
  110.0 0.6 stack.181.cols_ref
  110.6 0.6 stack.214.slot_ref
  111.3 4.0 %collective-permute-done.3.refs_1_ = bf16[128,4096]{1,0:T(8,128)(2,1)} collective-permute-done((bf16[128,4096]{1,0:T(8,128)(2,1)}, bf16[128,4096]{1,0:T(8,128)(2,1)}, u32[]{:S(2)}, u32[]{:S(2)}) %collective-permute-start.3) | collective-permute-done | bytes 1048608 | tf_op jit(solution)/shard_map/ppermute | solution.py:155
  115.3 11.3 %collective-permute-done.6.refs_3_ = bf16[128,4096]{1,0:T(8,128)(2,1)} collective-permute-done((bf16[128,4096]{1,0:T(8,128)(2,1)S(1)}, bf16[128,4096]{1,0:T(8,128)(2,1)}, u32[]{:S(2)}, u32[]{:S(2)}) %collective-permute-start.6) | collective-permute-done | bytes 1048608 | tf_op jit(solution)/shard_map/ppermute | solution.py:155
  126.6 0.0 collective-permute-done.7.refs_5_
  126.6 0.0 collective-permute-done.9.refs_7_
  126.6 0.0 copy-start.7
  126.6 0.0 copy-start.8
  126.7 8.7 %mlp.1 = f32[32,8,128]{2,1,0:T(8,128)} custom-call(s32[16]{0:T(128)} %stack.181.cols_ref, s32[32]{0:T(128)} %stack.214.slot_ref, bf16[128,4096]{1,0:T(8,128)(2,1)} %constant_dynamic-update-slice_fusion.refs_0_, bf16[128,4096]{1,0:T(8,128)(2,1)} %collective-permute-done.3.refs_1_, bf16[128,4096]{1,0:T(8,128)(2,1)} %copy-done.2, ...), custom_call_target="tpu_custom_call" | custom-call | tf_op jit(solution)/shard_map/mlp/pallas_call | solution.py:66
  135.4 9.3 %all-to-all-start.2 = ((f32[32,8,128]{2,1,0:T(8,128)}), f32[32,8,128]{2,1,0:T(8,128)S(1)}, u32[]{:S(2)}, u32[]{:S(2)}) async-start(f32[32,8,128]{2,1,0:T(8,128)} %mlp.1), calls=%async_computation.2 | async-start | bytes 262144 | tf_op jit(solution)/shard_map/all_to_all | solution.py:173
  146.0 0.9 convolution_bitcast_fusion.right_ref
  146.9 10.0 %all-to-all-done.2.parts_ref = f32[32,8,128]{2,1,0:T(8,128)S(1)} async-done(((f32[32,8,128]{2,1,0:T(8,128)}), f32[32,8,128]{2,1,0:T(8,128)S(1)}, u32[]{:S(2)}, u32[]{:S(2)}) %all-to-all-start.2) | async-done | bytes 131104 | tf_op jit(solution)/shard_map/all_to_all | solution.py:173
  156.9 0.6 copy-done.5
  157.5 2.1 %norm.1 = (f32[8,128]{1,0:T(8,128)}, f32[16,8,128]{2,1,0:T(8,128)}) custom-call(f32[32,8,128]{2,1,0:T(8,128)} %copy-done.5, f32[2,8,64]{2,1,0:T(8,128)} %convolution_bitcast_fusion.right_ref, s32[1]{0:T(128)S(6)} %copy.19.train_len_ref, s32[1]{0:T(128)S(6)} %copy.20.roll_len_ref), custom_call_target="tpu_custom_call" | custom-call | tf_op jit(solution)/shard_map/norm/pallas_call | solution.py:176
  159.6 15.8 %all-to-all-start.4 = ((f32[16,8,128]{2,1,0:T(8,128)}), f32[16,8,128]{2,1,0:T(8,128)S(1)}, u32[]{:S(2)}, u32[]{:S(2)}) async-start(f32[16,8,128]{2,1,0:T(8,128)} %get-tuple-element.8), calls=%async_computation.4 | async-start | bytes 131072 | tf_op jit(solution)/shard_map/all_to_all | solution.py:182
  175.4 2.3 %collective-permute-start.10 = (f32[8,128]{1,0:T(8,128)}, f32[8,128]{1,0:T(8,128)S(1)}, u32[]{:S(2)}, u32[]{:S(2)}) collective-permute-start(f32[8,128]{1,0:T(8,128)} %get-tuple-element.7), channel_id=1, source_target_pairs={{0,1},{1,2},{2,3},{3,0},{4,5},{5,6},{6,7},{7,4},{8,9},{9,10},{10,1... | collective-permute-start | bytes 12296 | tf_op jit(solution)/shard_map/ppermute | solution.py:185
  177.8 4.2 %collective-permute-start.11 = (f32[8,128]{1,0:T(8,128)}, f32[8,128]{1,0:T(8,128)S(1)}, u32[]{:S(2)}, u32[]{:S(2)}) collective-permute-start(f32[8,128]{1,0:T(8,128)} %get-tuple-element.7), channel_id=1, source_target_pairs={{0,3},{1,0},{2,1},{3,2},{4,7},{5,4},{6,5},{7,6},{8,11},{9,8},{10,9... | collective-permute-start | bytes 12296 | tf_op jit(solution)/shard_map/ppermute | solution.py:185
  182.0 2.0 collective-permute-start.12
  184.0 0.0 collective-permute-done.10
  184.0 0.0 collective-permute-done.11
  184.0 4.3 %collective-permute-done.12 = f32[8,128]{1,0:T(8,128)S(1)} collective-permute-done((f32[8,128]{1,0:T(8,128)}, f32[8,128]{1,0:T(8,128)S(1)}, u32[]{:S(2)}, u32[]{:S(2)}) %collective-permute-start.12) | collective-permute-done | bytes 4128 | tf_op jit(solution)/shard_map/ppermute | solution.py:185
  188.3 0.7 pad_maximum_fusion.3
  189.0 1.0 all-to-all-done.4.roll_ref
  190.0 13.8 %all_to_all.25.train_ref = f32[8,4,8,128]{3,2,1,0:T(8,128)} all-to-all(f32[8,4,8,128]{3,2,1,0:T(8,128)S(1)} %broadcast_in_dim.11), channel_id=1, replica_groups=mesh['x'=4,'zh'=2,'co'=2,'zl'=8,'y'=4] {'zl'}, dimensions={0} | all-to-all | bytes 262144 | tf_op jit(solution)/shard_map/all_to_all | solution.py:186
  203.8 0.0 copy-done.6
  203.8 2.1 %score.1 = f32[16,32]{1,0:T(8,128)} custom-call(f32[8,4,8,128]{3,2,1,0:T(8,128)} %all_to_all.25.train_ref, f32[16,8,128]{2,1,0:T(8,128)} %copy-done.6, s32[1]{0:T(128)} %bitcast.58.y_ref), custom_call_target="tpu_custom_call" | custom-call | tf_op jit(solution)/shard_map/score/pallas_call | solution.py:189
  (13 shorter events, 0.1 us)
Async XLA Ops:
  0.0 146.0 %copy-start = (bf16[4096,64]{0,1:T(8,128)(2,1)S(1)}, bf16[4096,64]{0,1:T(8,128)(2,1)}, u32[]{:S(2)}) copy-start(bf16[4096,64]{0,1:T(8,128)(2,1)} %param.19) | copy-start | bytes 1572868
  0.9 28.7 %collective-permute-start = (bf16[16,4096]{1,0:T(8,128)(2,1)S(1)}, bf16[16,4096]{1,0:T(8,128)(2,1)S(1)}, u32[]{:S(2)}, u32[]{:S(2)}) collective-permute-start(bf16[16,4096]{1,0:T(8,128)(2,1)S(1)} %pad_maximum_fusion.2), channel_id=1, source_target_pairs={{0,16},{4,20},{8,24},{12,28},{16,0},{20,4},{24,8},{28,12},{1,17},{... | collective-permute-start | bytes 393224 | tf_op jit(solution)/shard_map/ppermute | solution.py:141
  12.5 27.1 %collective-permute-start.8 = (bf16[256,896]{0,1:T(8,128)(2,1)S(1)}, bf16[256,896]{0,1:T(8,128)(2,1)}, u32[]{:S(2)}, u32[]{:S(2)}) collective-permute-start(bf16[256,896]{0,1:T(8,128)(2,1)S(1)} %constant_dynamic-update-slice_fusion.7), channel_id=1, source_target_pairs={{0,64},{64,0},{1,65},{65,1},{2,66},{66,2},{3,67},{67,3},{4,68},{68... | collective-permute-start | bytes 1376264 | tf_op jit(solution)/shard_map/ppermute | solution.py:137
  24.8 4.2 %copy-start.3 = (bf16[1,8,4096]{2,1,0:T(8,128)(2,1)S(1)}, bf16[1,8,4096]{2,1,0:T(8,128)(2,1)}, u32[]{:S(2)}) copy-start(bf16[1,8,4096]{2,1,0:T(8,128)(2,1)} %param.10) | copy-start | bytes 196612
  24.8 4.8 %copy-start.4 = (bf16[1,8,4096]{2,1,0:T(8,128)(2,1)S(1)}, bf16[1,8,4096]{2,1,0:T(8,128)(2,1)}, u32[]{:S(2)}) copy-start(bf16[1,8,4096]{2,1,0:T(8,128)(2,1)} %param.13) | copy-start | bytes 196612
  24.8 26.2 %all-to-all-start = ((bf16[4,256,896]{2,1,0:T(8,128)(2,1)}), bf16[4,256,896]{2,1,0:T(8,128)(2,1)S(1)}, u32[]{:S(2)}, u32[]{:S(2)}) async-start(bf16[4,256,896]{2,1,0:T(8,128)(2,1)} %broadcast_in_dim.9), calls=%async_computation | async-start | bytes 3670016 | tf_op jit(solution)/shard_map/all_to_all | solution.py:160
  30.3 46.5 %collective-permute-start.1 = (bf16[32,4096]{1,0:T(8,128)(2,1)}, bf16[32,4096]{1,0:T(8,128)(2,1)S(1)}, u32[]{:S(2)}, u32[]{:S(2)}) collective-permute-start(bf16[32,4096]{1,0:T(8,128)(2,1)} %pad_maximum_fusion.1), channel_id=1, source_target_pairs={{0,8},{4,12},{8,0},{12,4},{16,24},{20,28},{24,16},{28,20},{1,9},{5... | collective-permute-start | bytes 786440 | tf_op jit(solution)/shard_map/ppermute | solution.py:141
  51.0 48.3 %copy-start.1 = (bf16[4,256,896]{2,1,0:T(8,128)(2,1)}, bf16[4,256,896]{2,1,0:T(8,128)(2,1)S(1)}, u32[]{:S(2)}) copy-start(bf16[4,256,896]{2,1,0:T(8,128)(2,1)S(1)} %all-to-all-done.refs_4_) | copy-start | bytes 5505028
  52.5 51.0 %all-to-all-start.1 = ((bf16[4,256,896]{2,1,0:T(8,128)(2,1)}), bf16[4,256,896]{2,1,0:T(8,128)(2,1)}, u32[]{:S(2)}, u32[]{:S(2)}) async-start(bf16[4,256,896]{2,1,0:T(8,128)(2,1)} %broadcast_in_dim.10), calls=%async_computation.1 | async-start | bytes 3670016 | tf_op jit(solution)/shard_map/all_to_all | solution.py:160
  76.8 15.1 %collective-permute-start.4 = (bf16[64,4096]{1,0:T(8,128)(2,1)S(1)}, bf16[64,4096]{1,0:T(8,128)(2,1)}, u32[]{:S(2)}, u32[]{:S(2)}) collective-permute-start(bf16[64,4096]{1,0:T(8,128)(2,1)S(1)} %pad_maximum_fusion), channel_id=1, source_target_pairs={{0,4},{4,0},{8,12},{12,8},{16,20},{20,16},{24,28},{28,24},{1,5},{5... | collective-permute-start | bytes 1572872 | tf_op jit(solution)/shard_map/ppermute | solution.py:143
  78.7 17.8 %collective-permute-start.2 = (bf16[64,4096]{1,0:T(8,128)(2,1)S(1)}, bf16[64,4096]{1,0:T(8,128)(2,1)S(1)}, u32[]{:S(2)}, u32[]{:S(2)}) collective-permute-start(bf16[64,4096]{1,0:T(8,128)(2,1)S(1)} %pad_maximum_fusion), channel_id=1, source_target_pairs={{0,1},{1,0},{2,3},{3,2},{32,35},{33,34},{34,33},{35,32},{4,5},{5,4... | collective-permute-start | bytes 1572872 | tf_op jit(solution)/shard_map/ppermute | solution.py:153
  91.9 14.6 %collective-permute-start.5 = (bf16[64,4096]{1,0:T(8,128)(2,1)}, bf16[64,4096]{1,0:T(8,128)(2,1)}, u32[]{:S(2)}, u32[]{:S(2)}) collective-permute-start(bf16[64,4096]{1,0:T(8,128)(2,1)} %collective-permute-done.4), channel_id=1, source_target_pairs={{0,1},{1,0},{2,3},{3,2},{32,35},{33,34},{34,33},{35,32},{4,5},{5,4... | collective-permute-start | bytes 1572872 | tf_op jit(solution)/shard_map/ppermute | solution.py:153
  97.4 17.9 %collective-permute-start.3 = (bf16[128,4096]{1,0:T(8,128)(2,1)}, bf16[128,4096]{1,0:T(8,128)(2,1)}, u32[]{:S(2)}, u32[]{:S(2)}) collective-permute-start(bf16[128,4096]{1,0:T(8,128)(2,1)} %constant_dynamic-update-slice_fusion.refs_0_), channel_id=1, source_target_pairs={{0,3},{1,2},{2,1},{3,0},{32,33},{33,32},{34,35},{35,34},{4,7},{5,6... | collective-permute-start | bytes 3145736 | tf_op jit(solution)/shard_map/ppermute | solution.py:155
  99.3 27.3 %collective-permute-start.7 = (bf16[4,256,896]{2,1,0:T(8,128)(2,1)S(1)}, bf16[4,256,896]{2,1,0:T(8,128)(2,1)}, u32[]{:S(2)}, u32[]{:S(2)}) collective-permute-start(bf16[4,256,896]{2,1,0:T(8,128)(2,1)S(1)} %all-to-all-done.refs_4_), channel_id=1, source_target_pairs={{0,32},{32,0},{1,33},{33,1},{2,34},{34,2},{3,35},{35,3},{4,36},{36... | collective-permute-start | bytes 5505032 | tf_op jit(solution)/shard_map/ppermute | solution.py:165
  103.5 23.1 %collective-permute-start.9 = (bf16[4,256,896]{2,1,0:T(8,128)(2,1)}, bf16[4,256,896]{2,1,0:T(8,128)(2,1)}, u32[]{:S(2)}, u32[]{:S(2)}) collective-permute-start(bf16[4,256,896]{2,1,0:T(8,128)(2,1)} %all-to-all-done.1.refs_6_), channel_id=1, source_target_pairs={{0,32},{32,0},{1,33},{33,1},{2,34},{34,2},{3,35},{35,3},{4,36},{36... | collective-permute-start | bytes 5505032 | tf_op jit(solution)/shard_map/ppermute | solution.py:165
  107.6 19.0 %copy-start.2 = (bf16[128,4096]{1,0:T(8,128)(2,1)}, bf16[128,4096]{1,0:T(8,128)(2,1)S(1)}, u32[]{:S(2)}) copy-start(bf16[128,4096]{1,0:T(8,128)(2,1)S(1)} %constant_dynamic-update-slice_fusion.5.refs_2_) | copy-start | bytes 3145732
  107.6 19.0 %collective-permute-start.6 = (bf16[128,4096]{1,0:T(8,128)(2,1)S(1)}, bf16[128,4096]{1,0:T(8,128)(2,1)}, u32[]{:S(2)}, u32[]{:S(2)}) collective-permute-start(bf16[128,4096]{1,0:T(8,128)(2,1)S(1)} %constant_dynamic-update-slice_fusion.5.refs_2_), channel_id=1, source_target_pairs={{0,3},{1,2},{2,1},{3,0},{32,33},{33,32},{34,35},{35,34},{4,7},{5,6... | collective-permute-start | bytes 3145736 | tf_op jit(solution)/shard_map/ppermute | solution.py:155
  126.6 19.4 %copy-start.7 = (bf16[1,8,4096]{2,1,0:T(8,128)(2,1)S(1)}, bf16[1,8,4096]{2,1,0:T(8,128)(2,1)}, u32[]{:S(2)}) copy-start(bf16[1,8,4096]{2,1,0:T(8,128)(2,1)} %param.14) | copy-start | bytes 196612
  126.6 19.4 %copy-start.8 = (bf16[1,8,4096]{2,1,0:T(8,128)(2,1)S(1)}, bf16[1,8,4096]{2,1,0:T(8,128)(2,1)}, u32[]{:S(2)}) copy-start(bf16[1,8,4096]{2,1,0:T(8,128)(2,1)} %param.11) | copy-start | bytes 196612
  135.4 21.5 %all-to-all-start.2 = ((f32[32,8,128]{2,1,0:T(8,128)}), f32[32,8,128]{2,1,0:T(8,128)S(1)}, u32[]{:S(2)}, u32[]{:S(2)}) async-start(f32[32,8,128]{2,1,0:T(8,128)} %mlp.1), calls=%async_computation.2 | async-start | bytes 262144 | tf_op jit(solution)/shard_map/all_to_all | solution.py:173
  156.8 0.7 copy-start.5
  159.6 30.4 %all-to-all-start.4 = ((f32[16,8,128]{2,1,0:T(8,128)}), f32[16,8,128]{2,1,0:T(8,128)S(1)}, u32[]{:S(2)}, u32[]{:S(2)}) async-start(f32[16,8,128]{2,1,0:T(8,128)} %get-tuple-element.8), calls=%async_computation.4 | async-start | bytes 131072 | tf_op jit(solution)/shard_map/all_to_all | solution.py:182
  175.4 8.6 %collective-permute-start.10 = (f32[8,128]{1,0:T(8,128)}, f32[8,128]{1,0:T(8,128)S(1)}, u32[]{:S(2)}, u32[]{:S(2)}) collective-permute-start(f32[8,128]{1,0:T(8,128)} %get-tuple-element.7), channel_id=1, source_target_pairs={{0,1},{1,2},{2,3},{3,0},{4,5},{5,6},{6,7},{7,4},{8,9},{9,10},{10,1... | collective-permute-start | bytes 12296 | tf_op jit(solution)/shard_map/ppermute | solution.py:185
  177.8 6.2 %collective-permute-start.11 = (f32[8,128]{1,0:T(8,128)}, f32[8,128]{1,0:T(8,128)S(1)}, u32[]{:S(2)}, u32[]{:S(2)}) collective-permute-start(f32[8,128]{1,0:T(8,128)} %get-tuple-element.7), channel_id=1, source_target_pairs={{0,3},{1,0},{2,1},{3,2},{4,7},{5,4},{6,5},{7,6},{8,11},{9,8},{10,9... | collective-permute-start | bytes 12296 | tf_op jit(solution)/shard_map/ppermute | solution.py:185
  182.0 6.4 %collective-permute-start.12 = (f32[8,128]{1,0:T(8,128)}, f32[8,128]{1,0:T(8,128)S(1)}, u32[]{:S(2)}, u32[]{:S(2)}) collective-permute-start(f32[8,128]{1,0:T(8,128)} %get-tuple-element.7), channel_id=1, source_target_pairs={{0,2},{1,3},{2,0},{3,1},{4,6},{5,7},{6,4},{7,5},{8,10},{9,11},{10,... | collective-permute-start | bytes 12296 | tf_op jit(solution)/shard_map/ppermute | solution.py:185
  190.0 13.9 %copy-start.6 = (f32[16,8,128]{2,1,0:T(8,128)}, f32[16,8,128]{2,1,0:T(8,128)S(1)}, u32[]{:S(2)}) copy-start(f32[16,8,128]{2,1,0:T(8,128)S(1)} %all-to-all-done.4.roll_ref) | copy-start | bytes 196612

commit v8 on v7

--- a/solution.py
+++ b/solution.py
@@ -91,11 +91,12 @@
         )
         mean = jnp.sum(grad * grad) / (RANK * RANK)
         inv = 1.0 / jnp.sqrt(jnp.full((8, RANK), mean + 1e-6))
-        ref[...] = jnp.broadcast_to(jnp.concatenate([one * inv, right], axis=-1), ref.shape)
+        both = jnp.concatenate([one * inv, right], axis=-1).astype(ref.dtype)
+        ref[...] = jnp.broadcast_to(both, ref.shape)
 
 
 def score_kernel(train_ref, roll_ref, y_ref, out_ref):
-    t = train_ref[...].reshape(-1, 2 * RANK)
+    t = train_ref[...].astype(jnp.float32).reshape(-1, 2 * RANK)
     r = roll_ref[...].reshape(-1, 2 * RANK)
     dims = (((1,), (1,)), ((), ()))
     a = lax.dot_general(
@@ -171,7 +172,7 @@
     cot = jnp.concatenate([train_cotangent[0], roll_cotangent[0]], axis=0)
     right = jnp.dot(cot, out_project, preferred_element_type=jnp.float32).reshape(2, 8, RANK)
     parts = lax.all_to_all(parts, ("zl", "y"), 0, 0, tiled=True)
-    small = jax.ShapeDtypeStruct((8, 2 * RANK), jnp.float32)
+    small = jax.ShapeDtypeStruct((8, 2 * RANK), jnp.bfloat16)
     vmem, smem = pl.BlockSpec(memory_space=pltpu.VMEM), pl.BlockSpec(memory_space=pltpu.SMEM)
     train, roll = pl.pallas_call(
         norm_kernel,

time: 208 us -> 223 us (1.072)
  blocking collectives: 13.8 us -> 46.9 us
  starting transfers between devices: 87.1 us -> 71.2 us
    all_to_all x0 -> x1, blocking collectives: none -> 32.8 us  [on_device(): roll_all = lax.all_to_all(roll, ('x', 'zh', 'co'), 0, 0, tiled=True)]
    all_to_all x1 -> x0, starting transfers between devices: 15.8 us -> none  [on_device(): roll_all = lax.all_to_all(roll, ('x', 'zh', 'co'), 0, 0, tiled=True)]
    unnamed x24 -> x22, local copies, waits for them, and re-layouts: 5.38 us -> 5.35 us
  transfers between devices with their start and end apart: 17 -> 16, of which waited for: 9 -> 8; matrix products, arithmetic and copies ran while one was open for 8% -> 7% of each run, Pallas kernels for 0% -> 0%
where the time goes in v8:
time: 223 us; the launch traced here: 222 us
  waiting for transfers between devices  72.1 us (32%)
  starting transfers between devices  71.2 us (32%)
  blocking collectives  46.9 us (21%)
  local copies, waits for them, and re-layouts  13.9 us (6%)
  Pallas kernels  12.9 us (6%)
  other arithmetic  2.32 us (1%)
    all_to_all x1, blocking collectives, on_device(): roll_all = lax.all_to_all(roll, ('x', 'zh', 'co'), 0, 0, tiled=True)  32.8 us
    ppermute x2, waiting for transfers between devices, on_device(): got = lax.ppermute(block, 'zl', [(i, i ^ k) for i in range(NZL)])  19.9 us
    ppermute x2, waiting for transfers between devices, on_device(): xs += [both, lax.ppermute(both, ('co', 'y'), step2)]  15.4 us
    all_to_all x1, blocking collectives, on_device(): lax.all_to_all(jnp.broadcast_to(jnp.stack(near), (NZL, NY, 8, 2 * RANK)),...  14.1 us
    ppermute x2, starting transfers between devices, on_device(): got = lax.ppermute(block, 'zl', [(i, i ^ k) for i in range(NZL)])  12.7 us
    ppermute x1, starting transfers between devices, on_device(): other = lax.ppermute(w, 'zh', shift(2, 1))  10.6 us
    all_to_all x2, waiting for transfers between devices, over_x(): return lax.all_to_all(spread, 'x', 0, 0, tiled=True)  10.1 us
    all_to_all x1, waiting for transfers between devices, on_device(): parts = lax.all_to_all(parts, ('zl', 'y'), 0, 0, tiled=True)  9.94 us
  transfers between devices with their start and end apart: 16, of which 8 were waited for; matrix products, arithmetic and copies ran while one was open for 7% of the time, Pallas kernels for 0%

profile of v8, /device:TPU:1, one launch (start us, length us, event | category | flops | bytes accessed | tf_op | source)
XLA Modules:
  0.0 221.7 jit_solution(17311426153998600549)
XLA Ops:
  0.0 0.0 copy-start
  0.0 0.9 pad_maximum_fusion.2
  0.9 9.6 %collective-permute-start = (bf16[16,4096]{1,0:T(8,128)(2,1)S(1)}, bf16[16,4096]{1,0:T(8,128)(2,1)S(1)}, u32[]{:S(2)}, u32[]{:S(2)}) collective-permute-start(bf16[16,4096]{1,0:T(8,128)(2,1)S(1)} %pad_maximum_fusion.2), channel_id=1, source_target_pairs={{0,16},{4,20},{8,24},{12,28},{16,0},{20,4},{24,8},{28,12},{1,17},{... | collective-permute-start | bytes 393224 | tf_op jit(solution)/shard_map/ppermute | solution.py:142
  10.6 1.0 constant_dynamic-update-slice_fusion.8
  11.6 1.0 constant_dynamic-update-slice_fusion.7
  12.5 10.6 %collective-permute-start.8 = (bf16[256,896]{0,1:T(8,128)(2,1)S(1)}, bf16[256,896]{0,1:T(8,128)(2,1)}, u32[]{:S(2)}, u32[]{:S(2)}) collective-permute-start(bf16[256,896]{0,1:T(8,128)(2,1)S(1)} %constant_dynamic-update-slice_fusion.7), channel_id=1, source_target_pairs={{0,64},{64,0},{1,65},{65,1},{2,66},{66,2},{3,67},{67,3},{4,68},{68... | collective-permute-start | bytes 1376264 | tf_op jit(solution)/shard_map/ppermute | solution.py:138
  23.2 0.2 copy.11
  23.4 1.4 broadcast_in_dim.9
  24.8 4.1 %all-to-all-start = ((bf16[4,256,896]{2,1,0:T(8,128)(2,1)}), bf16[4,256,896]{2,1,0:T(8,128)(2,1)S(1)}, u32[]{:S(2)}, u32[]{:S(2)}) async-start(bf16[4,256,896]{2,1,0:T(8,128)(2,1)} %broadcast_in_dim.9), calls=%async_computation | async-start | bytes 3670016 | tf_op jit(solution)/shard_map/all_to_all | solution.py:161
  29.0 0.0 copy-done.3
  29.0 0.6 constant_dynamic-update-slice_fusion.4
  29.6 0.0 collective-permute-done
  29.6 0.0 copy-done.4
  29.6 0.7 pad_maximum_fusion.1
  30.3 3.1 %collective-permute-start.1 = (bf16[32,4096]{1,0:T(8,128)(2,1)}, bf16[32,4096]{1,0:T(8,128)(2,1)S(1)}, u32[]{:S(2)}, u32[]{:S(2)}) collective-permute-start(bf16[32,4096]{1,0:T(8,128)(2,1)} %pad_maximum_fusion.1), channel_id=1, source_target_pairs={{0,8},{4,12},{8,0},{12,4},{16,24},{20,28},{24,16},{28,20},{1,9},{5... | collective-permute-start | bytes 786440 | tf_op jit(solution)/shard_map/ppermute | solution.py:142
  33.4 0.6 constant_dynamic-update-slice_fusion.3
  34.0 5.6 %collective-permute-done.8 = bf16[256,896]{0,1:T(8,128)(2,1)} collective-permute-done((bf16[256,896]{0,1:T(8,128)(2,1)S(1)}, bf16[256,896]{0,1:T(8,128)(2,1)}, u32[]{:S(2)}, u32[]{:S(2)}) %collective-permute-start.8) | collective-permute-done | bytes 458784 | tf_op jit(solution)/shard_map/ppermute | solution.py:138
  39.6 1.3 copy.12
  40.9 10.1 %all-to-all-done.refs_4_ = bf16[4,256,896]{2,1,0:T(8,128)(2,1)S(1)} async-done(((bf16[4,256,896]{2,1,0:T(8,128)(2,1)}), bf16[4,256,896]{2,1,0:T(8,128)(2,1)S(1)}, u32[]{:S(2)}, u32[]{:S(2)}) %all-to-all-start) | async-done | bytes 1835040 | tf_op jit(solution)/shard_map/all_to_all | solution.py:161
  51.0 1.5 broadcast_in_dim.10
  52.5 4.4 %all-to-all-start.1 = ((bf16[4,256,896]{2,1,0:T(8,128)(2,1)}), bf16[4,256,896]{2,1,0:T(8,128)(2,1)}, u32[]{:S(2)}, u32[]{:S(2)}) async-start(bf16[4,256,896]{2,1,0:T(8,128)(2,1)} %broadcast_in_dim.10), calls=%async_computation.1 | async-start | bytes 3670016 | tf_op jit(solution)/shard_map/all_to_all | solution.py:161
  56.9 19.9 %collective-permute-done.1 = bf16[32,4096]{1,0:T(8,128)(2,1)S(1)} collective-permute-done((bf16[32,4096]{1,0:T(8,128)(2,1)}, bf16[32,4096]{1,0:T(8,128)(2,1)S(1)}, u32[]{:S(2)}, u32[]{:S(2)}) %collective-permute-start.1) | collective-permute-done | bytes 262176 | tf_op jit(solution)/shard_map/ppermute | solution.py:142
  76.8 1.9 collective-permute-start.4
  78.7 4.6 %collective-permute-start.2 = (bf16[64,4096]{1,0:T(8,128)(2,1)S(1)}, bf16[64,4096]{1,0:T(8,128)(2,1)S(1)}, u32[]{:S(2)}, u32[]{:S(2)}) collective-permute-start(bf16[64,4096]{1,0:T(8,128)(2,1)S(1)} %pad_maximum_fusion), channel_id=1, source_target_pairs={{0,1},{1,0},{2,3},{3,2},{32,35},{33,34},{34,33},{35,32},{4,5},{5,4... | collective-permute-start | bytes 1572872 | tf_op jit(solution)/shard_map/ppermute | solution.py:154
  83.4 0.7 constant_dynamic-update-slice_fusion.2
  84.1 0.7 constant_dynamic-update-slice_fusion.1
  84.8 7.1 %collective-permute-done.4 = bf16[64,4096]{1,0:T(8,128)(2,1)} collective-permute-done((bf16[64,4096]{1,0:T(8,128)(2,1)S(1)}, bf16[64,4096]{1,0:T(8,128)(2,1)}, u32[]{:S(2)}, u32[]{:S(2)}) %collective-permute-start.4) | collective-permute-done | bytes 524320 | tf_op jit(solution)/shard_map/ppermute | solution.py:144
  91.9 4.6 %collective-permute-start.5 = (bf16[64,4096]{1,0:T(8,128)(2,1)}, bf16[64,4096]{1,0:T(8,128)(2,1)}, u32[]{:S(2)}, u32[]{:S(2)}) collective-permute-start(bf16[64,4096]{1,0:T(8,128)(2,1)} %collective-permute-done.4), channel_id=1, source_target_pairs={{0,1},{1,0},{2,3},{3,2},{32,35},{33,34},{34,33},{35,32},{4,5},{5,4... | collective-permute-start | bytes 1572872 | tf_op jit(solution)/shard_map/ppermute | solution.py:154
  96.6 0.0 collective-permute-done.2
  96.6 0.8 constant_dynamic-update-slice_fusion.refs_0_
  97.4 1.9 collective-permute-start.3
  99.3 0.0 copy-done.1
  99.3 4.1 %collective-permute-start.7 = (bf16[4,256,896]{2,1,0:T(8,128)(2,1)S(1)}, bf16[4,256,896]{2,1,0:T(8,128)(2,1)}, u32[]{:S(2)}, u32[]{:S(2)}) collective-permute-start(bf16[4,256,896]{2,1,0:T(8,128)(2,1)S(1)} %all-to-all-done.refs_4_), channel_id=1, source_target_pairs={{0,32},{32,0},{1,33},{33,1},{2,34},{34,2},{3,35},{35,3},{4,36},{36... | collective-permute-start | bytes 5505032 | tf_op jit(solution)/shard_map/ppermute | solution.py:166
  103.5 0.0 all-to-all-done.1.refs_6_
  103.5 1.9 collective-permute-start.9
  105.4 1.1 constant_dynamic-update-slice_fusion.6
  106.5 0.0 collective-permute-done.5
  106.5 1.1 constant_dynamic-update-slice_fusion.5.refs_2_
  107.6 0.0 copy-start.2
  107.6 2.3 %collective-permute-start.6 = (bf16[128,4096]{1,0:T(8,128)(2,1)S(1)}, bf16[128,4096]{1,0:T(8,128)(2,1)}, u32[]{:S(2)}, u32[]{:S(2)}) collective-permute-start(bf16[128,4096]{1,0:T(8,128)(2,1)S(1)} %constant_dynamic-update-slice_fusion.5.refs_2_), channel_id=1, source_target_pairs={{0,3},{1,2},{2,1},{3,0},{32,33},{33,32},{34,35},{35,34},{4,7},{5,6... | collective-permute-start | bytes 3145736 | tf_op jit(solution)/shard_map/ppermute | solution.py:156
  110.0 0.6 stack.181.cols_ref
  110.6 0.6 stack.214.slot_ref
  111.2 4.1 %collective-permute-done.3.refs_1_ = bf16[128,4096]{1,0:T(8,128)(2,1)} collective-permute-done((bf16[128,4096]{1,0:T(8,128)(2,1)}, bf16[128,4096]{1,0:T(8,128)(2,1)}, u32[]{:S(2)}, u32[]{:S(2)}) %collective-permute-start.3) | collective-permute-done | bytes 1048608 | tf_op jit(solution)/shard_map/ppermute | solution.py:156
  115.3 11.3 %collective-permute-done.6.refs_3_ = bf16[128,4096]{1,0:T(8,128)(2,1)} collective-permute-done((bf16[128,4096]{1,0:T(8,128)(2,1)S(1)}, bf16[128,4096]{1,0:T(8,128)(2,1)}, u32[]{:S(2)}, u32[]{:S(2)}) %collective-permute-start.6) | collective-permute-done | bytes 1048608 | tf_op jit(solution)/shard_map/ppermute | solution.py:156
  126.6 0.0 collective-permute-done.7.refs_5_
  126.6 0.0 collective-permute-done.9.refs_7_
  126.6 0.0 copy-start.6
  126.6 0.0 copy-start.7
  126.7 8.7 %mlp.1 = f32[32,8,128]{2,1,0:T(8,128)} custom-call(s32[16]{0:T(128)} %stack.181.cols_ref, s32[32]{0:T(128)} %stack.214.slot_ref, bf16[128,4096]{1,0:T(8,128)(2,1)} %constant_dynamic-update-slice_fusion.refs_0_, bf16[128,4096]{1,0:T(8,128)(2,1)} %collective-permute-done.3.refs_1_, bf16[128,4096]{1,0:T(8,128)(2,1)} %copy-done.2, ...), custom_call_target="tpu_custom_call" | custom-call | tf_op jit(solution)/shard_map/mlp/pallas_call | solution.py:66
  135.4 9.3 %all-to-all-start.2 = ((f32[32,8,128]{2,1,0:T(8,128)}), f32[32,8,128]{2,1,0:T(8,128)S(1)}, u32[]{:S(2)}, u32[]{:S(2)}) async-start(f32[32,8,128]{2,1,0:T(8,128)} %mlp.1), calls=%async_computation.2 | async-start | bytes 262144 | tf_op jit(solution)/shard_map/all_to_all | solution.py:174
  146.0 0.9 convolution_bitcast_fusion.right_ref
  146.9 9.9 %all-to-all-done.2.parts_ref = f32[32,8,128]{2,1,0:T(8,128)S(1)} async-done(((f32[32,8,128]{2,1,0:T(8,128)}), f32[32,8,128]{2,1,0:T(8,128)S(1)}, u32[]{:S(2)}, u32[]{:S(2)}) %all-to-all-start.2) | async-done | bytes 131104 | tf_op jit(solution)/shard_map/all_to_all | solution.py:174
  156.8 0.6 copy-done.5
  157.5 2.1 norm.1
  159.5 2.3 %collective-permute-start.10 = (bf16[8,128]{1,0:T(8,128)(2,1)}, bf16[8,128]{1,0:T(8,128)(2,1)S(1)}, u32[]{:S(2)}, u32[]{:S(2)}) collective-permute-start(bf16[8,128]{1,0:T(8,128)(2,1)} %get-tuple-element.7), channel_id=1, source_target_pairs={{0,1},{1,2},{2,3},{3,0},{4,5},{5,6},{6,7},{7,4},{8,9},{9,10},{10,1... | collective-permute-start | bytes 6152 | tf_op jit(solution)/shard_map/ppermute | solution.py:186
  161.8 4.2 %collective-permute-start.11 = (bf16[8,128]{1,0:T(8,128)(2,1)}, bf16[8,128]{1,0:T(8,128)(2,1)S(1)}, u32[]{:S(2)}, u32[]{:S(2)}) collective-permute-start(bf16[8,128]{1,0:T(8,128)(2,1)} %get-tuple-element.7), channel_id=1, source_target_pairs={{0,3},{1,0},{2,1},{3,2},{4,7},{5,4},{6,5},{7,6},{8,11},{9,8},{10,9... | collective-permute-start | bytes 6152 | tf_op jit(solution)/shard_map/ppermute | solution.py:186
  166.0 2.0 collective-permute-start.12
  168.1 0.0 collective-permute-done.10
  168.1 0.0 collective-permute-done.11
  168.1 4.0 %collective-permute-done.12 = bf16[8,128]{1,0:T(8,128)(2,1)S(1)} collective-permute-done((bf16[8,128]{1,0:T(8,128)(2,1)}, bf16[8,128]{1,0:T(8,128)(2,1)S(1)}, u32[]{:S(2)}, u32[]{:S(2)}) %collective-permute-start.12) | collective-permute-done | bytes 2080 | tf_op jit(solution)/shard_map/ppermute | solution.py:186
  172.1 0.6 pad_maximum_fusion.3
  172.7 14.1 %all_to_all.25.train_ref = bf16[8,4,8,128]{3,2,1,0:T(8,128)(2,1)} all-to-all(bf16[8,4,8,128]{3,2,1,0:T(8,128)(2,1)S(1)} %broadcast_in_dim.11), channel_id=1, replica_groups=mesh['x'=4,'zh'=2,'co'=2,'zl'=8,'y'=4] {'zl'}, dimensions={0} | all-to-all | bytes 131072 | tf_op jit(solution)/shard_map/all_to_all | solution.py:187
  186.8 32.8 %all_to_all.26.roll_ref = f32[16,8,128]{2,1,0:T(8,128)} all-to-all(f32[16,8,128]{2,1,0:T(8,128)} %get-tuple-element.8), channel_id=1, replica_groups=mesh['x'=4,'zh'=2,'co'=2,'zl'=8,'y'=4] {'x','zh','co'}, dimensions={0} | all-to-all | bytes 131072 | tf_op jit(solution)/shard_map/all_to_all | solution.py:183
  219.6 2.1 score.1
  (10 shorter events, 0.1 us)
Async XLA Ops:
  0.0 146.0 %copy-start = (bf16[4096,64]{0,1:T(8,128)(2,1)S(1)}, bf16[4096,64]{0,1:T(8,128)(2,1)}, u32[]{:S(2)}) copy-start(bf16[4096,64]{0,1:T(8,128)(2,1)} %param.19) | copy-start | bytes 1572868
  0.9 28.6 %collective-permute-start = (bf16[16,4096]{1,0:T(8,128)(2,1)S(1)}, bf16[16,4096]{1,0:T(8,128)(2,1)S(1)}, u32[]{:S(2)}, u32[]{:S(2)}) collective-permute-start(bf16[16,4096]{1,0:T(8,128)(2,1)S(1)} %pad_maximum_fusion.2), channel_id=1, source_target_pairs={{0,16},{4,20},{8,24},{12,28},{16,0},{20,4},{24,8},{28,12},{1,17},{... | collective-permute-start | bytes 393224 | tf_op jit(solution)/shard_map/ppermute | solution.py:142
  12.5 27.1 %collective-permute-start.8 = (bf16[256,896]{0,1:T(8,128)(2,1)S(1)}, bf16[256,896]{0,1:T(8,128)(2,1)}, u32[]{:S(2)}, u32[]{:S(2)}) collective-permute-start(bf16[256,896]{0,1:T(8,128)(2,1)S(1)} %constant_dynamic-update-slice_fusion.7), channel_id=1, source_target_pairs={{0,64},{64,0},{1,65},{65,1},{2,66},{66,2},{3,67},{67,3},{4,68},{68... | collective-permute-start | bytes 1376264 | tf_op jit(solution)/shard_map/ppermute | solution.py:138
  24.8 4.2 %copy-start.3 = (bf16[1,8,4096]{2,1,0:T(8,128)(2,1)S(1)}, bf16[1,8,4096]{2,1,0:T(8,128)(2,1)}, u32[]{:S(2)}) copy-start(bf16[1,8,4096]{2,1,0:T(8,128)(2,1)} %param.10) | copy-start | bytes 196612
  24.8 4.8 %copy-start.4 = (bf16[1,8,4096]{2,1,0:T(8,128)(2,1)S(1)}, bf16[1,8,4096]{2,1,0:T(8,128)(2,1)}, u32[]{:S(2)}) copy-start(bf16[1,8,4096]{2,1,0:T(8,128)(2,1)} %param.13) | copy-start | bytes 196612
  24.8 26.2 %all-to-all-start = ((bf16[4,256,896]{2,1,0:T(8,128)(2,1)}), bf16[4,256,896]{2,1,0:T(8,128)(2,1)S(1)}, u32[]{:S(2)}, u32[]{:S(2)}) async-start(bf16[4,256,896]{2,1,0:T(8,128)(2,1)} %broadcast_in_dim.9), calls=%async_computation | async-start | bytes 3670016 | tf_op jit(solution)/shard_map/all_to_all | solution.py:161
  30.3 46.5 %collective-permute-start.1 = (bf16[32,4096]{1,0:T(8,128)(2,1)}, bf16[32,4096]{1,0:T(8,128)(2,1)S(1)}, u32[]{:S(2)}, u32[]{:S(2)}) collective-permute-start(bf16[32,4096]{1,0:T(8,128)(2,1)} %pad_maximum_fusion.1), channel_id=1, source_target_pairs={{0,8},{4,12},{8,0},{12,4},{16,24},{20,28},{24,16},{28,20},{1,9},{5... | collective-permute-start | bytes 786440 | tf_op jit(solution)/shard_map/ppermute | solution.py:142
  51.0 48.3 %copy-start.1 = (bf16[4,256,896]{2,1,0:T(8,128)(2,1)}, bf16[4,256,896]{2,1,0:T(8,128)(2,1)S(1)}, u32[]{:S(2)}) copy-start(bf16[4,256,896]{2,1,0:T(8,128)(2,1)S(1)} %all-to-all-done.refs_4_) | copy-start | bytes 5505028
  52.5 51.0 %all-to-all-start.1 = ((bf16[4,256,896]{2,1,0:T(8,128)(2,1)}), bf16[4,256,896]{2,1,0:T(8,128)(2,1)}, u32[]{:S(2)}, u32[]{:S(2)}) async-start(bf16[4,256,896]{2,1,0:T(8,128)(2,1)} %broadcast_in_dim.10), calls=%async_computation.1 | async-start | bytes 3670016 | tf_op jit(solution)/shard_map/all_to_all | solution.py:161
  76.8 15.1 %collective-permute-start.4 = (bf16[64,4096]{1,0:T(8,128)(2,1)S(1)}, bf16[64,4096]{1,0:T(8,128)(2,1)}, u32[]{:S(2)}, u32[]{:S(2)}) collective-permute-start(bf16[64,4096]{1,0:T(8,128)(2,1)S(1)} %pad_maximum_fusion), channel_id=1, source_target_pairs={{0,4},{4,0},{8,12},{12,8},{16,20},{20,16},{24,28},{28,24},{1,5},{5... | collective-permute-start | bytes 1572872 | tf_op jit(solution)/shard_map/ppermute | solution.py:144
  78.7 17.8 %collective-permute-start.2 = (bf16[64,4096]{1,0:T(8,128)(2,1)S(1)}, bf16[64,4096]{1,0:T(8,128)(2,1)S(1)}, u32[]{:S(2)}, u32[]{:S(2)}) collective-permute-start(bf16[64,4096]{1,0:T(8,128)(2,1)S(1)} %pad_maximum_fusion), channel_id=1, source_target_pairs={{0,1},{1,0},{2,3},{3,2},{32,35},{33,34},{34,33},{35,32},{4,5},{5,4... | collective-permute-start | bytes 1572872 | tf_op jit(solution)/shard_map/ppermute | solution.py:154
  91.9 14.6 %collective-permute-start.5 = (bf16[64,4096]{1,0:T(8,128)(2,1)}, bf16[64,4096]{1,0:T(8,128)(2,1)}, u32[]{:S(2)}, u32[]{:S(2)}) collective-permute-start(bf16[64,4096]{1,0:T(8,128)(2,1)} %collective-permute-done.4), channel_id=1, source_target_pairs={{0,1},{1,0},{2,3},{3,2},{32,35},{33,34},{34,33},{35,32},{4,5},{5,4... | collective-permute-start | bytes 1572872 | tf_op jit(solution)/shard_map/ppermute | solution.py:154
  97.4 17.9 %collective-permute-start.3 = (bf16[128,4096]{1,0:T(8,128)(2,1)}, bf16[128,4096]{1,0:T(8,128)(2,1)}, u32[]{:S(2)}, u32[]{:S(2)}) collective-permute-start(bf16[128,4096]{1,0:T(8,128)(2,1)} %constant_dynamic-update-slice_fusion.refs_0_), channel_id=1, source_target_pairs={{0,3},{1,2},{2,1},{3,0},{32,33},{33,32},{34,35},{35,34},{4,7},{5,6... | collective-permute-start | bytes 3145736 | tf_op jit(solution)/shard_map/ppermute | solution.py:156
  99.3 27.3 %collective-permute-start.7 = (bf16[4,256,896]{2,1,0:T(8,128)(2,1)S(1)}, bf16[4,256,896]{2,1,0:T(8,128)(2,1)}, u32[]{:S(2)}, u32[]{:S(2)}) collective-permute-start(bf16[4,256,896]{2,1,0:T(8,128)(2,1)S(1)} %all-to-all-done.refs_4_), channel_id=1, source_target_pairs={{0,32},{32,0},{1,33},{33,1},{2,34},{34,2},{3,35},{35,3},{4,36},{36... | collective-permute-start | bytes 5505032 | tf_op jit(solution)/shard_map/ppermute | solution.py:166
  103.5 23.1 %collective-permute-start.9 = (bf16[4,256,896]{2,1,0:T(8,128)(2,1)}, bf16[4,256,896]{2,1,0:T(8,128)(2,1)}, u32[]{:S(2)}, u32[]{:S(2)}) collective-permute-start(bf16[4,256,896]{2,1,0:T(8,128)(2,1)} %all-to-all-done.1.refs_6_), channel_id=1, source_target_pairs={{0,32},{32,0},{1,33},{33,1},{2,34},{34,2},{3,35},{35,3},{4,36},{36... | collective-permute-start | bytes 5505032 | tf_op jit(solution)/shard_map/ppermute | solution.py:166
  107.6 19.0 %copy-start.2 = (bf16[128,4096]{1,0:T(8,128)(2,1)}, bf16[128,4096]{1,0:T(8,128)(2,1)S(1)}, u32[]{:S(2)}) copy-start(bf16[128,4096]{1,0:T(8,128)(2,1)S(1)} %constant_dynamic-update-slice_fusion.5.refs_2_) | copy-start | bytes 3145732
  107.6 19.0 %collective-permute-start.6 = (bf16[128,4096]{1,0:T(8,128)(2,1)S(1)}, bf16[128,4096]{1,0:T(8,128)(2,1)}, u32[]{:S(2)}, u32[]{:S(2)}) collective-permute-start(bf16[128,4096]{1,0:T(8,128)(2,1)S(1)} %constant_dynamic-update-slice_fusion.5.refs_2_), channel_id=1, source_target_pairs={{0,3},{1,2},{2,1},{3,0},{32,33},{33,32},{34,35},{35,34},{4,7},{5,6... | collective-permute-start | bytes 3145736 | tf_op jit(solution)/shard_map/ppermute | solution.py:156
  126.6 19.4 %copy-start.6 = (bf16[1,8,4096]{2,1,0:T(8,128)(2,1)S(1)}, bf16[1,8,4096]{2,1,0:T(8,128)(2,1)}, u32[]{:S(2)}) copy-start(bf16[1,8,4096]{2,1,0:T(8,128)(2,1)} %param.14) | copy-start | bytes 196612
  126.6 19.4 %copy-start.7 = (bf16[1,8,4096]{2,1,0:T(8,128)(2,1)S(1)}, bf16[1,8,4096]{2,1,0:T(8,128)(2,1)}, u32[]{:S(2)}) copy-start(bf16[1,8,4096]{2,1,0:T(8,128)(2,1)} %param.11) | copy-start | bytes 196612
  135.4 21.4 %all-to-all-start.2 = ((f32[32,8,128]{2,1,0:T(8,128)}), f32[32,8,128]{2,1,0:T(8,128)S(1)}, u32[]{:S(2)}, u32[]{:S(2)}) async-start(f32[32,8,128]{2,1,0:T(8,128)} %mlp.1), calls=%async_computation.2 | async-start | bytes 262144 | tf_op jit(solution)/shard_map/all_to_all | solution.py:174
  156.8 0.6 copy-start.5
  159.5 8.5 %collective-permute-start.10 = (bf16[8,128]{1,0:T(8,128)(2,1)}, bf16[8,128]{1,0:T(8,128)(2,1)S(1)}, u32[]{:S(2)}, u32[]{:S(2)}) collective-permute-start(bf16[8,128]{1,0:T(8,128)(2,1)} %get-tuple-element.7), channel_id=1, source_target_pairs={{0,1},{1,2},{2,3},{3,0},{4,5},{5,6},{6,7},{7,4},{8,9},{9,10},{10,1... | collective-permute-start | bytes 6152 | tf_op jit(solution)/shard_map/ppermute | solution.py:186
  161.8 6.3 %collective-permute-start.11 = (bf16[8,128]{1,0:T(8,128)(2,1)}, bf16[8,128]{1,0:T(8,128)(2,1)S(1)}, u32[]{:S(2)}, u32[]{:S(2)}) collective-permute-start(bf16[8,128]{1,0:T(8,128)(2,1)} %get-tuple-element.7), channel_id=1, source_target_pairs={{0,3},{1,0},{2,1},{3,2},{4,7},{5,4},{6,5},{7,6},{8,11},{9,8},{10,9... | collective-permute-start | bytes 6152 | tf_op jit(solution)/shard_map/ppermute | solution.py:186
  166.0 6.0 %collective-permute-start.12 = (bf16[8,128]{1,0:T(8,128)(2,1)}, bf16[8,128]{1,0:T(8,128)(2,1)S(1)}, u32[]{:S(2)}, u32[]{:S(2)}) collective-permute-start(bf16[8,128]{1,0:T(8,128)(2,1)} %get-tuple-element.7), channel_id=1, source_target_pairs={{0,2},{1,3},{2,0},{3,1},{4,6},{5,7},{6,4},{7,5},{8,10},{9,11},{10,... | collective-permute-start | bytes 6152 | tf_op jit(solution)/shard_map/ppermute | solution.py:186

commit v9 on v7

--- a/solution.py
+++ b/solution.py
@@ -94,6 +94,11 @@
         ref[...] = jnp.broadcast_to(jnp.concatenate([one * inv, right], axis=-1), ref.shape)
 
 
+def repeat_kernel(*refs):
+    for k in range(NY):
+        refs[NY][:, k] = jnp.broadcast_to(refs[k][...], (NZL,) + refs[k].shape)
+
+
 def score_kernel(train_ref, roll_ref, y_ref, out_ref):
     t = train_ref[...].reshape(-1, 2 * RANK)
     r = roll_ref[...].reshape(-1, 2 * RANK)
@@ -184,7 +189,15 @@
     )
     near = [train] + [lax.ppermute(train, "y", shift(NY, k)) for k in (1, 3, 2)]
     train_all = lax.all_to_all(
-        jnp.broadcast_to(jnp.stack(near), (NZL, NY, 8, 2 * RANK)), "zl", 0, 0, tiled=True
+        pl.pallas_call(
+            repeat_kernel,
+            out_shape=jax.ShapeDtypeStruct((NZL, NY, 8, 2 * RANK), jnp.float32),
+            name="repeat",
+        )(*near),
+        "zl",
+        0,
+        0,
+        tiled=True,
     )
     scores = pl.pallas_call(
         score_kernel,

time: 208 us -> 209 us (level)
    unnamed x24 -> x30, local copies, waits for them, and re-layouts: 5.38 us -> 5.95 us
  transfers between devices with their start and end apart: 17 -> 17, of which waited for: 9 -> 8; matrix products, arithmetic and copies ran while one was open for 8% -> 7% of each run, Pallas kernels for 0% -> 1%
where the time goes in v9:
time: 209 us; the launch traced here: 207 us
  starting transfers between devices  87.2 us (42%)
  waiting for transfers between devices  72.2 us (35%)
  local copies, waits for them, and re-layouts  14.6 us (7%)
  Pallas kernels  14.3 us (7%)
  blocking collectives  14.3 us (7%)
    ppermute x2, waiting for transfers between devices, on_device(): got = lax.ppermute(block, 'zl', [(i, i ^ k) for i in range(NZL)])  19.8 us
    all_to_all x1, starting transfers between devices, on_device(): roll_all = lax.all_to_all(roll, ('x', 'zh', 'co'), 0, 0, tiled=True)  15.9 us
    ppermute x2, waiting for transfers between devices, on_device(): xs += [both, lax.ppermute(both, ('co', 'y'), step2)]  15.3 us
    all_to_all x1, blocking collectives, on_device(): lax.all_to_all(pl.pallas_call(repeat_kernel, out_shape=jax.ShapeDtypeStru...  14.3 us
    ppermute x2, starting transfers between devices, on_device(): got = lax.ppermute(block, 'zl', [(i, i ^ k) for i in range(NZL)])  12.7 us
    ppermute x1, starting transfers between devices, on_device(): other = lax.ppermute(w, 'zh', shift(2, 1))  10.6 us
    all_to_all x2, waiting for transfers between devices, over_x(): return lax.all_to_all(spread, 'x', 0, 0, tiled=True)  10.1 us
    all_to_all x1, waiting for transfers between devices, on_device(): parts = lax.all_to_all(parts, ('zl', 'y'), 0, 0, tiled=True)  9.94 us
  transfers between devices with their start and end apart: 17, of which 8 were waited for; matrix products, arithmetic and copies ran while one was open for 7% of the time, Pallas kernels for 1%

profile of v9, /device:TPU:1, one launch (start us, length us, event | category | flops | bytes accessed | tf_op | source)
XLA Modules:
  0.0 206.7 jit_solution(15593995929421843447)
XLA Ops:
  0.0 0.0 copy-start
  0.0 0.9 pad_maximum_fusion.2
  0.9 9.6 %collective-permute-start = (bf16[16,4096]{1,0:T(8,128)(2,1)S(1)}, bf16[16,4096]{1,0:T(8,128)(2,1)S(1)}, u32[]{:S(2)}, u32[]{:S(2)}) collective-permute-start(bf16[16,4096]{1,0:T(8,128)(2,1)S(1)} %pad_maximum_fusion.2), channel_id=1, source_target_pairs={{0,16},{4,20},{8,24},{12,28},{16,0},{20,4},{24,8},{28,12},{1,17},{... | collective-permute-start | bytes 393224 | tf_op jit(solution)/shard_map/ppermute | solution.py:146
  10.6 1.0 constant_dynamic-update-slice_fusion.8
  11.6 1.0 constant_dynamic-update-slice_fusion.7
  12.5 10.6 %collective-permute-start.8 = (bf16[256,896]{0,1:T(8,128)(2,1)S(1)}, bf16[256,896]{0,1:T(8,128)(2,1)}, u32[]{:S(2)}, u32[]{:S(2)}) collective-permute-start(bf16[256,896]{0,1:T(8,128)(2,1)S(1)} %constant_dynamic-update-slice_fusion.7), channel_id=1, source_target_pairs={{0,64},{64,0},{1,65},{65,1},{2,66},{66,2},{3,67},{67,3},{4,68},{68... | collective-permute-start | bytes 1376264 | tf_op jit(solution)/shard_map/ppermute | solution.py:142
  23.2 0.2 copy.11
  23.4 1.4 broadcast_in_dim.6
  24.8 4.1 %all-to-all-start = ((bf16[4,256,896]{2,1,0:T(8,128)(2,1)}), bf16[4,256,896]{2,1,0:T(8,128)(2,1)S(1)}, u32[]{:S(2)}, u32[]{:S(2)}) async-start(bf16[4,256,896]{2,1,0:T(8,128)(2,1)} %broadcast_in_dim.6), calls=%async_computation | async-start | bytes 3670016 | tf_op jit(solution)/shard_map/all_to_all | solution.py:165
  29.0 0.6 constant_dynamic-update-slice_fusion.4
  29.6 0.0 collective-permute-done
  29.6 0.7 pad_maximum_fusion.1
  30.3 3.1 %collective-permute-start.1 = (bf16[32,4096]{1,0:T(8,128)(2,1)}, bf16[32,4096]{1,0:T(8,128)(2,1)S(1)}, u32[]{:S(2)}, u32[]{:S(2)}) collective-permute-start(bf16[32,4096]{1,0:T(8,128)(2,1)} %pad_maximum_fusion.1), channel_id=1, source_target_pairs={{0,8},{4,12},{8,0},{12,4},{16,24},{20,28},{24,16},{28,20},{1,9},{5... | collective-permute-start | bytes 786440 | tf_op jit(solution)/shard_map/ppermute | solution.py:146
  33.4 0.6 constant_dynamic-update-slice_fusion.3
  34.1 5.6 %collective-permute-done.8 = bf16[256,896]{0,1:T(8,128)(2,1)} collective-permute-done((bf16[256,896]{0,1:T(8,128)(2,1)S(1)}, bf16[256,896]{0,1:T(8,128)(2,1)}, u32[]{:S(2)}, u32[]{:S(2)}) %collective-permute-start.8) | collective-permute-done | bytes 458784 | tf_op jit(solution)/shard_map/ppermute | solution.py:142
  39.6 1.3 copy.12
  40.9 10.1 %all-to-all-done.refs_4_ = bf16[4,256,896]{2,1,0:T(8,128)(2,1)S(1)} async-done(((bf16[4,256,896]{2,1,0:T(8,128)(2,1)}), bf16[4,256,896]{2,1,0:T(8,128)(2,1)S(1)}, u32[]{:S(2)}, u32[]{:S(2)}) %all-to-all-start) | async-done | bytes 1835040 | tf_op jit(solution)/shard_map/all_to_all | solution.py:165
  51.0 1.5 broadcast_in_dim.7
  52.5 4.4 %all-to-all-start.1 = ((bf16[4,256,896]{2,1,0:T(8,128)(2,1)}), bf16[4,256,896]{2,1,0:T(8,128)(2,1)}, u32[]{:S(2)}, u32[]{:S(2)}) async-start(bf16[4,256,896]{2,1,0:T(8,128)(2,1)} %broadcast_in_dim.7), calls=%async_computation.1 | async-start | bytes 3670016 | tf_op jit(solution)/shard_map/all_to_all | solution.py:165
  57.0 19.8 %collective-permute-done.1 = bf16[32,4096]{1,0:T(8,128)(2,1)S(1)} collective-permute-done((bf16[32,4096]{1,0:T(8,128)(2,1)}, bf16[32,4096]{1,0:T(8,128)(2,1)S(1)}, u32[]{:S(2)}, u32[]{:S(2)}) %collective-permute-start.1) | collective-permute-done | bytes 262176 | tf_op jit(solution)/shard_map/ppermute | solution.py:146
  76.8 1.9 collective-permute-start.4
  78.7 4.6 %collective-permute-start.2 = (bf16[64,4096]{1,0:T(8,128)(2,1)S(1)}, bf16[64,4096]{1,0:T(8,128)(2,1)S(1)}, u32[]{:S(2)}, u32[]{:S(2)}) collective-permute-start(bf16[64,4096]{1,0:T(8,128)(2,1)S(1)} %pad_maximum_fusion), channel_id=1, source_target_pairs={{0,1},{1,0},{2,3},{3,2},{32,35},{33,34},{34,33},{35,32},{4,5},{5,4... | collective-permute-start | bytes 1572872 | tf_op jit(solution)/shard_map/ppermute | solution.py:158
  83.4 0.7 constant_dynamic-update-slice_fusion.2
  84.1 0.7 constant_dynamic-update-slice_fusion.1
  84.8 7.2 %collective-permute-done.4 = bf16[64,4096]{1,0:T(8,128)(2,1)} collective-permute-done((bf16[64,4096]{1,0:T(8,128)(2,1)S(1)}, bf16[64,4096]{1,0:T(8,128)(2,1)}, u32[]{:S(2)}, u32[]{:S(2)}) %collective-permute-start.4) | collective-permute-done | bytes 524320 | tf_op jit(solution)/shard_map/ppermute | solution.py:148
  91.9 4.6 %collective-permute-start.5 = (bf16[64,4096]{1,0:T(8,128)(2,1)}, bf16[64,4096]{1,0:T(8,128)(2,1)}, u32[]{:S(2)}, u32[]{:S(2)}) collective-permute-start(bf16[64,4096]{1,0:T(8,128)(2,1)} %collective-permute-done.4), channel_id=1, source_target_pairs={{0,1},{1,0},{2,3},{3,2},{32,35},{33,34},{34,33},{35,32},{4,5},{5,4... | collective-permute-start | bytes 1572872 | tf_op jit(solution)/shard_map/ppermute | solution.py:158
  96.6 0.0 collective-permute-done.2
  96.6 0.8 constant_dynamic-update-slice_fusion.refs_0_
  97.4 1.9 collective-permute-start.3
  99.3 4.1 %collective-permute-start.7 = (bf16[4,256,896]{2,1,0:T(8,128)(2,1)S(1)}, bf16[4,256,896]{2,1,0:T(8,128)(2,1)}, u32[]{:S(2)}, u32[]{:S(2)}) collective-permute-start(bf16[4,256,896]{2,1,0:T(8,128)(2,1)S(1)} %all-to-all-done.refs_4_), channel_id=1, source_target_pairs={{0,32},{32,0},{1,33},{33,1},{2,34},{34,2},{3,35},{35,3},{4,36},{36... | collective-permute-start | bytes 5505032 | tf_op jit(solution)/shard_map/ppermute | solution.py:170
  103.5 0.0 all-to-all-done.1.refs_6_
  103.5 1.9 collective-permute-start.9
  105.4 1.1 constant_dynamic-update-slice_fusion.6
  106.5 0.0 collective-permute-done.5
  106.5 1.1 constant_dynamic-update-slice_fusion.5.refs_2_
  107.6 2.3 %collective-permute-start.6 = (bf16[128,4096]{1,0:T(8,128)(2,1)S(1)}, bf16[128,4096]{1,0:T(8,128)(2,1)}, u32[]{:S(2)}, u32[]{:S(2)}) collective-permute-start(bf16[128,4096]{1,0:T(8,128)(2,1)S(1)} %constant_dynamic-update-slice_fusion.5.refs_2_), channel_id=1, source_target_pairs={{0,3},{1,2},{2,1},{3,0},{32,33},{33,32},{34,35},{35,34},{4,7},{5,6... | collective-permute-start | bytes 3145736 | tf_op jit(solution)/shard_map/ppermute | solution.py:160
  110.0 0.7 stack.166.cols_ref
  110.7 0.6 stack.199.slot_ref
  111.3 4.0 %collective-permute-done.3.refs_1_ = bf16[128,4096]{1,0:T(8,128)(2,1)} collective-permute-done((bf16[128,4096]{1,0:T(8,128)(2,1)}, bf16[128,4096]{1,0:T(8,128)(2,1)}, u32[]{:S(2)}, u32[]{:S(2)}) %collective-permute-start.3) | collective-permute-done | bytes 1048608 | tf_op jit(solution)/shard_map/ppermute | solution.py:160
  115.3 11.3 %collective-permute-done.6.refs_3_ = bf16[128,4096]{1,0:T(8,128)(2,1)} collective-permute-done((bf16[128,4096]{1,0:T(8,128)(2,1)S(1)}, bf16[128,4096]{1,0:T(8,128)(2,1)}, u32[]{:S(2)}, u32[]{:S(2)}) %collective-permute-start.6) | collective-permute-done | bytes 1048608 | tf_op jit(solution)/shard_map/ppermute | solution.py:160
  126.6 0.0 collective-permute-done.7.refs_5_
  126.6 0.0 collective-permute-done.9.refs_7_
  126.6 0.0 copy-start.7
  126.6 0.0 copy-start.8
  126.7 8.7 %mlp.1 = f32[32,8,128]{2,1,0:T(8,128)} custom-call(s32[16]{0:T(128)} %stack.166.cols_ref, s32[32]{0:T(128)} %stack.199.slot_ref, bf16[128,4096]{1,0:T(8,128)(2,1)} %constant_dynamic-update-slice_fusion.refs_0_, bf16[128,4096]{1,0:T(8,128)(2,1)} %collective-permute-done.3.refs_1_, bf16[128,4096]{1,0:T(8,128)(2,1)} %copy-done.2, ...), custom_call_target="tpu_custom_call" | custom-call | tf_op jit(solution)/shard_map/mlp/pallas_call | solution.py:66
  135.4 9.3 %all-to-all-start.2 = ((f32[32,8,128]{2,1,0:T(8,128)}), f32[32,8,128]{2,1,0:T(8,128)S(1)}, u32[]{:S(2)}, u32[]{:S(2)}) async-start(f32[32,8,128]{2,1,0:T(8,128)} %mlp.1), calls=%async_computation.2 | async-start | bytes 262144 | tf_op jit(solution)/shard_map/all_to_all | solution.py:178
  146.0 0.9 convolution_bitcast_fusion.right_ref
  146.9 9.9 %all-to-all-done.2.parts_ref = f32[32,8,128]{2,1,0:T(8,128)S(1)} async-done(((f32[32,8,128]{2,1,0:T(8,128)}), f32[32,8,128]{2,1,0:T(8,128)S(1)}, u32[]{:S(2)}, u32[]{:S(2)}) %all-to-all-start.2) | async-done | bytes 131104 | tf_op jit(solution)/shard_map/all_to_all | solution.py:178
  156.8 0.6 copy-done.5
  157.5 2.1 %norm.1 = (f32[8,128]{1,0:T(8,128)}, f32[16,8,128]{2,1,0:T(8,128)}) custom-call(f32[32,8,128]{2,1,0:T(8,128)} %copy-done.5, f32[2,8,64]{2,1,0:T(8,128)} %convolution_bitcast_fusion.right_ref, s32[1]{0:T(128)S(6)} %copy.19.train_len_ref, s32[1]{0:T(128)S(6)} %copy.20.roll_len_ref), custom_call_target="tpu_custom_call" | custom-call | tf_op jit(solution)/shard_map/norm/pallas_call | solution.py:181
  159.5 15.9 %all-to-all-start.4 = ((f32[16,8,128]{2,1,0:T(8,128)}), f32[16,8,128]{2,1,0:T(8,128)S(1)}, u32[]{:S(2)}, u32[]{:S(2)}) async-start(f32[16,8,128]{2,1,0:T(8,128)} %get-tuple-element.8), calls=%async_computation.4 | async-start | bytes 131072 | tf_op jit(solution)/shard_map/all_to_all | solution.py:187
  175.5 2.3 %collective-permute-start.10 = (f32[8,128]{1,0:T(8,128)}, f32[8,128]{1,0:T(8,128)S(1)}, u32[]{:S(2)}, u32[]{:S(2)}) collective-permute-start(f32[8,128]{1,0:T(8,128)} %get-tuple-element.7.refs_0_), channel_id=1, source_target_pairs={{0,1},{1,2},{2,3},{3,0},{4,5},{5,6},{6,7},{7,4},{8,9},{9,10},{10,1... | collective-permute-start | bytes 12296 | tf_op jit(solution)/shard_map/ppermute | solution.py:190
  177.8 4.2 %collective-permute-start.11 = (f32[8,128]{1,0:T(8,128)}, f32[8,128]{1,0:T(8,128)S(1)}, u32[]{:S(2)}, u32[]{:S(2)}) collective-permute-start(f32[8,128]{1,0:T(8,128)} %get-tuple-element.7.refs_0_), channel_id=1, source_target_pairs={{0,3},{1,0},{2,1},{3,2},{4,7},{5,4},{6,5},{7,6},{8,11},{9,8},{10,9... | collective-permute-start | bytes 12296 | tf_op jit(solution)/shard_map/ppermute | solution.py:190
  182.0 2.0 collective-permute-start.12
  184.0 0.0 collective-permute-done.10.refs_1_
  184.1 0.0 copy-start.9
  184.1 0.0 collective-permute-done.11.refs_2_
  184.1 4.3 %collective-permute-done.12.refs_3_ = f32[8,128]{1,0:T(8,128)S(1)} collective-permute-done((f32[8,128]{1,0:T(8,128)}, f32[8,128]{1,0:T(8,128)S(1)}, u32[]{:S(2)}, u32[]{:S(2)}) %collective-permute-start.12) | collective-permute-done | bytes 4128 | tf_op jit(solution)/shard_map/ppermute | solution.py:190
  188.4 0.0 copy-done.10
  188.4 0.6 copy-done.11
  189.0 1.4 repeat.1
  190.3 0.0 all-to-all-done.4.roll_ref
  190.3 14.3 %all_to_all.25.train_ref = f32[8,4,8,128]{3,2,1,0:T(8,128)} all-to-all(f32[8,4,8,128]{3,2,1,0:T(8,128)} %repeat.1), channel_id=1, replica_groups=mesh['x'=4,'zh'=2,'co'=2,'zl'=8,'y'=4] {'zl'}, dimensions={0} | all-to-all | bytes 262144 | tf_op jit(solution)/shard_map/all_to_all | solution.py:191
  204.6 2.1 %score.1 = f32[16,32]{1,0:T(8,128)} custom-call(f32[8,4,8,128]{3,2,1,0:T(8,128)} %all_to_all.25.train_ref, f32[16,8,128]{2,1,0:T(8,128)} %copy-done.6, s32[1]{0:T(128)} %bitcast.54.y_ref), custom_call_target="tpu_custom_call" | custom-call | tf_op jit(solution)/shard_map/score/pallas_call | solution.py:202
  (18 shorter events, 0.1 us)
Async XLA Ops:
  0.0 146.0 %copy-start = (bf16[4096,64]{0,1:T(8,128)(2,1)S(1)}, bf16[4096,64]{0,1:T(8,128)(2,1)}, u32[]{:S(2)}) copy-start(bf16[4096,64]{0,1:T(8,128)(2,1)} %param.19) | copy-start | bytes 1572868
  0.9 28.7 %collective-permute-start = (bf16[16,4096]{1,0:T(8,128)(2,1)S(1)}, bf16[16,4096]{1,0:T(8,128)(2,1)S(1)}, u32[]{:S(2)}, u32[]{:S(2)}) collective-permute-start(bf16[16,4096]{1,0:T(8,128)(2,1)S(1)} %pad_maximum_fusion.2), channel_id=1, source_target_pairs={{0,16},{4,20},{8,24},{12,28},{16,0},{20,4},{24,8},{28,12},{1,17},{... | collective-permute-start | bytes 393224 | tf_op jit(solution)/shard_map/ppermute | solution.py:146
  12.5 27.1 %collective-permute-start.8 = (bf16[256,896]{0,1:T(8,128)(2,1)S(1)}, bf16[256,896]{0,1:T(8,128)(2,1)}, u32[]{:S(2)}, u32[]{:S(2)}) collective-permute-start(bf16[256,896]{0,1:T(8,128)(2,1)S(1)} %constant_dynamic-update-slice_fusion.7), channel_id=1, source_target_pairs={{0,64},{64,0},{1,65},{65,1},{2,66},{66,2},{3,67},{67,3},{4,68},{68... | collective-permute-start | bytes 1376264 | tf_op jit(solution)/shard_map/ppermute | solution.py:142
  24.8 4.2 %copy-start.3 = (bf16[1,8,4096]{2,1,0:T(8,128)(2,1)S(1)}, bf16[1,8,4096]{2,1,0:T(8,128)(2,1)}, u32[]{:S(2)}) copy-start(bf16[1,8,4096]{2,1,0:T(8,128)(2,1)} %param.10) | copy-start | bytes 196612
  24.8 4.8 %copy-start.4 = (bf16[1,8,4096]{2,1,0:T(8,128)(2,1)S(1)}, bf16[1,8,4096]{2,1,0:T(8,128)(2,1)}, u32[]{:S(2)}) copy-start(bf16[1,8,4096]{2,1,0:T(8,128)(2,1)} %param.13) | copy-start | bytes 196612
  24.8 26.2 %all-to-all-start = ((bf16[4,256,896]{2,1,0:T(8,128)(2,1)}), bf16[4,256,896]{2,1,0:T(8,128)(2,1)S(1)}, u32[]{:S(2)}, u32[]{:S(2)}) async-start(bf16[4,256,896]{2,1,0:T(8,128)(2,1)} %broadcast_in_dim.6), calls=%async_computation | async-start | bytes 3670016 | tf_op jit(solution)/shard_map/all_to_all | solution.py:165
  30.3 46.5 %collective-permute-start.1 = (bf16[32,4096]{1,0:T(8,128)(2,1)}, bf16[32,4096]{1,0:T(8,128)(2,1)S(1)}, u32[]{:S(2)}, u32[]{:S(2)}) collective-permute-start(bf16[32,4096]{1,0:T(8,128)(2,1)} %pad_maximum_fusion.1), channel_id=1, source_target_pairs={{0,8},{4,12},{8,0},{12,4},{16,24},{20,28},{24,16},{28,20},{1,9},{5... | collective-permute-start | bytes 786440 | tf_op jit(solution)/shard_map/ppermute | solution.py:146
  51.0 48.3 %copy-start.1 = (bf16[4,256,896]{2,1,0:T(8,128)(2,1)}, bf16[4,256,896]{2,1,0:T(8,128)(2,1)S(1)}, u32[]{:S(2)}) copy-start(bf16[4,256,896]{2,1,0:T(8,128)(2,1)S(1)} %all-to-all-done.refs_4_) | copy-start | bytes 5505028
  52.5 50.9 %all-to-all-start.1 = ((bf16[4,256,896]{2,1,0:T(8,128)(2,1)}), bf16[4,256,896]{2,1,0:T(8,128)(2,1)}, u32[]{:S(2)}, u32[]{:S(2)}) async-start(bf16[4,256,896]{2,1,0:T(8,128)(2,1)} %broadcast_in_dim.7), calls=%async_computation.1 | async-start | bytes 3670016 | tf_op jit(solution)/shard_map/all_to_all | solution.py:165
  76.8 15.1 %collective-permute-start.4 = (bf16[64,4096]{1,0:T(8,128)(2,1)S(1)}, bf16[64,4096]{1,0:T(8,128)(2,1)}, u32[]{:S(2)}, u32[]{:S(2)}) collective-permute-start(bf16[64,4096]{1,0:T(8,128)(2,1)S(1)} %pad_maximum_fusion), channel_id=1, source_target_pairs={{0,4},{4,0},{8,12},{12,8},{16,20},{20,16},{24,28},{28,24},{1,5},{5... | collective-permute-start | bytes 1572872 | tf_op jit(solution)/shard_map/ppermute | solution.py:148
  78.7 17.8 %collective-permute-start.2 = (bf16[64,4096]{1,0:T(8,128)(2,1)S(1)}, bf16[64,4096]{1,0:T(8,128)(2,1)S(1)}, u32[]{:S(2)}, u32[]{:S(2)}) collective-permute-start(bf16[64,4096]{1,0:T(8,128)(2,1)S(1)} %pad_maximum_fusion), channel_id=1, source_target_pairs={{0,1},{1,0},{2,3},{3,2},{32,35},{33,34},{34,33},{35,32},{4,5},{5,4... | collective-permute-start | bytes 1572872 | tf_op jit(solution)/shard_map/ppermute | solution.py:158
  91.9 14.6 %collective-permute-start.5 = (bf16[64,4096]{1,0:T(8,128)(2,1)}, bf16[64,4096]{1,0:T(8,128)(2,1)}, u32[]{:S(2)}, u32[]{:S(2)}) collective-permute-start(bf16[64,4096]{1,0:T(8,128)(2,1)} %collective-permute-done.4), channel_id=1, source_target_pairs={{0,1},{1,0},{2,3},{3,2},{32,35},{33,34},{34,33},{35,32},{4,5},{5,4... | collective-permute-start | bytes 1572872 | tf_op jit(solution)/shard_map/ppermute | solution.py:158
  97.4 17.9 %collective-permute-start.3 = (bf16[128,4096]{1,0:T(8,128)(2,1)}, bf16[128,4096]{1,0:T(8,128)(2,1)}, u32[]{:S(2)}, u32[]{:S(2)}) collective-permute-start(bf16[128,4096]{1,0:T(8,128)(2,1)} %constant_dynamic-update-slice_fusion.refs_0_), channel_id=1, source_target_pairs={{0,3},{1,2},{2,1},{3,0},{32,33},{33,32},{34,35},{35,34},{4,7},{5,6... | collective-permute-start | bytes 3145736 | tf_op jit(solution)/shard_map/ppermute | solution.py:160
  99.3 27.3 %collective-permute-start.7 = (bf16[4,256,896]{2,1,0:T(8,128)(2,1)S(1)}, bf16[4,256,896]{2,1,0:T(8,128)(2,1)}, u32[]{:S(2)}, u32[]{:S(2)}) collective-permute-start(bf16[4,256,896]{2,1,0:T(8,128)(2,1)S(1)} %all-to-all-done.refs_4_), channel_id=1, source_target_pairs={{0,32},{32,0},{1,33},{33,1},{2,34},{34,2},{3,35},{35,3},{4,36},{36... | collective-permute-start | bytes 5505032 | tf_op jit(solution)/shard_map/ppermute | solution.py:170
  103.5 23.1 %collective-permute-start.9 = (bf16[4,256,896]{2,1,0:T(8,128)(2,1)}, bf16[4,256,896]{2,1,0:T(8,128)(2,1)}, u32[]{:S(2)}, u32[]{:S(2)}) collective-permute-start(bf16[4,256,896]{2,1,0:T(8,128)(2,1)} %all-to-all-done.1.refs_6_), channel_id=1, source_target_pairs={{0,32},{32,0},{1,33},{33,1},{2,34},{34,2},{3,35},{35,3},{4,36},{36... | collective-permute-start | bytes 5505032 | tf_op jit(solution)/shard_map/ppermute | solution.py:170
  107.6 19.0 %copy-start.2 = (bf16[128,4096]{1,0:T(8,128)(2,1)}, bf16[128,4096]{1,0:T(8,128)(2,1)S(1)}, u32[]{:S(2)}) copy-start(bf16[128,4096]{1,0:T(8,128)(2,1)S(1)} %constant_dynamic-update-slice_fusion.5.refs_2_) | copy-start | bytes 3145732
  107.6 19.0 %collective-permute-start.6 = (bf16[128,4096]{1,0:T(8,128)(2,1)S(1)}, bf16[128,4096]{1,0:T(8,128)(2,1)}, u32[]{:S(2)}, u32[]{:S(2)}) collective-permute-start(bf16[128,4096]{1,0:T(8,128)(2,1)S(1)} %constant_dynamic-update-slice_fusion.5.refs_2_), channel_id=1, source_target_pairs={{0,3},{1,2},{2,1},{3,0},{32,33},{33,32},{34,35},{35,34},{4,7},{5,6... | collective-permute-start | bytes 3145736 | tf_op jit(solution)/shard_map/ppermute | solution.py:160
  126.6 19.4 %copy-start.7 = (bf16[1,8,4096]{2,1,0:T(8,128)(2,1)S(1)}, bf16[1,8,4096]{2,1,0:T(8,128)(2,1)}, u32[]{:S(2)}) copy-start(bf16[1,8,4096]{2,1,0:T(8,128)(2,1)} %param.14) | copy-start | bytes 196612
  126.6 19.4 %copy-start.8 = (bf16[1,8,4096]{2,1,0:T(8,128)(2,1)S(1)}, bf16[1,8,4096]{2,1,0:T(8,128)(2,1)}, u32[]{:S(2)}) copy-start(bf16[1,8,4096]{2,1,0:T(8,128)(2,1)} %param.11) | copy-start | bytes 196612
  135.4 21.4 %all-to-all-start.2 = ((f32[32,8,128]{2,1,0:T(8,128)}), f32[32,8,128]{2,1,0:T(8,128)S(1)}, u32[]{:S(2)}, u32[]{:S(2)}) async-start(f32[32,8,128]{2,1,0:T(8,128)} %mlp.1), calls=%async_computation.2 | async-start | bytes 262144 | tf_op jit(solution)/shard_map/all_to_all | solution.py:178
  156.8 0.7 copy-start.5
  159.5 30.8 %all-to-all-start.4 = ((f32[16,8,128]{2,1,0:T(8,128)}), f32[16,8,128]{2,1,0:T(8,128)S(1)}, u32[]{:S(2)}, u32[]{:S(2)}) async-start(f32[16,8,128]{2,1,0:T(8,128)} %get-tuple-element.8), calls=%async_computation.4 | async-start | bytes 131072 | tf_op jit(solution)/shard_map/all_to_all | solution.py:187
  175.5 8.6 %collective-permute-start.10 = (f32[8,128]{1,0:T(8,128)}, f32[8,128]{1,0:T(8,128)S(1)}, u32[]{:S(2)}, u32[]{:S(2)}) collective-permute-start(f32[8,128]{1,0:T(8,128)} %get-tuple-element.7.refs_0_), channel_id=1, source_target_pairs={{0,1},{1,2},{2,3},{3,0},{4,5},{5,6},{6,7},{7,4},{8,9},{9,10},{10,1... | collective-permute-start | bytes 12296 | tf_op jit(solution)/shard_map/ppermute | solution.py:190
  177.8 6.3 %collective-permute-start.11 = (f32[8,128]{1,0:T(8,128)}, f32[8,128]{1,0:T(8,128)S(1)}, u32[]{:S(2)}, u32[]{:S(2)}) collective-permute-start(f32[8,128]{1,0:T(8,128)} %get-tuple-element.7.refs_0_), channel_id=1, source_target_pairs={{0,3},{1,0},{2,1},{3,2},{4,7},{5,4},{6,5},{7,6},{8,11},{9,8},{10,9... | collective-permute-start | bytes 12296 | tf_op jit(solution)/shard_map/ppermute | solution.py:190
  182.0 6.4 %collective-permute-start.12 = (f32[8,128]{1,0:T(8,128)}, f32[8,128]{1,0:T(8,128)S(1)}, u32[]{:S(2)}, u32[]{:S(2)}) collective-permute-start(f32[8,128]{1,0:T(8,128)} %get-tuple-element.7.refs_0_), channel_id=1, source_target_pairs={{0,2},{1,3},{2,0},{3,1},{4,6},{5,7},{6,4},{7,5},{8,10},{9,11},{10,... | collective-permute-start | bytes 12296 | tf_op jit(solution)/shard_map/ppermute | solution.py:190
  184.1 4.3 %copy-start.9 = (f32[8,128]{1,0:T(8,128)}, f32[8,128]{1,0:T(8,128)S(1)}, u32[]{:S(2)}) copy-start(f32[8,128]{1,0:T(8,128)S(1)} %collective-permute-done.10.refs_1_) | copy-start | bytes 12292
  184.1 4.3 %copy-start.10 = (f32[8,128]{1,0:T(8,128)}, f32[8,128]{1,0:T(8,128)S(1)}, u32[]{:S(2)}) copy-start(f32[8,128]{1,0:T(8,128)S(1)} %collective-permute-done.11.refs_2_) | copy-start | bytes 12292
  188.4 0.6 copy-start.11
  190.3 14.3 %copy-start.6 = (f32[16,8,128]{2,1,0:T(8,128)}, f32[16,8,128]{2,1,0:T(8,128)S(1)}, u32[]{:S(2)}) copy-start(f32[16,8,128]{2,1,0:T(8,128)S(1)} %all-to-all-done.4.roll_ref) | copy-start | bytes 196612
